TPU v7x, 512 devices: a whole 4x4x16 slice. The times are simulated.
512 devices in a mesh: wide: 128 (over x, z, core), narrow: 4 (over y).
Axes of the slice: x: 4, y: 4, z: 16, core: 2. Of those that a mesh axis runs over, the one named last changes fastest.
Arguments:
- distance: float32 [128, 2048, 512], P('wide', None, 'narrow'), may hold values from -1 to 1
- occupancy: int32 [128, 256, 64], P('wide', None, 'narrow'), may hold values 0 or 1
- material: int32 [128, 256, 64], P('wide', None, 'narrow'), may hold values from 0 to 15
- colours: float32 [3, 16], replicated, may hold values from 0.1 to 1
- absorb: float32 [16], replicated, may hold values from 0.5 to 4
- kernel_x: float32 [256, 256], replicated, may hold values from -0.1875 to 0.1875
- kernel_y: float32 [128, 128], replicated, may hold values from -0.25 to 0.25
Outputs:
- image: float32 [4, 2048, 512], P(None, 'wide', 'narrow')
All inputs are finite; a program needn't handle non-finite values. No bound on the sum of `occupancy` on one device may be relied on, other than what follows from the above.
Results may differ from a plain program's by a relative error of at most 0.0003.
Values sent between devices are 32-bit elements; how exact they have to be, the bound alone decides.
No kernel may reach another device: no remote copies, remote signals or barrier semaphores. Data moves between devices by JAX's collectives and lax.ppermute only.
A program may use at most 64 MiB of HBM per device.

v0:
```python
import jax
import jax.numpy as jnp
from jax import lax
from jax.sharding import PartitionSpec as P


def extended(cells, sides, width):
    for axis, dim in sides:
        count = lax.axis_size(axis)
        ends = count - 1
        head = lax.slice_in_dim(cells, 0, width, axis=dim)
        tail = lax.slice_in_dim(cells, cells.shape[dim] - width, cells.shape[dim], axis=dim)
        cells = jnp.concatenate(
            [
                lax.ppermute(tail, axis, [(i, (i + 1) % count) for i in range(ends)]),
                cells,
                lax.ppermute(head, axis, [((i + 1) % count, i) for i in range(ends)]),
            ],
            axis=dim,
        )
    return cells


def partner(value, axis, distance):
    mask = 2**distance
    pairs = [(source, source ^ mask) for source in range(lax.axis_size(axis))]
    return lax.ppermute(value, axis, pairs)


def resample(fields, kernel_x, kernel_y):
    leading = fields.shape[:-2]
    col_count = fields.shape[-2]
    row_count = fields.shape[-1]
    block_x = kernel_x.shape[0]
    block_y = kernel_y.shape[0]
    blocked = fields.reshape(leading + (col_count // block_x, block_x, row_count))
    blended = 0.5 * blocked + jnp.einsum(
        "...bir,ij->...bjr", blocked, kernel_x, precision=lax.Precision.HIGHEST
    )
    blended = blended.reshape(leading + (col_count, row_count // block_y, block_y))
    blended = 0.5 * blended + jnp.einsum(
        "...xci,ij->...xcj", blended, kernel_y, precision=lax.Precision.HIGHEST
    )
    return blended.reshape(fields.shape)


def expand(values, col_count, row_count):
    shape = values.shape
    brick_rows = shape[-1]
    brick_cols = shape[-2]
    row_ids = jnp.arange(row_count, dtype=jnp.int32) // (row_count // brick_rows)
    spread = (row_ids[None, :] == jnp.arange(brick_rows, dtype=jnp.int32)[:, None]).astype(
        jnp.float32
    )
    wider = jnp.einsum("...y,yr->...r", values, spread, precision=lax.Precision.HIGHEST)
    grown = jnp.broadcast_to(
        wider[..., :, None, :], shape[:-2] + (brick_cols, col_count // brick_cols, row_count)
    )
    return grown.reshape(shape[:-2] + (col_count, row_count))


def brick_table(material, occupancy, colours, absorb):
    lookup = jnp.concatenate([colours, absorb[None, :]], axis=0)
    labels = jnp.arange(colours.shape[1], dtype=jnp.int32)
    selector = (material[None] == labels.reshape((-1,) + (1,) * material.ndim)).astype(jnp.float32)
    bricks = jnp.tensordot(lookup, selector, axes=((1,), (0,)), precision=lax.Precision.HIGHEST)
    return jnp.concatenate([bricks, occupancy.astype(jnp.float32)[None]], axis=0)


def shade(blended, brick_values, mask, step_length):
    dist_field = blended[0]
    density = jnp.exp(-2.0 * dist_field * dist_field)
    norm_sq = jnp.maximum(
        blended[1] * blended[1] + blended[2] * blended[2] + blended[3] * blended[3], 0.1
    )
    facing = 0.25 + 0.75 * jnp.abs(blended[3]) * lax.rsqrt(norm_sq)
    opacity = mask * (1.0 - jnp.exp(-brick_values[3] * density * step_length))
    colour = brick_values[:3] * (facing * opacity)[None]
    return (colour, opacity)


def composite(nearer, farther):
    return nearer + (1.0 - nearer[3])[None] * farther


def local(distance, occupancy, material, colours, absorb, kernel_x, kernel_y):
    slices, col_count, row_count = distance.shape
    devices = lax.axis_size("wide")
    step_length = 4.0 / (slices * devices)
    padded = extended(distance, (("wide", 0), ("narrow", 2)), 1)
    grad_z = 0.5 * (padded[2:, :, 1:-1] - padded[:-2, :, 1:-1])
    grad_y = 0.5 * (padded[1:-1, :, 2:] - padded[1:-1, :, :-2])
    pad_cols = jnp.pad(distance, ((0, 0), (1, 1), (0, 0)))
    grad_x = 0.5 * (pad_cols[:, 2:] - pad_cols[:, :-2])
    blended = resample(jnp.stack([distance, grad_x, grad_y, grad_z]), kernel_x, kernel_y)
    table = brick_table(material, occupancy, colours, absorb)
    brick_values = expand(table, col_count, row_count)
    colour, opacity = shade(blended, brick_values, brick_values[4], step_length)
    transmit = jnp.ones((col_count, row_count), jnp.float32)
    contrib = jnp.concatenate([colour[:, 0], opacity[0][None]], axis=0)
    accumulated = transmit[None] * contrib
    block_cols = col_count // devices
    my_index = lax.axis_index("wide")
    holding = accumulated
    for level_index in range(devices.bit_length() - 1):
        my_bit = my_index >> level_index & 1
        halves = holding.reshape(4, -1, 2, block_cols, row_count)
        kept_half = lax.dynamic_index_in_dim(halves, my_bit, 2, keepdims=False)
        sent_half = lax.dynamic_index_in_dim(halves, 1 - my_bit, 2, keepdims=False)
        received = partner(sent_half, "wide", level_index)
        nearer = jnp.where(my_bit == 0, kept_half, received)
        farther = jnp.where(my_bit == 0, received, kept_half)
        merged = composite(nearer, farther)
        holding = merged.reshape(4, -1, row_count)
    return holding


def solution(mesh):
    in_specs = (
        P("wide", None, "narrow"),
        P("wide", None, "narrow"),
        P("wide", None, "narrow"),
        P(),
        P(),
        P(),
        P(),
    )
    out_specs = P(None, "wide", "narrow")
    return jax.shard_map(local, mesh=mesh, in_specs=in_specs, out_specs=out_specs, check_vma=False)
```

profile of v0, /device:TPU:2, one launch (start us, length us, event | category | flops | bytes accessed | tf_op | source)
XLA Modules:
  0.0 223.0 jit_solution(17145685858983137209)
XLA Ops:
  0.0 2.0 collective-permute-start
  2.1 10.8 %collective-permute-start.1 = (f32[1,2048,128]{2,1,0:T(8,128)}, f32[1,2048,128]{2,1,0:T(8,128)S(1)}, u32[]{:S(2)}, u32[]{:S(2)}) collective-permute-start(f32[1,2048,128]{2,1,0:T(8,128)} %param.7), channel_id=1, source_target_pairs={{4,0},{8,4},{12,8},{16,12},{20,16},{24,20},{28,24},{32,28},{36,32}... | collective-permute-start | bytes 3145736 | tf_op jit(solution)/shard_map/ppermute | solution.py:17
  12.9 0.7 convert_element_type.8
  13.6 1.0 convolution_bitcast_fusion
  14.6 1.5 fusion.43
  16.2 7.4 %collective-permute-done = f32[1,2048,128]{2,1,0:T(8,128)S(1)} collective-permute-done((f32[1,2048,128]{2,1,0:T(8,128)}, f32[1,2048,128]{2,1,0:T(8,128)S(1)}, u32[]{:S(2)}, u32[]{:S(2)}) %collective-permute-start) | collective-permute-done | bytes 1048608 | tf_op jit(solution)/shard_map/ppermute | solution.py:15
  23.7 1.3 subtract_multiply_fusion.1
  25.5 1.1 constant_dynamic-update-slice_fusion
  26.6 3.6 %fusion.60 = (f32[3,2048,1]{2,1,0:T(8,128)}, f32[3,2048,1]{2,1,0:T(8,128)}) fusion(f32[3,2048,128]{2,1,0:T(8,128)S(1)} %get-tuple-element.11), kind=kLoop, calls=%fused_computation.115 | loop fusion | bytes 98304 | tf_op jit(solution)/shard_map/slice | solution.py:11
  30.3 2.9 %copy.28 = f32[3,2048,1]{1,2,0:T(1,128)} copy(f32[3,2048,1]{2,1,0:T(8,128)} %get-tuple-element.7) | data formatting | bytes 49152 | tf_op jit(solution)/shard_map/slice | solution.py:11
  33.2 1.3 collective-permute-start.2
  34.5 3.0 %copy.30 = f32[3,2048,1]{1,2,0:T(1,128)} copy(f32[3,2048,1]{2,1,0:T(8,128)} %get-tuple-element.8) | data formatting | bytes 49152 | tf_op jit(solution)/shard_map/slice | solution.py:12
  37.5 5.1 %collective-permute-start.3 = (f32[3,2048,1]{1,2,0:T(1,128)}, f32[3,2048,1]{1,2,0:T(1,128)}, u32[]{:S(2)}, u32[]{:S(2)}) collective-permute-start(f32[3,2048,1]{1,2,0:T(1,128)} %copy.30), channel_id=1, source_target_pairs={{0,1},{1,2},{2,3},{4,5},{5,6},{6,7},{8,9},{9,10},{10,11},{12,13},{... | collective-permute-start | bytes 73736 | tf_op jit(solution)/shard_map/ppermute | solution.py:15
  42.6 1.6 fusion.39
  44.2 2.6 %copy.32 = f32[1,1,8,256,128]{3,4,2,0,1:T(8,128)} copy(f32[1,1,8,256,128]{4,3,2,1,0:T(8,128)} %bitcast.150) | data formatting | bytes 2097152 | tf_op jit(solution)/shard_map/stack | solution.py:95
  46.9 2.5 %copy.35 = f32[1,1,8,256,128]{3,4,2,0,1:T(8,128)} copy(f32[1,1,8,256,128]{4,3,2,1,0:T(8,128)} %bitcast.154) | data formatting | bytes 2097152 | tf_op jit(solution)/shard_map/stack | solution.py:95
  49.4 2.6 %copy.33 = f32[1,1,8,256,128]{3,4,2,0,1:T(8,128)} copy(f32[1,1,8,256,128]{4,3,2,1,0:T(8,128)} %bitcast.151) | data formatting | bytes 2097152 | tf_op jit(solution)/shard_map/stack | solution.py:95
  51.9 2.9 %copy.29 = f32[3,2048,1]{2,1,0:T(8,128)} copy(f32[3,2048,1]{1,2,0:T(1,128)} %collective-permute-done.2) | data formatting | bytes 49152 | tf_op jit(solution)/shard_map/ppermute | solution.py:17
  54.8 2.9 %copy.31 = f32[3,2048,1]{2,1,0:T(8,128)} copy(f32[3,2048,1]{1,2,0:T(1,128)} %collective-permute-done.3) | data formatting | bytes 49152 | tf_op jit(solution)/shard_map/ppermute | solution.py:15
  57.7 3.5 %fusion.28 = f32[1,2048,128]{2,1,0:T(8,128)} fusion(f32[3,2048,128]{2,1,0:T(8,128)S(1)} %get-tuple-element.11, f32[3,2048,1]{2,1,0:T(8,128)} %copy.31, f32[3,2048,1]{2,1,0:T(8,128)} %copy.29), kind=kLoop, calls=%fused_computation.41 | loop fusion | flops 1048576 | bytes 4243456 | tf_op jit(solution)/shard_map/mul | solution.py:92
  61.2 1.6 copy.34
  62.8 8.2 %bitcast_add_fusion = f32[4,1,8,256,128]{3,4,2,0,1:T(8,128)} fusion(f32[1,1,8,256,128]{3,4,2,0,1:T(8,128)} %copy.35, f32[1,1,8,256,128]{3,4,2,0,1:T(8,128)S(1)} %copy.34, f32[1,1,8,256,128]{3,4,2,0,1:T(8,128)} %copy.33, f32[1,1,8,256,128]{3,4,2,0,1:T(8,128)} %copy.32, f32[256,256]{1,0:T(8,128)S(1)} %copy-done), kind=kOutput, calls=%fused_computation.5 | convolution fusion | flops 3229614080 | bytes 8650752 | tf_op jit(solution)/shard_map/...bir,ij->...bjr/dot_general | solution.py:37
  71.0 5.4 %copy.36 = f32[4,1,8,256,128]{4,3,2,0,1:T(8,128)} copy(f32[4,1,8,256,128]{3,4,2,0,1:T(8,128)} %bitcast_add_fusion) | data formatting | bytes 8388608 | tf_op jit(solution)/shard_map/add | solution.py:37
  76.4 6.0 %multiply_add_fusion = f32[4,2048,128]{2,1,0:T(8,128)S(1)} fusion(f32[4,2048,128]{2,1,0:T(8,128)} %bitcast.136, f32[128,128]{1,0:T(8,128)S(1)} %copy-done.9), kind=kOutput, calls=%fused_computation.8 | convolution fusion | flops 1612709888 | bytes 8454144 | tf_op jit(solution)/shard_map/...xci,ij->...xcj/dot_general | solution.py:41
  82.8 0.5 copy-done.8
  83.5 0.5 fusion.14
  85.5 1.7 fusion.3
  87.1 1.9 collective-permute-start.4
  89.1 4.4 %collective-permute-done.4 = f32[4,64,16,128]{3,2,1,0:T(8,128)} collective-permute-done((f32[4,64,16,128]{3,2,1,0:T(8,128)}, f32[4,64,16,128]{3,2,1,0:T(8,128)}, u32[]{:S(2)}, u32[]{:S(2)}) %collective-permute-start.4) | collective-permute-done | bytes 2097184 | tf_op jit(solution)/shard_map/ppermute | solution.py:27
  93.5 1.4 broadcast_select_fusion
  95.0 2.0 multiply_add_fusion.1
  97.0 1.3 copy-done.4
  98.4 1.1 dynamic-slice_bitcast_fusion
  99.5 2.0 collective-permute-start.5
  101.5 26.2 %collective-permute-done.5 = f32[4,32,16,128]{3,2,1,0:T(8,128)S(1)} collective-permute-done((f32[4,32,16,128]{3,2,1,0:T(8,128)}, f32[4,32,16,128]{3,2,1,0:T(8,128)S(1)}, u32[]{:S(2)}, u32[]{:S(2)}) %collective-permute-start.5) | collective-permute-done | bytes 1048608 | tf_op jit(solution)/shard_map/ppermute | solution.py:27
  127.7 1.8 bitcast_select_fusion.1
  129.5 1.4 fusion.30
  131.0 1.9 collective-permute-start.6
  133.0 25.3 %collective-permute-done.6 = f32[4,16,16,128]{3,2,1,0:T(8,128)S(1)} collective-permute-done((f32[4,16,16,128]{3,2,1,0:T(8,128)S(1)}, f32[4,16,16,128]{3,2,1,0:T(8,128)S(1)}, u32[]{:S(2)}, u32[]{:S(2)}) %collective-permute-start.6) | collective-permute-done | bytes 524320 | tf_op jit(solution)/shard_map/ppermute | solution.py:27
  158.5 6.5 %collective-permute-start.7 = (f32[4,8,16,128]{3,2,1,0:T(8,128)S(1)}, f32[4,8,16,128]{3,2,1,0:T(8,128)S(1)}, u32[]{:S(2)}, u32[]{:S(2)}) collective-permute-start(f32[4,8,16,128]{3,2,1,0:T(8,128)S(1)} %dynamic-slice_bitcast_fusion.2), channel_id=1, source_target_pairs={{0,32},{4,36},{8,40},{12,44},{16,48},{20,52},{24,56},{28,60},{32,0... | collective-permute-start | bytes 786440 | tf_op jit(solution)/shard_map/ppermute | solution.py:27
  165.0 23.4 %collective-permute-done.7 = f32[4,8,16,128]{3,2,1,0:T(8,128)S(1)} collective-permute-done((f32[4,8,16,128]{3,2,1,0:T(8,128)S(1)}, f32[4,8,16,128]{3,2,1,0:T(8,128)S(1)}, u32[]{:S(2)}, u32[]{:S(2)}) %collective-permute-start.7) | collective-permute-done | bytes 262176 | tf_op jit(solution)/shard_map/ppermute | solution.py:27
  188.6 9.4 %collective-permute-start.8 = (f32[4,4,16,128]{3,2,1,0:T(8,128)S(1)}, f32[4,4,16,128]{3,2,1,0:T(8,128)S(1)}, u32[]{:S(2)}, u32[]{:S(2)}) collective-permute-start(f32[4,4,16,128]{3,2,1,0:T(8,128)S(1)} %dynamic-slice_bitcast_fusion.3), channel_id=1, source_target_pairs={{0,64},{4,68},{8,72},{12,76},{16,80},{20,84},{24,88},{28,92},{32,9... | collective-permute-start | bytes 393224 | tf_op jit(solution)/shard_map/ppermute | solution.py:27
  198.1 10.7 %collective-permute-done.8 = f32[4,4,16,128]{3,2,1,0:T(8,128)S(1)} collective-permute-done((f32[4,4,16,128]{3,2,1,0:T(8,128)S(1)}, f32[4,4,16,128]{3,2,1,0:T(8,128)S(1)}, u32[]{:S(2)}, u32[]{:S(2)}) %collective-permute-start.8) | collective-permute-done | bytes 131104 | tf_op jit(solution)/shard_map/ppermute | solution.py:27
  208.9 2.4 %collective-permute-start.9 = (f32[4,2,16,128]{3,2,1,0:T(8,128)S(1)}, f32[4,2,16,128]{3,2,1,0:T(8,128)S(1)}, u32[]{:S(2)}, u32[]{:S(2)}) collective-permute-start(f32[4,2,16,128]{3,2,1,0:T(8,128)S(1)} %dynamic-slice_bitcast_fusion.4), channel_id=1, source_target_pairs={{0,128},{4,132},{8,136},{12,140},{16,144},{20,148},{24,152},{28,15... | collective-permute-start | bytes 196616 | tf_op jit(solution)/shard_map/ppermute | solution.py:27
  211.3 3.7 %collective-permute-done.9 = f32[4,2,16,128]{3,2,1,0:T(8,128)S(1)} collective-permute-done((f32[4,2,16,128]{3,2,1,0:T(8,128)S(1)}, f32[4,2,16,128]{3,2,1,0:T(8,128)S(1)}, u32[]{:S(2)}, u32[]{:S(2)}) %collective-permute-start.9) | collective-permute-done | bytes 65568 | tf_op jit(solution)/shard_map/ppermute | solution.py:27
  215.1 3.9 %collective-permute-start.10 = (f32[4,1,16,128]{3,2,1,0:T(8,128)S(1)}, f32[4,1,16,128]{3,2,1,0:T(8,128)S(1)}, u32[]{:S(2)}, u32[]{:S(2)}) collective-permute-start(f32[4,1,16,128]{3,2,1,0:T(8,128)S(1)} %constant_dynamic-slice_fusion), channel_id=1, source_target_pairs={{0,256},{4,260},{8,264},{12,268},{16,272},{20,276},{24,280},{28,28... | collective-permute-start | bytes 98312 | tf_op jit(solution)/shard_map/ppermute | solution.py:27
  219.0 3.4 %collective-permute-done.10 = f32[4,1,16,128]{3,2,1,0:T(8,128)S(1)} collective-permute-done((f32[4,1,16,128]{3,2,1,0:T(8,128)S(1)}, f32[4,1,16,128]{3,2,1,0:T(8,128)S(1)}, u32[]{:S(2)}, u32[]{:S(2)}) %collective-permute-start.10) | collective-permute-done | bytes 32800 | tf_op jit(solution)/shard_map/ppermute | solution.py:27
  222.4 0.6 add_bitcast_fusion
  (54 shorter events, 3.2 us)
Async XLA Ops:
  0.0 62.8 %copy-start = (f32[256,256]{1,0:T(8,128)S(1)}, f32[256,256]{1,0:T(8,128)}, u32[]{:S(2)}) copy-start(f32[256,256]{1,0:T(8,128)} %param.12) | copy-start | bytes 786436
  0.0 23.7 %copy-start.6 = (f32[1,2048,128]{2,1,0:T(8,128)S(1)}, f32[1,2048,128]{2,1,0:T(8,128)}, u32[]{:S(2)}) copy-start(f32[1,2048,128]{2,1,0:T(8,128)} %param.7) | copy-start | bytes 3145732
  0.0 23.6 %collective-permute-start = (f32[1,2048,128]{2,1,0:T(8,128)}, f32[1,2048,128]{2,1,0:T(8,128)S(1)}, u32[]{:S(2)}, u32[]{:S(2)}) collective-permute-start(f32[1,2048,128]{2,1,0:T(8,128)} %param.7), channel_id=1, source_target_pairs={{0,4},{4,8},{8,12},{12,16},{16,20},{20,24},{24,28},{28,32},{32,36}... | collective-permute-start | bytes 3145736 | tf_op jit(solution)/shard_map/ppermute | solution.py:15
  2.1 23.4 %collective-permute-start.1 = (f32[1,2048,128]{2,1,0:T(8,128)}, f32[1,2048,128]{2,1,0:T(8,128)S(1)}, u32[]{:S(2)}, u32[]{:S(2)}) collective-permute-start(f32[1,2048,128]{2,1,0:T(8,128)} %param.7), channel_id=1, source_target_pairs={{4,0},{8,4},{12,8},{16,12},{20,16},{24,20},{28,24},{32,28},{36,32}... | collective-permute-start | bytes 3145736 | tf_op jit(solution)/shard_map/ppermute | solution.py:17
  33.2 18.7 %collective-permute-start.2 = (f32[3,2048,1]{1,2,0:T(1,128)}, f32[3,2048,1]{1,2,0:T(1,128)}, u32[]{:S(2)}, u32[]{:S(2)}) collective-permute-start(f32[3,2048,1]{1,2,0:T(1,128)} %copy.28), channel_id=1, source_target_pairs={{1,0},{2,1},{3,2},{5,4},{6,5},{7,6},{9,8},{10,9},{11,10},{13,12},{... | collective-permute-start | bytes 73736 | tf_op jit(solution)/shard_map/ppermute | solution.py:17
  37.5 17.4 %collective-permute-start.3 = (f32[3,2048,1]{1,2,0:T(1,128)}, f32[3,2048,1]{1,2,0:T(1,128)}, u32[]{:S(2)}, u32[]{:S(2)}) collective-permute-start(f32[3,2048,1]{1,2,0:T(1,128)} %copy.30), channel_id=1, source_target_pairs={{0,1},{1,2},{2,3},{4,5},{5,6},{6,7},{8,9},{9,10},{10,11},{12,13},{... | collective-permute-start | bytes 73736 | tf_op jit(solution)/shard_map/ppermute | solution.py:15
  71.0 5.4 %copy-start.9 = (f32[128,128]{1,0:T(8,128)S(1)}, f32[128,128]{1,0:T(8,128)}, u32[]{:S(2)}) copy-start(f32[128,128]{1,0:T(8,128)} %param.13) | copy-start | bytes 196612
  82.4 0.9 copy-start.8
  83.4 1.0 slice-start
  85.5 1.7 copy-start.2
  87.1 6.4 %collective-permute-start.4 = (f32[4,64,16,128]{3,2,1,0:T(8,128)}, f32[4,64,16,128]{3,2,1,0:T(8,128)}, u32[]{:S(2)}, u32[]{:S(2)}) collective-permute-start(f32[4,64,16,128]{3,2,1,0:T(8,128)} %fusion.3), channel_id=1, source_target_pairs={{0,4},{4,0},{8,12},{12,8},{16,20},{20,16},{24,28},{28,24},{32,36},... | collective-permute-start | bytes 6291464 | tf_op jit(solution)/shard_map/ppermute | solution.py:27
  89.1 5.9 %copy-start.3 = (f32[1,64,2,16,128]{4,3,2,1,0:T(8,128)S(1)}, f32[1,64,2,16,128]{4,3,2,1,0:T(8,128)}, u32[]{:S(2)}) copy-start(f32[1,64,2,16,128]{4,3,2,1,0:T(8,128)} %copy-done.2) | copy-start | bytes 3145732
  97.0 1.3 copy-start.4
  99.5 30.1 %copy-start.5 = (f32[4,64,16,128]{3,2,1,0:T(8,128)S(1)}, f32[4,64,16,128]{3,2,1,0:T(8,128)}, u32[]{:S(2)}) copy-start(f32[4,64,16,128]{3,2,1,0:T(8,128)} %copy-done.4) | copy-start | bytes 6291460
  99.5 28.3 %collective-permute-start.5 = (f32[4,32,16,128]{3,2,1,0:T(8,128)}, f32[4,32,16,128]{3,2,1,0:T(8,128)S(1)}, u32[]{:S(2)}, u32[]{:S(2)}) collective-permute-start(f32[4,32,16,128]{3,2,1,0:T(8,128)} %dynamic-slice_bitcast_fusion), channel_id=1, source_target_pairs={{0,8},{4,12},{8,0},{12,4},{16,24},{20,28},{24,16},{28,20},{32,40},... | collective-permute-start | bytes 3145736 | tf_op jit(solution)/shard_map/ppermute | solution.py:27
  127.7 1.8 copy-start.7
  131.0 27.2 %collective-permute-start.6 = (f32[4,16,16,128]{3,2,1,0:T(8,128)S(1)}, f32[4,16,16,128]{3,2,1,0:T(8,128)S(1)}, u32[]{:S(2)}, u32[]{:S(2)}) collective-permute-start(f32[4,16,16,128]{3,2,1,0:T(8,128)S(1)} %dynamic-slice_bitcast_fusion.1), channel_id=1, source_target_pairs={{0,16},{4,20},{8,24},{12,28},{16,0},{20,4},{24,8},{28,12},{32,48},... | collective-permute-start | bytes 1572872 | tf_op jit(solution)/shard_map/ppermute | solution.py:27
  158.2 64.8 %copy-start.1 = (f32[256,256]{1,0:T(8,128)S(1)}, f32[256,256]{1,0:T(8,128)}, u32[]{:S(2)}) copy-start(f32[256,256]{1,0:T(8,128)} %param.12) | copy-start | bytes 786436
  158.5 29.9 %collective-permute-start.7 = (f32[4,8,16,128]{3,2,1,0:T(8,128)S(1)}, f32[4,8,16,128]{3,2,1,0:T(8,128)S(1)}, u32[]{:S(2)}, u32[]{:S(2)}) collective-permute-start(f32[4,8,16,128]{3,2,1,0:T(8,128)S(1)} %dynamic-slice_bitcast_fusion.2), channel_id=1, source_target_pairs={{0,32},{4,36},{8,40},{12,44},{16,48},{20,52},{24,56},{28,60},{32,0... | collective-permute-start | bytes 786440 | tf_op jit(solution)/shard_map/ppermute | solution.py:27
  188.6 20.2 %collective-permute-start.8 = (f32[4,4,16,128]{3,2,1,0:T(8,128)S(1)}, f32[4,4,16,128]{3,2,1,0:T(8,128)S(1)}, u32[]{:S(2)}, u32[]{:S(2)}) collective-permute-start(f32[4,4,16,128]{3,2,1,0:T(8,128)S(1)} %dynamic-slice_bitcast_fusion.3), channel_id=1, source_target_pairs={{0,64},{4,68},{8,72},{12,76},{16,80},{20,84},{24,88},{28,92},{32,9... | collective-permute-start | bytes 393224 | tf_op jit(solution)/shard_map/ppermute | solution.py:27
  208.9 6.2 %collective-permute-start.9 = (f32[4,2,16,128]{3,2,1,0:T(8,128)S(1)}, f32[4,2,16,128]{3,2,1,0:T(8,128)S(1)}, u32[]{:S(2)}, u32[]{:S(2)}) collective-permute-start(f32[4,2,16,128]{3,2,1,0:T(8,128)S(1)} %dynamic-slice_bitcast_fusion.4), channel_id=1, source_target_pairs={{0,128},{4,132},{8,136},{12,140},{16,144},{20,148},{24,152},{28,15... | collective-permute-start | bytes 196616 | tf_op jit(solution)/shard_map/ppermute | solution.py:27
  215.1 7.3 %collective-permute-start.10 = (f32[4,1,16,128]{3,2,1,0:T(8,128)S(1)}, f32[4,1,16,128]{3,2,1,0:T(8,128)S(1)}, u32[]{:S(2)}, u32[]{:S(2)}) collective-permute-start(f32[4,1,16,128]{3,2,1,0:T(8,128)S(1)} %constant_dynamic-slice_fusion), channel_id=1, source_target_pairs={{0,256},{4,260},{8,264},{12,268},{16,272},{20,276},{24,280},{28,28... | collective-permute-start | bytes 98312 | tf_op jit(solution)/shard_map/ppermute | solution.py:27
where the time goes:
time: 224 us; the launch traced here: 223 us
  waiting for transfers between devices  105 us (47%)
  starting transfers between devices  47.4 us (21%)
  local copies, waits for them, and re-layouts  33.9 us (15%)
  other arithmetic  19.5 us (9%)
  matrix products  16.7 us (7%)
    ppermute x7, waiting for transfers between devices, partner(): return lax.ppermute(value, axis, pairs)  97.2 us
    ppermute x7, starting transfers between devices, partner(): return lax.ppermute(value, axis, pairs)  28.1 us
    ppermute x2, starting transfers between devices, extended(): lax.ppermute(head, axis, [((i + 1) % count, i) for i in range(ends)])  12.1 us
    another operation x4, local copies, waits for them, and re-layouts, local(): jnp.stack([distance, grad_x, grad_y, grad_z])  9.27 us
    dot_general x1, matrix products, resample(): jnp.einsum('...bir,ij->...bjr', blocked, kernel_x, precision=lax.Precisio...  8.23 us
    ppermute x2, waiting for transfers between devices, extended(): lax.ppermute(tail, axis, [(i, (i + 1) % count) for i in range(ends)])  7.44 us
    ppermute x2, starting transfers between devices, extended(): lax.ppermute(tail, axis, [(i, (i + 1) % count) for i in range(ends)])  7.18 us
    slice x2, local copies, waits for them, and re-layouts, extended(): head = lax.slice_in_dim(cells, 0, width, axis=dim)  6.58 us
  transfers between devices with their start and end apart: 11, of which 9 were waited for; matrix products, arithmetic and copies ran while one was open for 9% of the time, Pallas kernels for 0%

commit v1 on v0

v1 whole, which is shorter than its diff:
```python
import jax
import jax.numpy as jnp
from jax import lax
from jax.experimental import pallas as pl
from jax.experimental.pallas import tpu as pltpu
from jax.sharding import Mesh, PartitionSpec as P

GROUP = ("zp", "core")
GROUPS = ("x", "zg")
WIDE = ("x", "zg", "zp", "core")
BLOCKS = 8
SLICES = 8
PIECES = 16
COLS = 256
ROWS = 128
PIECE = COLS // PIECES
FIELDS = 4
VMEM = pl.BlockSpec(memory_space=pltpu.VMEM)
SMEM = pl.BlockSpec(memory_space=pltpu.SMEM)


def halves(value):
    high = value.astype(jnp.bfloat16)
    low = (value - high.astype(jnp.float32)).astype(jnp.bfloat16)
    return high, low


def product(a, b, dims=((1,), (0,))):
    a_high, a_low = a
    b_high, b_low = b

    def one(p, q):
        return lax.dot_general(p, q, (dims, ((), ())), preferred_element_type=jnp.float32)

    return one(a_high, b_high) + (one(a_low, b_high) + one(a_high, b_low))


def ones_where(condition):
    return jnp.where(condition, 1.0, 0.0)


def iota(shape, dim):
    return lax.broadcasted_iota(jnp.int32, shape, dim)


def edges_kernel(cells, material, occupancy, first, last, base):
    ends = ones_where(
        (iota((8, ROWS), 0) == 0) & (iota((8, ROWS), 1) == 0)
        | (iota((8, ROWS), 0) == 1) & (iota((8, ROWS), 1) == ROWS - 1)
    )
    taken = lax.dot_general(
        ends,
        cells[0],
        (((1,), (1,)), ((), ())),
        precision=lax.Precision.HIGHEST,
        preferred_element_type=jnp.float32,
    )
    for part in range(2 * BLOCKS):
        first[part : part + 1] = taken[0:1, part * ROWS : (part + 1) * ROWS]
        last[part : part + 1] = taken[1:2, part * ROWS : (part + 1) * ROWS]
    brick_rows = material.shape[2]
    lane = iota((brick_rows, ROWS), 1)
    row = iota((brick_rows, ROWS), 0)
    kinds = material[0].astype(jnp.float32).reshape(BLOCKS, 4, 8, brick_rows)
    masks = occupancy[0].astype(jnp.float32).reshape(BLOCKS, 4, 8, brick_rows)
    packed = jnp.zeros((BLOCKS * 8, ROWS), jnp.float32)
    for part in range(4):
        at = 2 * brick_rows * part
        packed += jnp.dot(
            kinds[:, part].reshape(BLOCKS * 8, brick_rows),
            ones_where(lane == row + at),
            preferred_element_type=jnp.float32,
        )
        packed += jnp.dot(
            masks[:, part].reshape(BLOCKS * 8, brick_rows),
            ones_where(lane == row + (at + brick_rows)),
            preferred_element_type=jnp.float32,
        )
    none = jnp.zeros((1, ROWS), jnp.float32)
    for block in range(BLOCKS):
        left, right = block * COLS - 1, (block + 1) * COLS
        base[block, 0:1] = cells[0, left : left + 1] if block else none
        base[block, 1:2] = cells[0, right : right + 1] if block < BLOCKS - 1 else none
        base[block, 2:8] = jnp.zeros((6, ROWS), jnp.float32)
        base[block, 8:16] = packed[block * 8 : block * 8 + 8]


def block_kernel(
    cells, small, before, after, colours, absorb, kernel_x, kernel_y, image, fields, bricks, step
):
    eye_y = ones_where(iota((ROWS, ROWS), 0) == iota((ROWS, ROWS), 1))
    along_y = 0.5 * eye_y + kernel_y[...]
    none = jnp.zeros((1, ROWS), jnp.float32)
    slope_y = 0.5 * (
        jnp.concatenate([none, along_y[:-1]], axis=0) - jnp.concatenate([along_y[1:], none], axis=0)
    )
    both_y = halves(jnp.concatenate([along_y, slope_y], axis=1))
    only_y = halves(along_y)
    eye_x = ones_where(iota((COLS, COLS), 0) == iota((COLS, COLS), 1))
    along_x = halves((0.5 * eye_x + kernel_x[...]).T)
    beside = jnp.concatenate(
        [
            jnp.concatenate([small[s, 2 + 2 * side : 3 + 2 * side], small[s, 3 + 2 * side : 4 + 2 * side]], axis=1)
            for s in range(SLICES)
            for side in range(2)
        ],
        axis=0,
    )
    beside = halves(beside.T)
    corner = jnp.concatenate([-0.5 * along_y[0:1], 0.5 * along_y[-1:]], axis=0)
    column_ends = product(halves(small[:, 0:2, :].reshape(2 * SLICES, ROWS)), only_y)
    outer = product(
        halves(jnp.concatenate([before[...], after[...]], axis=0)), only_y
    )
    outer = jnp.concatenate([outer[:COLS], outer[COLS:]], axis=1)
    outer = product(along_x, halves(outer))
    fields[0] = outer[:, :ROWS]
    fields[SLICES + 1] = outer[:, ROWS:]
    for pair in range(SLICES // 2):
        parts = []
        for s in (2 * pair, 2 * pair + 1):
            rows = product(halves(cells[s]), both_y)
            value = rows[:, :ROWS]
            row = iota((2 * SLICES, ROWS), 0)
            wanted = jnp.where(row == 2 * s, corner[0:1], 0.0) + jnp.where(row == 2 * s + 1, corner[1:2], 0.0)
            slope = rows[:, ROWS:] + product(beside, halves(wanted))
            ahead = jnp.concatenate([value[1:], column_ends[2 * s + 1 : 2 * s + 2]], axis=0)
            behind = jnp.concatenate([column_ends[2 * s : 2 * s + 1], value[:-1]], axis=0)
            parts += [value, 0.5 * (ahead - behind), slope]
        mixed = product(along_x, halves(jnp.concatenate(parts, axis=1)))
        for i, s in enumerate((2 * pair, 2 * pair + 1)):
            at = 3 * i * ROWS
            fields[1 + s] = mixed[:, at : at + ROWS]
            u = mixed[:, at + ROWS : at + 2 * ROWS]
            v = mixed[:, at + 2 * ROWS : at + 3 * ROWS]
            fields[SLICES + 2 + s] = u * u + v * v
    codes = small[:, 8:16, :].reshape(SLICES * 8, ROWS)
    brick_rows = ROWS // 8
    masks = pltpu.roll(codes, ROWS - brick_rows, 1)
    values = [jnp.zeros_like(codes)] * FIELDS
    for label in range(colours.shape[1]):
        found = codes == float(label)
        for f in range(FIELDS):
            entry = colours[f, label] if f < 3 else absorb[label]
            values[f] = jnp.where(found, entry, values[f])
    values[3] = values[3] * masks * step
    values = jnp.concatenate(values, axis=0)
    source = iota((ROWS, 4 * ROWS), 0)
    target = iota((ROWS, 4 * ROWS), 1)
    spread = ones_where(source == (target // ROWS) * (2 * brick_rows) + (target % ROWS) // 8)
    spread = spread.astype(jnp.bfloat16)
    high, low = halves(values)
    least = (values - high.astype(jnp.float32) - low.astype(jnp.float32)).astype(jnp.bfloat16)
    grown = (
        jnp.dot(least, spread, preferred_element_type=jnp.float32)
        + jnp.dot(low, spread, preferred_element_type=jnp.float32)
        + jnp.dot(high, spread, preferred_element_type=jnp.float32)
    )
    for f in range(FIELDS):
        for s in range(SLICES):
            for part in range(4):
                bricks[f, s, 8 * part : 8 * part + 8] = grown[
                    (f * SLICES + s) * 8 : (f * SLICES + s) * 8 + 8, part * ROWS : (part + 1) * ROWS
                ]

    def shade(piece, _):
        for i in range(PIECE // 8):
            at = pl.ds(pl.multiple_of(piece * PIECE + 8 * i, 8), 8)
            brick = pl.ds(piece * (PIECE // 8) + i, 1)
            transmit = jnp.ones((8, ROWS), jnp.float32)
            total = [jnp.zeros((8, ROWS), jnp.float32)] * FIELDS
            for s in range(SLICES):
                d = fields[1 + s, at]
                w = 0.5 * (fields[2 + s, at] - fields[s, at])
                norm = jnp.maximum(fields[SLICES + 2 + s, at] + w * w, 0.1)
                facing = 0.25 + 0.75 * jnp.abs(w) * lax.rsqrt(norm)
                density = jnp.exp(-2.0 * d * d)
                opacity = 1.0 - jnp.exp(-bricks[3, s, brick] * density)
                weight = transmit * opacity
                shaded = weight * facing
                for f in range(3):
                    total[f] = total[f] + shaded * bricks[f, s, brick]
                total[3] = total[3] + weight
                transmit = transmit * (1.0 - opacity)
            for f in range(FIELDS):
                image[piece, f, 8 * i : 8 * i + 8] = total[f]
        return 0

    lax.fori_loop(0, PIECES, shade, 0)


def merge_kernel(parts, image):
    total = parts[0]
    for group in range(1, PIECES):
        total = total + (1.0 - total[3])[None] * parts[group]
    image[...] = total


def local(distance, occupancy, material, colours, absorb, kernel_x, kernel_y):
    slices, col_count, row_count = distance.shape
    wide = lax.axis_size(WIDE)
    narrow = lax.axis_size("narrow")
    groups = wide // SLICES
    f32 = jnp.float32
    cells = lax.all_to_all(distance.reshape(BLOCKS, COLS, ROWS), GROUP, 0, 0, tiled=True)
    first, last, base = pl.pallas_call(
        edges_kernel,
        out_shape=[
            jax.ShapeDtypeStruct((2 * BLOCKS, ROWS), f32),
            jax.ShapeDtypeStruct((2 * BLOCKS, ROWS), f32),
            jax.ShapeDtypeStruct((BLOCKS, 16, ROWS), f32),
        ],
        in_specs=[VMEM] * 3,
        out_specs=[VMEM] * 3,
        name="edges",
    )(distance, material, occupancy)
    up = lax.ppermute(last, "narrow", [(i, i + 1) for i in range(narrow - 1)])
    down = lax.ppermute(first, "narrow", [(i + 1, i) for i in range(narrow - 1)])
    small = jnp.concatenate(
        [base[:, :2], up.reshape(BLOCKS, 2, ROWS), down.reshape(BLOCKS, 2, ROWS), base[:, 6:]], axis=1
    )
    small = lax.all_to_all(small, GROUP, 0, 0, tiled=True)
    before = lax.ppermute(cells[-1], WIDE, [(i, i + SLICES) for i in range(wide - SLICES)])
    after = lax.ppermute(cells[0], WIDE, [(i + SLICES, i) for i in range(wide - SLICES)])
    step = 4.0 / (slices * wide)

    def block(*refs):
        block_kernel(*refs, step)

    pieces = pl.pallas_call(
        block,
        out_shape=jax.ShapeDtypeStruct((PIECES, FIELDS, PIECE, ROWS), f32),
        in_specs=[VMEM] * 4 + [SMEM] * 2 + [VMEM] * 2,
        out_specs=VMEM,
        scratch_shapes=[
            pltpu.VMEM((2 * SLICES + 2, COLS, ROWS), f32),
            pltpu.VMEM((FIELDS, SLICES, COLS // 8, ROWS), f32),
        ],
        compiler_params=pltpu.CompilerParams(vmem_limit_bytes=40 * 1024 * 1024),
        name="block",
    )(cells, small, before, after, colours, absorb, kernel_x, kernel_y)
    parts = lax.all_to_all(pieces, GROUPS, 0, 0, tiled=True)
    image = pl.pallas_call(
        merge_kernel,
        out_shape=jax.ShapeDtypeStruct((FIELDS, PIECE, ROWS), f32),
        in_specs=[VMEM],
        out_specs=VMEM,
        name="merge",
    )(parts)
    return lax.ppermute(
        image, WIDE, [(j * SLICES + i, i * groups + j) for j in range(groups) for i in range(SLICES)]
    )


def solution(mesh):
    wide, narrow = mesh.devices.shape
    split = Mesh(
        mesh.devices.reshape(4, wide // 32, 4, 2, narrow), ("x", "zg", "zp", "core", "narrow")
    )
    held = P(WIDE, None, "narrow")
    return jax.shard_map(
        local,
        mesh=split,
        in_specs=(held, held, held, P(), P(), P(), P()),
        out_specs=P(None, WIDE, "narrow"),
        check_vma=False,
    )
```

time: 224 us -> 126 us (0.56)
  the two profiles are of different devices: /device:TPU:2 before, /device:TPU:44 now
where the time goes in v1:
time: 126 us; the launch traced here: 125 us
  blocking collectives  39.6 us (31%)
  waiting for transfers between devices  37.8 us (30%)
  starting transfers between devices  32.9 us (26%)
  Pallas kernels  10.3 us (8%)
  local copies, waits for them, and re-layouts  3.76 us (3%)
    all_to_all x1, blocking collectives, local(): parts = lax.all_to_all(pieces, GROUPS, 0, 0, tiled=True)  39.6 us
    ppermute x1, waiting for transfers between devices, local(): lax.ppermute(image, WIDE, [(j * SLICES + i, i * groups + j) for j in rang...  14.3 us
    ppermute x1, starting transfers between devices, local(): lax.ppermute(cells[0], WIDE, [(i + SLICES, i) for i in range(wide - SLICE...  10.4 us
    ppermute x1, waiting for transfers between devices, local(): lax.ppermute(cells[0], WIDE, [(i + SLICES, i) for i in range(wide - SLICE...  9.48 us
    all_to_all x1, waiting for transfers between devices, local(): lax.all_to_all(distance.reshape(BLOCKS, COLS, ROWS), GROUP, 0, 0, tiled=T...  8.82 us
    all_to_all x1, starting transfers between devices, local(): small = lax.all_to_all(small, GROUP, 0, 0, tiled=True)  6.74 us
    all_to_all x1, starting transfers between devices, local(): lax.all_to_all(distance.reshape(BLOCKS, COLS, ROWS), GROUP, 0, 0, tiled=T...  6.14 us
    pallas_call x1, Pallas kernels, local(): pl.pallas_call(block, out_shape=jax.ShapeDtypeStruct((PIECES, FIELDS, PIE...  5.66 us
  transfers between devices with their start and end apart: 7, of which 5 were waited for; matrix products, arithmetic and copies ran while one was open for 3% of the time, Pallas kernels for 2%

profile of v1, /device:TPU:44, one launch (start us, length us, event | category | flops | bytes accessed | tf_op | source)
XLA Modules:
  0.0 125.1 jit_solution(12849968275538342097)
XLA Ops:
  0.0 0.0 copy-start.4
  0.0 6.1 %all-to-all-start = ((f32[8,256,128]{2,1,0:T(8,128)}), f32[8,256,128]{2,1,0:T(8,128)S(1)}, u32[]{:S(2)}, u32[]{:S(2)}) async-start(f32[8,256,128]{2,1,0:T(8,128)} %bitcast.7), calls=%async_computation | async-start | bytes 2097152 | tf_op jit(solution)/shard_map/all_to_all | solution.py:205
  6.1 0.0 copy-done.4
  6.1 0.0 copy-start.5
  6.1 0.7 copy.9.occupancy
  6.9 0.0 copy-done.5
  6.9 0.8 copy.8.material
  7.6 2.9 %edges.1 = (f32[16,128]{1,0:T(8,128)}, f32[16,128]{1,0:T(8,128)}, f32[8,16,128]{2,1,0:T(8,128)}) custom-call(f32[1,2048,128]{2,1,0:T(8,128)} %cells.1, s32[1,256,16]{2,1,0:T(8,128)} %copy.8.material, s32[1,256,16]{2,1,0:T(8,128)} %copy.9.occupancy), custom_call_target="tpu_custom_call" | custom-call | tf_op jit(solution)/shard_map/edges/pallas_call | solution.py:206
  10.6 3.5 %collective-permute-start = (f32[16,128]{1,0:T(8,128)}, f32[16,128]{1,0:T(8,128)S(1)}, u32[]{:S(2)}, u32[]{:S(2)}) collective-permute-start(f32[16,128]{1,0:T(8,128)} %get-tuple-element.9), channel_id=1, source_target_pairs={{0,1},{1,2},{2,3},{4,5},{5,6},{6,7},{8,9},{9,10},{10,11},{12,13},{... | collective-permute-start | bytes 24584 | tf_op jit(solution)/shard_map/ppermute | solution.py:217
  14.0 2.4 %collective-permute-start.1 = (f32[16,128]{1,0:T(8,128)}, f32[16,128]{1,0:T(8,128)S(1)}, u32[]{:S(2)}, u32[]{:S(2)}) collective-permute-start(f32[16,128]{1,0:T(8,128)} %get-tuple-element.10), channel_id=1, source_target_pairs={{1,0},{2,1},{3,2},{5,4},{6,5},{7,6},{9,8},{10,9},{11,10},{13,12},{... | collective-permute-start | bytes 24584 | tf_op jit(solution)/shard_map/ppermute | solution.py:218
  16.4 0.8 slice.12
  17.2 0.8 slice.13
  18.0 0.0 collective-permute-done
  18.0 1.8 %collective-permute-done.1 = f32[16,128]{1,0:T(8,128)S(1)} collective-permute-done((f32[16,128]{1,0:T(8,128)}, f32[16,128]{1,0:T(8,128)S(1)}, u32[]{:S(2)}, u32[]{:S(2)}) %collective-permute-start.1) | collective-permute-done | bytes 8224 | tf_op jit(solution)/shard_map/ppermute | solution.py:218
  19.8 0.6 pad_maximum_fusion
  20.4 8.8 %all-to-all-done.refs_0_ = f32[8,256,128]{2,1,0:T(8,128)S(1)} async-done(((f32[8,256,128]{2,1,0:T(8,128)}), f32[8,256,128]{2,1,0:T(8,128)S(1)}, u32[]{:S(2)}, u32[]{:S(2)}) %all-to-all-start) | async-done | bytes 1048608 | tf_op jit(solution)/shard_map/all_to_all | solution.py:205
  29.3 6.7 %all-to-all-start.1 = ((f32[8,16,128]{2,1,0:T(8,128)}), f32[8,16,128]{2,1,0:T(8,128)S(1)}, u32[]{:S(2)}, u32[]{:S(2)}) async-start(f32[8,16,128]{2,1,0:T(8,128)} %pad_maximum_fusion), calls=%async_computation.1 | async-start | bytes 131072 | tf_op jit(solution)/shard_map/all_to_all | solution.py:222
  36.0 0.0 copy-start
  36.0 0.0 copy-start.1
  36.0 0.0 copy-start.2
  36.0 0.0 copy-start.3
  36.0 10.4 %collective-permute-start.3 = (f32[256,128]{1,0:T(8,128)S(1)}, f32[256,128]{1,0:T(8,128)S(1)}, u32[]{:S(2)}, u32[]{:S(2)}) collective-permute-start(f32[256,128]{1,0:T(8,128)S(1)} %get-tuple-element.11), channel_id=1, source_target_pairs={{32,0},{36,4},{40,8},{44,12},{48,16},{52,20},{56,24},{60,28},{64,3... | collective-permute-start | bytes 393224 | tf_op jit(solution)/shard_map/ppermute | solution.py:224
  46.5 1.9 %collective-permute-start.2 = (f32[256,128]{1,0:T(8,128)S(1)}, f32[256,128]{1,0:T(8,128)S(1)}, u32[]{:S(2)}, u32[]{:S(2)}) collective-permute-start(f32[256,128]{1,0:T(8,128)S(1)} %get-tuple-element.12), channel_id=1, source_target_pairs={{0,32},{4,36},{8,40},{12,44},{16,48},{20,52},{24,56},{28,60},{32,6... | collective-permute-start | bytes 393224 | tf_op jit(solution)/shard_map/ppermute | solution.py:223
  48.4 0.0 all-to-all-done.1.refs_1_
  48.4 9.5 %collective-permute-done.3.refs_3_ = f32[256,128]{1,0:T(8,128)S(1)} collective-permute-done((f32[256,128]{1,0:T(8,128)S(1)}, f32[256,128]{1,0:T(8,128)S(1)}, u32[]{:S(2)}, u32[]{:S(2)}) %collective-permute-start.3) | collective-permute-done | bytes 131104 | tf_op jit(solution)/shard_map/ppermute | solution.py:224
  57.9 3.4 %collective-permute-done.2.refs_2_ = f32[256,128]{1,0:T(8,128)S(1)} collective-permute-done((f32[256,128]{1,0:T(8,128)S(1)}, f32[256,128]{1,0:T(8,128)S(1)}, u32[]{:S(2)}, u32[]{:S(2)}) %collective-permute-start.2) | collective-permute-done | bytes 131104 | tf_op jit(solution)/shard_map/ppermute | solution.py:223
  61.3 0.0 copy-done
  61.3 0.0 copy-done.1
  61.3 0.0 copy-done.2
  61.3 0.0 copy-done.3
  61.3 5.7 %block.1 = f32[16,4,16,128]{3,2,1,0:T(8,128)S(1)} custom-call(f32[8,256,128]{2,1,0:T(8,128)S(1)} %all-to-all-done.refs_0_, f32[8,16,128]{2,1,0:T(8,128)S(1)} %all-to-all-done.1.refs_1_, f32[256,128]{1,0:T(8,128)S(1)} %collective-permute-done.2.refs_2_, f32[256,128]{1,0:T(8,128)S(1)} %collective-permute-done.3.refs_3_, f32[3,16]{1,0:T(4,128)S(1)} %copy-done.2, ...), custom_call_target="tpu_custom_call" | custom-call | tf_op jit(solution)/shard_map/block/pallas_call | solution.py:230
  67.0 39.6 %all_to_all.15.parts = f32[16,4,16,128]{3,2,1,0:T(8,128)} all-to-all(f32[16,4,16,128]{3,2,1,0:T(8,128)S(1)} %block.1), channel_id=1, replica_groups=mesh['x'=4,'zg'=4,'zp'=4,'core'=2,'narrow'=4] {'x','zg'}, dimensions={0} | all-to-all | bytes 1048576 | tf_op jit(solution)/shard_map/all_to_all | solution.py:242
  106.6 1.7 %merge.1 = f32[4,16,128]{2,1,0:T(8,128)} custom-call(f32[16,4,16,128]{3,2,1,0:T(8,128)} %all_to_all.15.parts), custom_call_target="tpu_custom_call" | custom-call | tf_op jit(solution)/shard_map/merge/pallas_call | solution.py:243
  108.3 1.9 %collective-permute-start.4 = (f32[4,16,128]{2,1,0:T(8,128)}, f32[4,16,128]{2,1,0:T(8,128)S(1)}, u32[]{:S(2)}, u32[]{:S(2)}) collective-permute-start(f32[4,16,128]{2,1,0:T(8,128)} %merge.1), channel_id=1, source_target_pairs={{0,0},{4,64},{8,128},{12,192},{16,256},{20,320},{24,384},{28,448},... | collective-permute-start | bytes 98312 | tf_op jit(solution)/shard_map/ppermute | solution.py:250
  110.2 14.3 %collective-permute-done.4 = f32[4,16,128]{2,1,0:T(8,128)S(1)} collective-permute-done((f32[4,16,128]{2,1,0:T(8,128)}, f32[4,16,128]{2,1,0:T(8,128)S(1)}, u32[]{:S(2)}, u32[]{:S(2)}) %collective-permute-start.4) | collective-permute-done | bytes 32800 | tf_op jit(solution)/shard_map/ppermute | solution.py:250
  124.5 0.6 copy.11
  (1 shorter events, 0.0 us)
Async XLA Ops:
  0.0 6.1 %copy-start.4 = (s32[1,256,16]{1,2,0:T(8,128)S(1)}, s32[1,256,16]{1,2,0:T(8,128)}, u32[]{:S(2)}) copy-start(s32[1,256,16]{1,2,0:T(8,128)} %param.8) | copy-start | bytes 49156
  0.0 29.3 %all-to-all-start = ((f32[8,256,128]{2,1,0:T(8,128)}), f32[8,256,128]{2,1,0:T(8,128)S(1)}, u32[]{:S(2)}, u32[]{:S(2)}) async-start(f32[8,256,128]{2,1,0:T(8,128)} %bitcast.7), calls=%async_computation | async-start | bytes 2097152 | tf_op jit(solution)/shard_map/all_to_all | solution.py:205
  6.1 0.7 copy-start.5
  10.6 7.5 %collective-permute-start = (f32[16,128]{1,0:T(8,128)}, f32[16,128]{1,0:T(8,128)S(1)}, u32[]{:S(2)}, u32[]{:S(2)}) collective-permute-start(f32[16,128]{1,0:T(8,128)} %get-tuple-element.9), channel_id=1, source_target_pairs={{0,1},{1,2},{2,3},{4,5},{5,6},{6,7},{8,9},{9,10},{10,11},{12,13},{... | collective-permute-start | bytes 24584 | tf_op jit(solution)/shard_map/ppermute | solution.py:217
  14.0 5.8 %collective-permute-start.1 = (f32[16,128]{1,0:T(8,128)}, f32[16,128]{1,0:T(8,128)S(1)}, u32[]{:S(2)}, u32[]{:S(2)}) collective-permute-start(f32[16,128]{1,0:T(8,128)} %get-tuple-element.10), channel_id=1, source_target_pairs={{1,0},{2,1},{3,2},{5,4},{6,5},{7,6},{9,8},{10,9},{11,10},{13,12},{... | collective-permute-start | bytes 24584 | tf_op jit(solution)/shard_map/ppermute | solution.py:218
  29.3 19.1 %all-to-all-start.1 = ((f32[8,16,128]{2,1,0:T(8,128)}), f32[8,16,128]{2,1,0:T(8,128)S(1)}, u32[]{:S(2)}, u32[]{:S(2)}) async-start(f32[8,16,128]{2,1,0:T(8,128)} %pad_maximum_fusion), calls=%async_computation.1 | async-start | bytes 131072 | tf_op jit(solution)/shard_map/all_to_all | solution.py:222
  36.0 25.3 %copy-start = (f32[256,256]{1,0:T(8,128)S(1)}, f32[256,256]{1,0:T(8,128)}, u32[]{:S(2)}) copy-start(f32[256,256]{1,0:T(8,128)} %refs_6_.1) | copy-start | bytes 786436
  36.0 25.3 %copy-start.1 = (f32[128,128]{1,0:T(8,128)S(1)}, f32[128,128]{1,0:T(8,128)}, u32[]{:S(2)}) copy-start(f32[128,128]{1,0:T(8,128)} %refs_7_.1) | copy-start | bytes 196612
  36.0 25.3 %copy-start.2 = (f32[3,16]{1,0:T(4,128)S(1)}, f32[3,16]{1,0:T(4,128)}, u32[]{:S(2)}) copy-start(f32[3,16]{1,0:T(4,128)} %refs_4_.1) | copy-start | bytes 580
  36.0 25.3 %copy-start.3 = (f32[16]{0:T(128)S(1)}, f32[16]{0:T(128)}, u32[]{:S(2)}) copy-start(f32[16]{0:T(128)} %refs_5_.1) | copy-start | bytes 196
  36.0 21.8 %collective-permute-start.3 = (f32[256,128]{1,0:T(8,128)S(1)}, f32[256,128]{1,0:T(8,128)S(1)}, u32[]{:S(2)}, u32[]{:S(2)}) collective-permute-start(f32[256,128]{1,0:T(8,128)S(1)} %get-tuple-element.11), channel_id=1, source_target_pairs={{32,0},{36,4},{40,8},{44,12},{48,16},{52,20},{56,24},{60,28},{64,3... | collective-permute-start | bytes 393224 | tf_op jit(solution)/shard_map/ppermute | solution.py:224
  46.5 14.8 %collective-permute-start.2 = (f32[256,128]{1,0:T(8,128)S(1)}, f32[256,128]{1,0:T(8,128)S(1)}, u32[]{:S(2)}, u32[]{:S(2)}) collective-permute-start(f32[256,128]{1,0:T(8,128)S(1)} %get-tuple-element.12), channel_id=1, source_target_pairs={{0,32},{4,36},{8,40},{12,44},{16,48},{20,52},{24,56},{28,60},{32,6... | collective-permute-start | bytes 393224 | tf_op jit(solution)/shard_map/ppermute | solution.py:223
  108.3 16.2 %collective-permute-start.4 = (f32[4,16,128]{2,1,0:T(8,128)}, f32[4,16,128]{2,1,0:T(8,128)S(1)}, u32[]{:S(2)}, u32[]{:S(2)}) collective-permute-start(f32[4,16,128]{2,1,0:T(8,128)} %merge.1), channel_id=1, source_target_pairs={{0,0},{4,64},{8,128},{12,192},{16,256},{20,320},{24,384},{28,448},... | collective-permute-start | bytes 98312 | tf_op jit(solution)/shard_map/ppermute | solution.py:250

commit v2 on v1

--- a/solution.py
+++ b/solution.py
@@ -1,19 +1,19 @@
+import functools
+
 import jax
 import jax.numpy as jnp
 from jax import lax
 from jax.experimental import pallas as pl
 from jax.experimental.pallas import tpu as pltpu
-from jax.sharding import Mesh, PartitionSpec as P
-
-GROUP = ("zp", "core")
-GROUPS = ("x", "zg")
-WIDE = ("x", "zg", "zp", "core")
+from jax.sharding import PartitionSpec as P
+
 BLOCKS = 8
 SLICES = 8
-PIECES = 16
 COLS = 256
 ROWS = 128
-PIECE = COLS // PIECES
+PIECE = 16
+NEAR = 8
+PART = COLS // NEAR
 FIELDS = 4
 VMEM = pl.BlockSpec(memory_space=pltpu.VMEM)
 SMEM = pl.BlockSpec(memory_space=pltpu.SMEM)
@@ -55,9 +55,11 @@
         precision=lax.Precision.HIGHEST,
         preferred_element_type=jnp.float32,
     )
-    for part in range(2 * BLOCKS):
-        first[part : part + 1] = taken[0:1, part * ROWS : (part + 1) * ROWS]
-        last[part : part + 1] = taken[1:2, part * ROWS : (part + 1) * ROWS]
+    for block in range(BLOCKS):
+        for part in range(2):
+            at = (2 * block + part) * ROWS
+            first[block, part : part + 1] = taken[0:1, at : at + ROWS]
+            last[block, part : part + 1] = taken[1:2, at : at + ROWS]
     brick_rows = material.shape[2]
     lane = iota((brick_rows, ROWS), 1)
     row = iota((brick_rows, ROWS), 0)
@@ -85,9 +87,16 @@
         base[block, 8:16] = packed[block * 8 : block * 8 + 8]
 
 
+def pack_kernel(base, up, down, small):
+    small[...] = base[...]
+    small[:, 2:4] = up[...]
+    small[:, 4:6] = down[...]
+
+
 def block_kernel(
-    cells, small, before, after, colours, absorb, kernel_x, kernel_y, image, fields, bricks, step
+    step, flip, cells, small, before, after, colours, absorb, kernel_x, kernel_y, image, fields, bricks
 ):
+    place = [s ^ flip[0] for s in range(SLICES)]
     eye_y = ones_where(iota((ROWS, ROWS), 0) == iota((ROWS, ROWS), 1))
     along_y = 0.5 * eye_y + kernel_y[...]
     none = jnp.zeros((1, ROWS), jnp.float32)
@@ -100,7 +109,7 @@
     along_x = halves((0.5 * eye_x + kernel_x[...]).T)
     beside = jnp.concatenate(
         [
-            jnp.concatenate([small[s, 2 + 2 * side : 3 + 2 * side], small[s, 3 + 2 * side : 4 + 2 * side]], axis=1)
+            jnp.concatenate([small[place[s], 2 + 2 * side : 3 + 2 * side], small[place[s], 3 + 2 * side : 4 + 2 * side]], axis=1)
             for s in range(SLICES)
             for side in range(2)
         ],
@@ -108,7 +117,8 @@
     )
     beside = halves(beside.T)
     corner = jnp.concatenate([-0.5 * along_y[0:1], 0.5 * along_y[-1:]], axis=0)
-    column_ends = product(halves(small[:, 0:2, :].reshape(2 * SLICES, ROWS)), only_y)
+    column_ends = jnp.concatenate([small[place[s], 0:2] for s in range(SLICES)], axis=0)
+    column_ends = product(halves(column_ends), only_y)
     outer = product(
         halves(jnp.concatenate([before[...], after[...]], axis=0)), only_y
     )
@@ -119,7 +129,7 @@
     for pair in range(SLICES // 2):
         parts = []
         for s in (2 * pair, 2 * pair + 1):
-            rows = product(halves(cells[s]), both_y)
+            rows = product(halves(cells[place[s]]), both_y)
             value = rows[:, :ROWS]
             row = iota((2 * SLICES, ROWS), 0)
             wanted = jnp.where(row == 2 * s, corner[0:1], 0.0) + jnp.where(row == 2 * s + 1, corner[1:2], 0.0)
@@ -163,105 +173,172 @@
                     (f * SLICES + s) * 8 : (f * SLICES + s) * 8 + 8, part * ROWS : (part + 1) * ROWS
                 ]
 
-    def shade(piece, _):
+    def shade(piece, part):
+        row = piece * (PART // 8) + part
+        at = pl.ds(pl.multiple_of(row * 8, 8), 8)
+        brick = pl.ds(row, 1)
+        transmit = jnp.ones((8, ROWS), jnp.float32)
+        total = [jnp.zeros((8, ROWS), jnp.float32)] * FIELDS
+        for s in range(SLICES):
+            d = fields[1 + s, at]
+            w = 0.5 * (fields[2 + s, at] - fields[s, at])
+            norm = jnp.maximum(fields[SLICES + 2 + s, at] + w * w, 0.1)
+            facing = 0.25 + 0.75 * jnp.abs(w) * lax.rsqrt(norm)
+            density = jnp.exp(-2.0 * d * d)
+            opacity = 1.0 - jnp.exp(-bricks[3, place[s], brick] * density)
+            weight = transmit * opacity
+            shaded = weight * facing
+            for f in range(3):
+                total[f] = total[f] + shaded * bricks[f, place[s], brick]
+            total[3] = total[3] + weight
+            transmit = transmit * (1.0 - opacity)
+        for f in range(FIELDS):
+            image[piece, f, 8 * part : 8 * part + 8] = total[f]
+
+    def shade_piece(piece, _):
+        for part in range(PART // 8):
+            shade(piece, part)
+        return 0
+
+    lax.fori_loop(0, NEAR, shade_piece, 0)
+
+
+def over(nearer, farther):
+    clear = 1.0 - nearer[3]
+    return [nearer[f] + clear * farther[f] for f in range(FIELDS)]
+
+
+def merge_near_kernel(half, parts, *out):
+    for apart in range(2):
+        chunk = half[0] ^ apart
         for i in range(PIECE // 8):
-            at = pl.ds(pl.multiple_of(piece * PIECE + 8 * i, 8), 8)
-            brick = pl.ds(piece * (PIECE // 8) + i, 1)
-            transmit = jnp.ones((8, ROWS), jnp.float32)
-            total = [jnp.zeros((8, ROWS), jnp.float32)] * FIELDS
-            for s in range(SLICES):
-                d = fields[1 + s, at]
-                w = 0.5 * (fields[2 + s, at] - fields[s, at])
-                norm = jnp.maximum(fields[SLICES + 2 + s, at] + w * w, 0.1)
-                facing = 0.25 + 0.75 * jnp.abs(w) * lax.rsqrt(norm)
-                density = jnp.exp(-2.0 * d * d)
-                opacity = 1.0 - jnp.exp(-bricks[3, s, brick] * density)
-                weight = transmit * opacity
-                shaded = weight * facing
-                for f in range(3):
-                    total[f] = total[f] + shaded * bricks[f, s, brick]
-                total[3] = total[3] + weight
-                transmit = transmit * (1.0 - opacity)
+            at = pl.ds(pl.multiple_of(chunk * PIECE + 8 * i, 8), 8)
+            total = [parts[0, f, at] for f in range(FIELDS)]
+            for group in range(1, NEAR):
+                total = over(total, [parts[group, f, at] for f in range(FIELDS)])
             for f in range(FIELDS):
-                image[piece, f, 8 * i : 8 * i + 8] = total[f]
-        return 0
-
-    lax.fori_loop(0, PIECES, shade, 0)
-
-
-def merge_kernel(parts, image):
-    total = parts[0]
-    for group in range(1, PIECES):
-        total = total + (1.0 - total[3])[None] * parts[group]
-    image[...] = total
+                out[apart][f, 8 * i : 8 * i + 8] = total[f]
+
+
+def merge_far_kernel(chunk, same, other, image):
+    even = chunk[0] == 0
+    for i in range(PIECE // 8):
+        at = slice(8 * i, 8 * i + 8)
+        pair = [(same[f, at], other[f, at]) for f in range(FIELDS)]
+        total = over([jnp.where(even, a, b) for a, b in pair], [jnp.where(even, b, a) for a, b in pair])
+        for f in range(FIELDS):
+            image[f, at] = total[f]
+
+
+def flip_of(group):
+    return ((group >> 1) & 1) * (SLICES - 2)
+
+
+def outer_blocks(distance, groups):
+    chips = SLICES // 2
+    me = lax.axis_index("wide")
+    group, chip, core = me // SLICES, me % SLICES // 2, me % 2
+    blocks = distance.reshape(chips, 2, COLS, ROWS)
+    ends = [pair for k in range(groups) for pair in ((8 * k, 8 * k + 1), (8 * k + 7, 8 * k + 6))]
+    shared = lax.ppermute(lax.dynamic_index_in_dim(blocks, 1 - core, 1, keepdims=False), "wide", ends)
+    own = lax.dynamic_index_in_dim(blocks, core, 1, keepdims=False)
+    first = chip == 0
+    given = jnp.where(jnp.where(first, core == 0, core == 1), own, shared)
+    before = after = jnp.zeros((COLS, ROWS), jnp.float32)
+    for j in range(chips):
+        back = chips - 1 - j
+        pairs = []
+        for k in range(groups - 1):
+            for c in range(2):
+                pairs.append((8 * k + 6 + c, 8 * (k + 1) + 2 * j + c))
+                pairs.append((8 * (k + 1) + c, 8 * k + 2 * back + c))
+        wanted = jnp.where(first, back ^ (flip_of(group - 1) // 2), j ^ (flip_of(group + 1) // 2))
+        came = lax.ppermute(lax.dynamic_index_in_dim(given, wanted, 0, keepdims=False), "wide", pairs)
+        before = jnp.where(chip == j, came, before)
+        after = jnp.where(chip == back, came, after)
+    return before, after
 
 
 def local(distance, occupancy, material, colours, absorb, kernel_x, kernel_y):
     slices, col_count, row_count = distance.shape
-    wide = lax.axis_size(WIDE)
+    wide = lax.axis_size("wide")
     narrow = lax.axis_size("narrow")
     groups = wide // SLICES
-    f32 = jnp.float32
-    cells = lax.all_to_all(distance.reshape(BLOCKS, COLS, ROWS), GROUP, 0, 0, tiled=True)
+    me = lax.axis_index("wide").astype(jnp.int32)
+    group = me // SLICES
+    flip = flip_of(group)
+    holder = [[SLICES * k + (i ^ flip_of(k)) for i in range(SLICES)] for k in range(groups)]
+
+    def one(*shape):
+        return jax.ShapeDtypeStruct(shape, jnp.float32)
+
+    cells = lax.all_to_all(
+        distance.reshape(BLOCKS, COLS, ROWS), "wide", 0, 0, tiled=True, axis_index_groups=holder
+    )
     first, last, base = pl.pallas_call(
         edges_kernel,
-        out_shape=[
-            jax.ShapeDtypeStruct((2 * BLOCKS, ROWS), f32),
-            jax.ShapeDtypeStruct((2 * BLOCKS, ROWS), f32),
-            jax.ShapeDtypeStruct((BLOCKS, 16, ROWS), f32),
-        ],
+        out_shape=[one(BLOCKS, 2, ROWS), one(BLOCKS, 2, ROWS), one(BLOCKS, 16, ROWS)],
         in_specs=[VMEM] * 3,
         out_specs=[VMEM] * 3,
         name="edges",
     )(distance, material, occupancy)
     up = lax.ppermute(last, "narrow", [(i, i + 1) for i in range(narrow - 1)])
     down = lax.ppermute(first, "narrow", [(i + 1, i) for i in range(narrow - 1)])
-    small = jnp.concatenate(
-        [base[:, :2], up.reshape(BLOCKS, 2, ROWS), down.reshape(BLOCKS, 2, ROWS), base[:, 6:]], axis=1
-    )
-    small = lax.all_to_all(small, GROUP, 0, 0, tiled=True)
-    before = lax.ppermute(cells[-1], WIDE, [(i, i + SLICES) for i in range(wide - SLICES)])
-    after = lax.ppermute(cells[0], WIDE, [(i + SLICES, i) for i in range(wide - SLICES)])
+    small = pl.pallas_call(
+        pack_kernel,
+        out_shape=one(BLOCKS, 16, ROWS),
+        in_specs=[VMEM] * 3,
+        out_specs=VMEM,
+        name="pack",
+    )(base, up, down)
+    before, after = outer_blocks(distance, groups)
+    cells, small, before, after = lax.optimization_barrier((cells, small, before, after))
+    small = lax.all_to_all(small, "wide", 0, 0, tiled=True, axis_index_groups=holder)
     step = 4.0 / (slices * wide)
-
-    def block(*refs):
-        block_kernel(*refs, step)
-
     pieces = pl.pallas_call(
-        block,
-        out_shape=jax.ShapeDtypeStruct((PIECES, FIELDS, PIECE, ROWS), f32),
-        in_specs=[VMEM] * 4 + [SMEM] * 2 + [VMEM] * 2,
+        functools.partial(block_kernel, step),
+        out_shape=one(NEAR, FIELDS, PART, ROWS),
+        in_specs=[SMEM] + [VMEM] * 4 + [SMEM] * 2 + [VMEM] * 2,
         out_specs=VMEM,
         scratch_shapes=[
-            pltpu.VMEM((2 * SLICES + 2, COLS, ROWS), f32),
-            pltpu.VMEM((FIELDS, SLICES, COLS // 8, ROWS), f32),
+            pltpu.VMEM((2 * SLICES + 2, COLS, ROWS), jnp.float32),
+            pltpu.VMEM((FIELDS, SLICES, COLS // 8, ROWS), jnp.float32),
         ],
         compiler_params=pltpu.CompilerParams(vmem_limit_bytes=40 * 1024 * 1024),
         name="block",
-    )(cells, small, before, after, colours, absorb, kernel_x, kernel_y)
-    parts = lax.all_to_all(pieces, GROUPS, 0, 0, tiled=True)
-    image = pl.pallas_call(
-        merge_kernel,
-        out_shape=jax.ShapeDtypeStruct((FIELDS, PIECE, ROWS), f32),
-        in_specs=[VMEM],
+    )(flip.reshape(1), cells, small, before, after, colours, absorb, kernel_x, kernel_y)
+    near = [[holder[k][i] for k in range(half, half + NEAR)] for i in range(SLICES) for half in range(0, groups, NEAR)]
+    parts = lax.all_to_all(pieces, "wide", 0, 0, tiled=True, axis_index_groups=near)
+    same, other = pl.pallas_call(
+        merge_near_kernel,
+        out_shape=[one(FIELDS, PIECE, ROWS)] * 2,
+        in_specs=[SMEM, VMEM],
+        out_specs=[VMEM] * 2,
+        name="merge_near",
+    )((group // NEAR).reshape(1), parts)
+    came = []
+    for apart, part in enumerate((same, other)):
+        pairs = [
+            (holder[k][i], groups * i + 2 * (k % NEAR) + (k // NEAR ^ apart))
+            for k in range(groups)
+            for i in range(SLICES)
+        ]
+        came.append(lax.ppermute(part, "wide", pairs))
+    return pl.pallas_call(
+        merge_far_kernel,
+        out_shape=one(FIELDS, PIECE, ROWS),
+        in_specs=[SMEM] + [VMEM] * 2,
         out_specs=VMEM,
-        name="merge",
-    )(parts)
-    return lax.ppermute(
-        image, WIDE, [(j * SLICES + i, i * groups + j) for j in range(groups) for i in range(SLICES)]
-    )
+        name="merge_far",
+    )((me & 1).reshape(1), *came)
 
 
 def solution(mesh):
-    wide, narrow = mesh.devices.shape
-    split = Mesh(
-        mesh.devices.reshape(4, wide // 32, 4, 2, narrow), ("x", "zg", "zp", "core", "narrow")
-    )
-    held = P(WIDE, None, "narrow")
+    held = P("wide", None, "narrow")
     return jax.shard_map(
         local,
-        mesh=split,
+        mesh=mesh,
         in_specs=(held, held, held, P(), P(), P(), P()),
-        out_specs=P(None, WIDE, "narrow"),
+        out_specs=P(None, "wide", "narrow"),
         check_vma=False,
     )

time: 126 us -> 124 us (0.984)
  the two profiles are of different devices: /device:TPU:44 before, /device:TPU:80 now
where the time goes in v2:
time: 124 us; the launch traced here: 123 us
  waiting for transfers between devices  52.5 us (42%)
  starting transfers between devices  52.3 us (42%)
  Pallas kernels  13.9 us (11%)
  local copies, waits for them, and re-layouts  3.65 us (3%)
    all_to_all x1, waiting for transfers between devices, local(): lax.all_to_all(pieces, 'wide', 0, 0, tiled=True, axis_index_groups=near)  25.2 us
    ppermute x2, starting transfers between devices, local(): came.append(lax.ppermute(part, 'wide', pairs))  13.8 us
    ppermute x2, waiting for transfers between devices, local(): came.append(lax.ppermute(part, 'wide', pairs))  12.1 us
    all_to_all x1, starting transfers between devices, local(): lax.all_to_all(small, 'wide', 0, 0, tiled=True, axis_index_groups=holder)  12 us
    all_to_all x1, starting transfers between devices, local(): lax.all_to_all(pieces, 'wide', 0, 0, tiled=True, axis_index_groups=near)  10.5 us
    all_to_all x1, waiting for transfers between devices, local(): lax.all_to_all(distance.reshape(BLOCKS, COLS, ROWS), 'wide', 0, 0, tiled=...  6.54 us
    pallas_call x1, Pallas kernels, local(): pl.pallas_call(functools.partial(block_kernel, step), out_shape=one(NEAR,...  6.43 us
    all_to_all x1, starting transfers between devices, local(): lax.all_to_all(distance.reshape(BLOCKS, COLS, ROWS), 'wide', 0, 0, tiled=...  5.68 us
  transfers between devices with their start and end apart: 12, of which 6 were waited for; matrix products, arithmetic and copies ran while one was open for 1% of the time, Pallas kernels for 4%

profile of v2, /device:TPU:80, one launch (start us, length us, event | category | flops | bytes accessed | tf_op | source)
XLA Modules:
  0.0 122.7 jit_solution(1819933986339304960)
XLA Ops:
  0.0 5.7 %all-to-all-start = ((f32[8,256,128]{2,1,0:T(8,128)}), f32[8,256,128]{2,1,0:T(8,128)S(1)}, u32[]{:S(2)}, u32[]{:S(2)}) async-start(f32[8,256,128]{2,1,0:T(8,128)} %bitcast.17), calls=%async_computation | async-start | bytes 2097152 | tf_op jit(solution)/shard_map/all_to_all | solution.py:275
  5.7 0.0 copy-done.4
  5.7 0.7 collective-permute-start.2
  6.5 0.0 collective-permute-done.2
  6.6 0.1 bitcast_select_fusion
  6.6 0.0 copy-start.8
  6.7 0.7 collective-permute-start.3
  7.4 0.7 collective-permute-start.4
  8.0 1.3 %collective-permute-start.5 = (f32[256,128]{1,0:T(8,128)S(1)}, f32[256,128]{1,0:T(8,128)S(1)}, u32[]{:S(2)}, u32[]{:S(2)}) collective-permute-start(f32[256,128]{1,0:T(8,128)S(1)} %get-tuple-element.26), channel_id=1, source_target_pairs={{24,40},{32,16},{28,44},{36,20},{56,72},{64,48},{60,76},{68,52},{8... | collective-permute-start | bytes 393224 | tf_op jit(solution)/shard_map/ppermute | solution.py:256
  9.3 0.0 copy-start.9
  9.3 0.7 collective-permute-start.6
  10.0 0.0 copy-done.8
  10.0 0.8 copy.8.material
  10.8 0.0 copy-done.9
  10.8 0.7 copy.9.occupancy
  11.5 2.9 %edges.1 = (f32[8,2,128]{2,1,0:T(2,128)}, f32[8,2,128]{2,1,0:T(2,128)}, f32[8,16,128]{2,1,0:T(8,128)}) custom-call(f32[1,2048,128]{2,1,0:T(8,128)} %cells.1, s32[1,256,16]{2,1,0:T(8,128)} %copy.8.material, s32[1,256,16]{2,1,0:T(8,128)} %copy.9.occupancy), custom_call_target="tpu_custom_call" | custom-call | tf_op jit(solution)/shard_map/edges/pallas_call | solution.py:278
  14.4 3.2 %collective-permute-start = (f32[8,2,128]{2,1,0:T(2,128)}, f32[8,2,128]{2,1,0:T(2,128)S(1)}, u32[]{:S(2)}, u32[]{:S(2)}) collective-permute-start(f32[8,2,128]{2,1,0:T(2,128)} %get-tuple-element.15), channel_id=1, source_target_pairs={{0,1},{1,2},{2,3},{4,5},{5,6},{6,7},{8,9},{9,10},{10,11},{12,13},{... | collective-permute-start | bytes 24584 | tf_op jit(solution)/shard_map/ppermute | solution.py:285
  17.6 2.6 %collective-permute-done.up = f32[8,2,128]{2,1,0:T(2,128)S(1)} collective-permute-done((f32[8,2,128]{2,1,0:T(2,128)}, f32[8,2,128]{2,1,0:T(2,128)S(1)}, u32[]{:S(2)}, u32[]{:S(2)}) %collective-permute-start) | collective-permute-done | bytes 8224 | tf_op jit(solution)/shard_map/ppermute | solution.py:285
  20.2 3.1 %collective-permute-start.1 = (f32[8,2,128]{2,1,0:T(2,128)}, f32[8,2,128]{2,1,0:T(2,128)S(1)}, u32[]{:S(2)}, u32[]{:S(2)}) collective-permute-start(f32[8,2,128]{2,1,0:T(2,128)} %get-tuple-element.16), channel_id=1, source_target_pairs={{1,0},{2,1},{3,2},{5,4},{6,5},{7,6},{9,8},{10,9},{11,10},{13,12},{... | collective-permute-start | bytes 24584 | tf_op jit(solution)/shard_map/ppermute | solution.py:286
  23.3 2.6 %collective-permute-done.1.down = f32[8,2,128]{2,1,0:T(2,128)S(1)} collective-permute-done((f32[8,2,128]{2,1,0:T(2,128)}, f32[8,2,128]{2,1,0:T(2,128)S(1)}, u32[]{:S(2)}, u32[]{:S(2)}) %collective-permute-start.1) | collective-permute-done | bytes 8224 | tf_op jit(solution)/shard_map/ppermute | solution.py:286
  25.9 0.0 copy-done.10
  25.9 0.6 copy-done.11
  26.5 1.5 %pack.1 = f32[8,16,128]{2,1,0:T(8,128)} custom-call(f32[8,16,128]{2,1,0:T(8,128)} %get-tuple-element.14.base, f32[8,2,128]{2,1,0:T(2,128)} %copy-done.10, f32[8,2,128]{2,1,0:T(2,128)} %copy-done.11), custom_call_target="tpu_custom_call" | custom-call | tf_op jit(solution)/shard_map/pack/pallas_call | solution.py:287
  28.0 0.0 collective-permute-done.3
  28.0 0.0 collective-permute-done.4
  28.0 0.0 collective-permute-done.5
  28.0 0.0 collective-permute-done.6
  28.0 0.0 copy-start
  28.1 6.5 %all-to-all-done.cells = f32[8,256,128]{2,1,0:T(8,128)S(1)} async-done(((f32[8,256,128]{2,1,0:T(8,128)}), f32[8,256,128]{2,1,0:T(8,128)S(1)}, u32[]{:S(2)}, u32[]{:S(2)}) %all-to-all-start) | async-done | bytes 1048608 | tf_op jit(solution)/shard_map/all_to_all | solution.py:275
  34.6 12.0 %all-to-all-start.1 = ((f32[8,16,128]{2,1,0:T(8,128)}), f32[8,16,128]{2,1,0:T(8,128)S(1)}, u32[]{:S(2)}, u32[]{:S(2)}) async-start(f32[8,16,128]{2,1,0:T(8,128)} %pack.1), calls=%async_computation.1 | async-start | bytes 131072 | tf_op jit(solution)/shard_map/all_to_all | solution.py:296
  46.7 3.5 %all-to-all-done.1.small = f32[8,16,128]{2,1,0:T(8,128)S(1)} async-done(((f32[8,16,128]{2,1,0:T(8,128)}), f32[8,16,128]{2,1,0:T(8,128)S(1)}, u32[]{:S(2)}, u32[]{:S(2)}) %all-to-all-start.1) | async-done | bytes 65568 | tf_op jit(solution)/shard_map/all_to_all | solution.py:296
  50.1 0.0 copy-done
  50.1 0.0 copy-done.1
  50.1 0.0 copy-done.2
  50.1 0.0 copy-done.3
  50.1 6.4 %block.1 = f32[8,4,32,128]{3,2,1,0:T(8,128)} custom-call(s32[1]{0:T(128)} %bitcast.2.flip, f32[8,256,128]{2,1,0:T(8,128)S(1)} %all-to-all-done.cells, f32[8,16,128]{2,1,0:T(8,128)S(1)} %all-to-all-done.1.small, f32[256,128]{1,0:T(8,128)S(1)} %get-tuple-element.19.before, f32[256,128]{1,0:T(8,128)S(1)} %get-tuple-element.20.after, f32[3,16]{1,0:T(4,128)S(1)} %copy-done.2, ...), custom_call_target="tpu_custom_call" | custom-call | tf_op jit(solution)/shard_map/block/pallas_call | solution.py:298
  56.6 10.5 %all-to-all-start.2 = ((f32[8,4,32,128]{3,2,1,0:T(8,128)}), f32[8,4,32,128]{3,2,1,0:T(8,128)S(1)}, u32[]{:S(2)}, u32[]{:S(2)}) async-start(f32[8,4,32,128]{3,2,1,0:T(8,128)} %block.1), calls=%async_computation.2 | async-start | bytes 1048576 | tf_op jit(solution)/shard_map/all_to_all | solution.py:311
  67.0 25.2 %all-to-all-done.2.parts = f32[8,4,32,128]{3,2,1,0:T(8,128)S(1)} async-done(((f32[8,4,32,128]{3,2,1,0:T(8,128)}), f32[8,4,32,128]{3,2,1,0:T(8,128)S(1)}, u32[]{:S(2)}, u32[]{:S(2)}) %all-to-all-start.2) | async-done | bytes 524320 | tf_op jit(solution)/shard_map/all_to_all | solution.py:311
  92.2 0.8 copy-done.5
  93.1 1.7 %merge_near.1 = (f32[4,16,128]{2,1,0:T(8,128)}, f32[4,16,128]{2,1,0:T(8,128)}) custom-call(s32[1]{0:T(128)} %bitcast.1.half, f32[8,4,32,128]{3,2,1,0:T(8,128)} %copy-done.5), custom_call_target="tpu_custom_call" | custom-call | tf_op jit(solution)/shard_map/merge_near/pallas_call | solution.py:312
  94.8 9.7 %collective-permute-start.7 = (f32[4,16,128]{2,1,0:T(8,128)}, f32[4,16,128]{2,1,0:T(8,128)S(1)}, u32[]{:S(2)}, u32[]{:S(2)}) collective-permute-start(f32[4,16,128]{2,1,0:T(8,128)} %get-tuple-element.21), channel_id=1, source_target_pairs={{0,0},{4,64},{8,128},{12,192},{16,256},{20,320},{24,384},{28,448},... | collective-permute-start | bytes 98312 | tf_op jit(solution)/shard_map/ppermute | solution.py:326
  104.5 4.1 %collective-permute-start.8 = (f32[4,16,128]{2,1,0:T(8,128)}, f32[4,16,128]{2,1,0:T(8,128)S(1)}, u32[]{:S(2)}, u32[]{:S(2)}) collective-permute-start(f32[4,16,128]{2,1,0:T(8,128)} %get-tuple-element.22), channel_id=1, source_target_pairs={{0,4},{4,68},{8,132},{12,196},{16,260},{20,324},{24,388},{28,452},... | collective-permute-start | bytes 98312 | tf_op jit(solution)/shard_map/ppermute | solution.py:326
  108.6 0.0 collective-permute-done.7.same
  108.6 0.0 copy-start.6
  108.6 12.1 %collective-permute-done.8.other = f32[4,16,128]{2,1,0:T(8,128)S(1)} collective-permute-done((f32[4,16,128]{2,1,0:T(8,128)}, f32[4,16,128]{2,1,0:T(8,128)S(1)}, u32[]{:S(2)}, u32[]{:S(2)}) %collective-permute-start.8) | collective-permute-done | bytes 32800 | tf_op jit(solution)/shard_map/ppermute | solution.py:326
  120.7 0.0 copy-done.6
  120.7 0.6 copy-done.7
  121.3 1.4 %merge_far.1 = f32[4,16,128]{2,1,0:T(8,128)} custom-call(s32[1]{0:T(128)} %bitcast.chunk, f32[4,16,128]{2,1,0:T(8,128)} %copy-done.6, f32[4,16,128]{2,1,0:T(8,128)} %copy-done.7), custom_call_target="tpu_custom_call" | custom-call | tf_op jit(solution)/shard_map/merge_far/pallas_call | solution.py:327
  (11 shorter events, 0.1 us)
Async XLA Ops:
  0.0 5.7 %copy-start.4 = (f32[1,2048,128]{2,1,0:T(8,128)S(1)}, f32[1,2048,128]{2,1,0:T(8,128)}, u32[]{:S(2)}) copy-start(f32[1,2048,128]{2,1,0:T(8,128)} %cells.1) | copy-start | bytes 3145732
  0.0 34.6 %all-to-all-start = ((f32[8,256,128]{2,1,0:T(8,128)}), f32[8,256,128]{2,1,0:T(8,128)S(1)}, u32[]{:S(2)}, u32[]{:S(2)}) async-start(f32[8,256,128]{2,1,0:T(8,128)} %bitcast.17), calls=%async_computation | async-start | bytes 2097152 | tf_op jit(solution)/shard_map/all_to_all | solution.py:275
  5.7 0.8 collective-permute-start.2
  6.6 3.4 %copy-start.8 = (s32[1,256,16]{1,2,0:T(8,128)S(1)}, s32[1,256,16]{1,2,0:T(8,128)}, u32[]{:S(2)}) copy-start(s32[1,256,16]{1,2,0:T(8,128)} %param.9) | copy-start | bytes 49156
  6.7 21.3 %collective-permute-start.3 = (f32[256,128]{1,0:T(8,128)S(1)}, f32[256,128]{1,0:T(8,128)S(1)}, u32[]{:S(2)}, u32[]{:S(2)}) collective-permute-start(f32[256,128]{1,0:T(8,128)S(1)} %get-tuple-element.28), channel_id=1, source_target_pairs={{24,56},{32,0},{28,60},{36,4},{56,88},{64,32},{60,92},{68,36},{88,... | collective-permute-start | bytes 393224 | tf_op jit(solution)/shard_map/ppermute | solution.py:256
  7.4 20.7 %collective-permute-start.4 = (f32[256,128]{1,0:T(8,128)S(1)}, f32[256,128]{1,0:T(8,128)S(1)}, u32[]{:S(2)}, u32[]{:S(2)}) collective-permute-start(f32[256,128]{1,0:T(8,128)S(1)} %get-tuple-element.27), channel_id=1, source_target_pairs={{24,48},{32,8},{28,52},{36,12},{56,80},{64,40},{60,84},{68,44},{88... | collective-permute-start | bytes 393224 | tf_op jit(solution)/shard_map/ppermute | solution.py:256
  8.0 20.0 %collective-permute-start.5 = (f32[256,128]{1,0:T(8,128)S(1)}, f32[256,128]{1,0:T(8,128)S(1)}, u32[]{:S(2)}, u32[]{:S(2)}) collective-permute-start(f32[256,128]{1,0:T(8,128)S(1)} %get-tuple-element.26), channel_id=1, source_target_pairs={{24,40},{32,16},{28,44},{36,20},{56,72},{64,48},{60,76},{68,52},{8... | collective-permute-start | bytes 393224 | tf_op jit(solution)/shard_map/ppermute | solution.py:256
  9.3 1.5 %copy-start.9 = (s32[1,256,16]{1,2,0:T(8,128)S(1)}, s32[1,256,16]{1,2,0:T(8,128)}, u32[]{:S(2)}) copy-start(s32[1,256,16]{1,2,0:T(8,128)} %param.8) | copy-start | bytes 49156
  9.3 18.7 %collective-permute-start.6 = (f32[256,128]{1,0:T(8,128)S(1)}, f32[256,128]{1,0:T(8,128)S(1)}, u32[]{:S(2)}, u32[]{:S(2)}) collective-permute-start(f32[256,128]{1,0:T(8,128)S(1)} %get-tuple-element.25), channel_id=1, source_target_pairs={{24,32},{32,24},{28,36},{36,28},{56,64},{64,56},{60,68},{68,60},{8... | collective-permute-start | bytes 393224 | tf_op jit(solution)/shard_map/ppermute | solution.py:256
  14.4 5.7 %collective-permute-start = (f32[8,2,128]{2,1,0:T(2,128)}, f32[8,2,128]{2,1,0:T(2,128)S(1)}, u32[]{:S(2)}, u32[]{:S(2)}) collective-permute-start(f32[8,2,128]{2,1,0:T(2,128)} %get-tuple-element.15), channel_id=1, source_target_pairs={{0,1},{1,2},{2,3},{4,5},{5,6},{6,7},{8,9},{9,10},{10,11},{12,13},{... | collective-permute-start | bytes 24584 | tf_op jit(solution)/shard_map/ppermute | solution.py:285
  20.2 5.8 %copy-start.10 = (f32[8,2,128]{2,1,0:T(2,128)}, f32[8,2,128]{2,1,0:T(2,128)S(1)}, u32[]{:S(2)}) copy-start(f32[8,2,128]{2,1,0:T(2,128)S(1)} %collective-permute-done.up) | copy-start | bytes 24580
  20.2 5.7 %collective-permute-start.1 = (f32[8,2,128]{2,1,0:T(2,128)}, f32[8,2,128]{2,1,0:T(2,128)S(1)}, u32[]{:S(2)}, u32[]{:S(2)}) collective-permute-start(f32[8,2,128]{2,1,0:T(2,128)} %get-tuple-element.16), channel_id=1, source_target_pairs={{1,0},{2,1},{3,2},{5,4},{6,5},{7,6},{9,8},{10,9},{11,10},{13,12},{... | collective-permute-start | bytes 24584 | tf_op jit(solution)/shard_map/ppermute | solution.py:286
  25.9 0.6 copy-start.11
  28.0 22.1 %copy-start = (f32[256,256]{1,0:T(8,128)S(1)}, f32[256,256]{1,0:T(8,128)}, u32[]{:S(2)}) copy-start(f32[256,256]{1,0:T(8,128)} %kernel_x.1) | copy-start | bytes 786436
  34.6 15.5 %copy-start.1 = (f32[128,128]{1,0:T(8,128)S(1)}, f32[128,128]{1,0:T(8,128)}, u32[]{:S(2)}) copy-start(f32[128,128]{1,0:T(8,128)} %kernel_y.1) | copy-start | bytes 196612
  34.6 15.5 %all-to-all-start.1 = ((f32[8,16,128]{2,1,0:T(8,128)}), f32[8,16,128]{2,1,0:T(8,128)S(1)}, u32[]{:S(2)}, u32[]{:S(2)}) async-start(f32[8,16,128]{2,1,0:T(8,128)} %pack.1), calls=%async_computation.1 | async-start | bytes 131072 | tf_op jit(solution)/shard_map/all_to_all | solution.py:296
  46.6 3.5 %copy-start.2 = (f32[3,16]{1,0:T(4,128)S(1)}, f32[3,16]{1,0:T(4,128)}, u32[]{:S(2)}) copy-start(f32[3,16]{1,0:T(4,128)} %colours.1) | copy-start | bytes 580
  46.6 3.5 %copy-start.3 = (f32[16]{0:T(128)S(1)}, f32[16]{0:T(128)}, u32[]{:S(2)}) copy-start(f32[16]{0:T(128)} %absorb.1) | copy-start | bytes 196
  56.6 35.7 %all-to-all-start.2 = ((f32[8,4,32,128]{3,2,1,0:T(8,128)}), f32[8,4,32,128]{3,2,1,0:T(8,128)S(1)}, u32[]{:S(2)}, u32[]{:S(2)}) async-start(f32[8,4,32,128]{3,2,1,0:T(8,128)} %block.1), calls=%async_computation.2 | async-start | bytes 1048576 | tf_op jit(solution)/shard_map/all_to_all | solution.py:311
  92.2 0.8 copy-start.5
  94.8 13.8 %collective-permute-start.7 = (f32[4,16,128]{2,1,0:T(8,128)}, f32[4,16,128]{2,1,0:T(8,128)S(1)}, u32[]{:S(2)}, u32[]{:S(2)}) collective-permute-start(f32[4,16,128]{2,1,0:T(8,128)} %get-tuple-element.21), channel_id=1, source_target_pairs={{0,0},{4,64},{8,128},{12,192},{16,256},{20,320},{24,384},{28,448},... | collective-permute-start | bytes 98312 | tf_op jit(solution)/shard_map/ppermute | solution.py:326
  104.5 16.2 %collective-permute-start.8 = (f32[4,16,128]{2,1,0:T(8,128)}, f32[4,16,128]{2,1,0:T(8,128)S(1)}, u32[]{:S(2)}, u32[]{:S(2)}) collective-permute-start(f32[4,16,128]{2,1,0:T(8,128)} %get-tuple-element.22), channel_id=1, source_target_pairs={{0,4},{4,68},{8,132},{12,196},{16,260},{20,324},{24,388},{28,452},... | collective-permute-start | bytes 98312 | tf_op jit(solution)/shard_map/ppermute | solution.py:326
  108.6 12.1 %copy-start.6 = (f32[4,16,128]{2,1,0:T(8,128)}, f32[4,16,128]{2,1,0:T(8,128)S(1)}, u32[]{:S(2)}) copy-start(f32[4,16,128]{2,1,0:T(8,128)S(1)} %collective-permute-done.7.same) | copy-start | bytes 98308
  120.7 0.6 copy-start.7

commit v3 on v2

v3 whole, which is shorter than its diff:
```python
import functools

import jax
import jax.numpy as jnp
from jax import lax
from jax.experimental import pallas as pl
from jax.experimental.pallas import tpu as pltpu
from jax.sharding import PartitionSpec as P

BLOCKS = 8
SLICES = 8
COLS = 256
ROWS = 128
PIECE = 16
CHIPS = 8
MESSAGE = COLS + 16
FIELDS = 4
VMEM = pl.BlockSpec(memory_space=pltpu.VMEM)
SMEM = pl.BlockSpec(memory_space=pltpu.SMEM)
ANY = pl.BlockSpec(memory_space=pl.ANY)


def halves(value):
    high = value.astype(jnp.bfloat16)
    low = (value - high.astype(jnp.float32)).astype(jnp.bfloat16)
    return high, low


def product(a, b, dims=((1,), (0,))):
    a_high, a_low = a
    b_high, b_low = b

    def one(p, q):
        return lax.dot_general(p, q, (dims, ((), ())), preferred_element_type=jnp.float32)

    return one(a_high, b_high) + (one(a_low, b_high) + one(a_high, b_low))


def ones_where(condition):
    return jnp.where(condition, 1.0, 0.0)


def iota(shape, dim):
    return lax.broadcasted_iota(jnp.int32, shape, dim)


def thirds(value):
    high = value.astype(jnp.bfloat16)
    rest = value - high.astype(jnp.float32)
    middle = rest.astype(jnp.bfloat16)
    return high, middle, (rest - middle.astype(jnp.float32)).astype(jnp.bfloat16)


def message_kernel(cells, material, occupancy, message, first, last, sides, held, bricks, sems):
    load = pltpu.make_async_copy(cells.at[0], held, sems.at[0])
    load.start()
    copies = []
    brick_rows = material.shape[1]
    lane = iota((brick_rows, ROWS), 1)
    row = iota((brick_rows, ROWS), 0)
    kinds = material[0].astype(jnp.float32).T.reshape(BLOCKS, 4, 8, brick_rows)
    masks = occupancy[0].astype(jnp.float32).T.reshape(BLOCKS, 4, 8, brick_rows)
    packed = jnp.zeros((BLOCKS * 8, ROWS), jnp.float32)
    for part in range(4):
        at = 2 * brick_rows * part
        packed += jnp.dot(
            kinds[:, part].reshape(BLOCKS * 8, brick_rows),
            ones_where(lane == row + at),
            preferred_element_type=jnp.float32,
        )
        packed += jnp.dot(
            masks[:, part].reshape(BLOCKS * 8, brick_rows),
            ones_where(lane == row + (at + brick_rows)),
            preferred_element_type=jnp.float32,
        )
    bricks[...] = packed.reshape(BLOCKS, 8, ROWS)
    copies.append(pltpu.make_async_copy(bricks, message.at[:, COLS + 8 : MESSAGE], sems.at[1 + BLOCKS]))
    copies[-1].start()
    load.wait()
    for block in range(BLOCKS):
        copies.append(
            pltpu.make_async_copy(
                held.at[block * COLS : (block + 1) * COLS], message.at[block, :COLS], sems.at[1 + block]
            )
        )
        copies[-1].start()
    ends = ones_where(
        (iota((8, ROWS), 0) == 0) & (iota((8, ROWS), 1) == 0)
        | (iota((8, ROWS), 0) == 1) & (iota((8, ROWS), 1) == ROWS - 1)
    ).astype(jnp.bfloat16)
    for block in range(BLOCKS):
        left, right = block * COLS, (block + 1) * COLS
        taken = sum(
            lax.dot_general(ends, term, (((1,), (1,)), ((), ())), preferred_element_type=jnp.float32)
            for term in reversed(thirds(held[left:right]))
        )
        for part in range(2):
            at = part * ROWS
            first[block, part : part + 1] = taken[0:1, at : at + ROWS]
            last[block, part : part + 1] = taken[1:2, at : at + ROWS]
        none = jnp.zeros((1, ROWS), jnp.float32)
        sides[block, 0:1] = held[left - 1 : left] if block else none
        sides[block, 1:2] = held[right : right + 1] if block < BLOCKS - 1 else none
    for copy in copies:
        copy.wait()


def beside_kernel(_, sides, up, down, message, rows, sem):
    rows[:, 0:2] = sides[...]
    rows[:, 2:4] = up[...]
    rows[:, 4:6] = down[...]
    rows[:, 6:8] = jnp.zeros((BLOCKS, 2, ROWS), jnp.float32)
    copy = pltpu.make_async_copy(rows, message.at[:, COLS : COLS + 8], sem)
    copy.start()
    copy.wait()


def block_kernel(
    step, core, cells, before, after, colours, absorb, kernel_x, kernel_y, kept, given, fields, bricks
):
    eye_y = ones_where(iota((ROWS, ROWS), 0) == iota((ROWS, ROWS), 1))
    along_y = 0.5 * eye_y + kernel_y[...]
    none = jnp.zeros((1, ROWS), jnp.float32)
    slope_y = 0.5 * (
        jnp.concatenate([none, along_y[:-1]], axis=0) - jnp.concatenate([along_y[1:], none], axis=0)
    )
    both_y = halves(jnp.concatenate([along_y, slope_y], axis=1))
    only_y = halves(along_y)
    eye_x = ones_where(iota((COLS, COLS), 0) == iota((COLS, COLS), 1))
    along_x = halves((0.5 * eye_x + kernel_x[...]).T)
    beside = jnp.concatenate(
        [
            jnp.concatenate([cells[s, at : at + 1], cells[s, at + 1 : at + 2]], axis=1)
            for s in range(SLICES)
            for at in (COLS + 2, COLS + 4)
        ],
        axis=0,
    )
    beside = halves(beside.T)
    corner = jnp.concatenate([-0.5 * along_y[0:1], 0.5 * along_y[-1:]], axis=0)
    column_ends = jnp.concatenate([cells[s, COLS : COLS + 2] for s in range(SLICES)], axis=0)
    column_ends = product(halves(column_ends), only_y)
    outer = product(
        halves(jnp.concatenate([before[...], after[...]], axis=0)), only_y
    )
    outer = jnp.concatenate([outer[:COLS], outer[COLS:]], axis=1)
    outer = product(along_x, halves(outer))
    fields[0] = outer[:, :ROWS]
    fields[SLICES + 1] = outer[:, ROWS:]
    for pair in range(SLICES // 2):
        parts = []
        for s in (2 * pair, 2 * pair + 1):
            rows = product(halves(cells[s, :COLS]), both_y)
            value = rows[:, :ROWS]
            row = iota((2 * SLICES, ROWS), 0)
            wanted = jnp.where(row == 2 * s, corner[0:1], 0.0) + jnp.where(row == 2 * s + 1, corner[1:2], 0.0)
            slope = rows[:, ROWS:] + product(beside, halves(wanted))
            ahead = jnp.concatenate([value[1:], column_ends[2 * s + 1 : 2 * s + 2]], axis=0)
            behind = jnp.concatenate([column_ends[2 * s : 2 * s + 1], value[:-1]], axis=0)
            parts += [value, 0.5 * (ahead - behind), slope]
        mixed = product(along_x, halves(jnp.concatenate(parts, axis=1)))
        for i, s in enumerate((2 * pair, 2 * pair + 1)):
            at = 3 * i * ROWS
            fields[1 + s] = mixed[:, at : at + ROWS]
            u = mixed[:, at + ROWS : at + 2 * ROWS]
            v = mixed[:, at + 2 * ROWS : at + 3 * ROWS]
            fields[SLICES + 2 + s] = u * u + v * v
    codes = cells[:, COLS + 8 : MESSAGE, :].reshape(SLICES * 8, ROWS)
    brick_rows = ROWS // 8
    masks = pltpu.roll(codes, ROWS - brick_rows, 1)
    values = [jnp.zeros_like(codes)] * FIELDS
    for label in range(colours.shape[1]):
        found = codes == float(label)
        for f in range(FIELDS):
            entry = colours[f, label] if f < 3 else absorb[label]
            values[f] = jnp.where(found, entry, values[f])
    values[3] = values[3] * masks * step
    values = jnp.concatenate(values, axis=0)
    source = iota((ROWS, 4 * ROWS), 0)
    target = iota((ROWS, 4 * ROWS), 1)
    spread = ones_where(source == (target // ROWS) * (2 * brick_rows) + (target % ROWS) // 8)
    spread = spread.astype(jnp.bfloat16)
    high, low = halves(values)
    least = (values - high.astype(jnp.float32) - low.astype(jnp.float32)).astype(jnp.bfloat16)
    grown = (
        jnp.dot(least, spread, preferred_element_type=jnp.float32)
        + jnp.dot(low, spread, preferred_element_type=jnp.float32)
        + jnp.dot(high, spread, preferred_element_type=jnp.float32)
    )
    for f in range(FIELDS):
        for s in range(SLICES):
            for part in range(4):
                bricks[f, s, 8 * part : 8 * part + 8] = grown[
                    (f * SLICES + s) * 8 : (f * SLICES + s) * 8 + 8, part * ROWS : (part + 1) * ROWS
                ]

    def shade(image, piece, chunk, part):
        row = chunk * (PIECE // 8) + part
        at = pl.ds(pl.multiple_of(row * 8, 8), 8)
        brick = pl.ds(row, 1)
        transmit = jnp.ones((8, ROWS), jnp.float32)
        total = [jnp.zeros((8, ROWS), jnp.float32)] * FIELDS
        for s in range(SLICES):
            d = fields[1 + s, at]
            w = 0.5 * (fields[2 + s, at] - fields[s, at])
            norm = jnp.maximum(fields[SLICES + 2 + s, at] + w * w, 0.1)
            facing = 0.25 + 0.75 * jnp.abs(w) * lax.rsqrt(norm)
            density = jnp.exp(-2.0 * d * d)
            opacity = 1.0 - jnp.exp(-bricks[3, s, brick] * density)
            weight = transmit * opacity
            shaded = weight * facing
            for f in range(3):
                total[f] = total[f] + shaded * bricks[f, s, brick]
            total[3] = total[3] + weight
            transmit = transmit * (1.0 - opacity)
        for f in range(FIELDS):
            image[piece, f, 8 * part : 8 * part + 8] = total[f]

    def shade_chip(chip, _):
        for part in range(PIECE // 8):
            shade(given, chip, 2 * chip + (1 - core[0]), part)
            shade(kept, chip, 2 * chip + core[0], part)
        return 0

    lax.fori_loop(0, CHIPS, shade_chip, 0)


def over(nearer, farther):
    clear = 1.0 - nearer[3]
    return [nearer[f] + clear * farther[f] for f in range(FIELDS)]


def merge_z_kernel(core, parts, image):
    for block in range(4):
        for i in range(PIECE // 8):
            at = slice(8 * i, 8 * i + 8)
            total = None
            for group in range(4):
                chip = (4 * group + block) ^ (CHIPS * core[0])
                part = [parts[chip, f, at] for f in range(FIELDS)]
                total = over(total, part) if total else part
            for f in range(FIELDS):
                image[block, f, at] = total[f]


def merge_x_kernel(parts, image):
    for i in range(PIECE // 8):
        at = slice(8 * i, 8 * i + 8)
        total = [parts[0, f, at] for f in range(FIELDS)]
        for x in range(1, 4):
            total = over(total, [parts[x, f, at] for f in range(FIELDS)])
        for f in range(FIELDS):
            image[f, at] = total[f]


def outer_blocks(distance, groups):
    chips = SLICES // 2
    me = lax.axis_index("wide")
    chip, core = me % SLICES // 2, me % 2
    blocks = distance.reshape(chips, 2, COLS, ROWS)
    ends = [pair for k in range(groups) for pair in ((8 * k, 8 * k + 1), (8 * k + 7, 8 * k + 6))]
    shared = lax.ppermute(lax.dynamic_index_in_dim(blocks, 1 - core, 1, keepdims=False), "wide", ends)
    own = lax.dynamic_index_in_dim(blocks, core, 1, keepdims=False)
    first = chip == 0
    given = jnp.where(jnp.where(first, core == 0, core == 1), own, shared)
    before = after = jnp.zeros((COLS, ROWS), jnp.float32)
    for j in range(chips):
        back = chips - 1 - j
        pairs = []
        for k in range(groups - 1):
            for c in range(2):
                pairs.append((8 * k + 6 + c, 8 * (k + 1) + 2 * j + c))
                pairs.append((8 * (k + 1) + c, 8 * k + 2 * back + c))
        wanted = jnp.where(first, back, j)
        came = lax.ppermute(lax.dynamic_index_in_dim(given, wanted, 0, keepdims=False), "wide", pairs)
        before = jnp.where(chip == j, came, before)
        after = jnp.where(chip == back, came, after)
    return before, after


def local(distance, occupancy, material, colours, absorb, kernel_x, kernel_y):
    slices, col_count, row_count = distance.shape
    wide = lax.axis_size("wide")
    narrow = lax.axis_size("narrow")
    groups = wide // SLICES
    me = lax.axis_index("wide").astype(jnp.int32)
    core = (me & 1).reshape(1)
    members = [[SLICES * k + i for i in range(SLICES)] for k in range(groups)]

    def one(*shape):
        return jax.ShapeDtypeStruct(shape, jnp.float32)

    before, after = outer_blocks(distance, groups)
    message, first, last, sides = pl.pallas_call(
        message_kernel,
        out_shape=[one(BLOCKS, MESSAGE, ROWS)] + [one(BLOCKS, 2, ROWS)] * 3,
        in_specs=[ANY] + [VMEM] * 2,
        out_specs=[ANY] + [VMEM] * 3,
        scratch_shapes=[
            pltpu.VMEM((col_count, row_count), jnp.float32),
            pltpu.VMEM((BLOCKS, 8, ROWS), jnp.float32),
            pltpu.SemaphoreType.DMA((2 + BLOCKS,)),
        ],
        name="message",
    )(distance, jnp.swapaxes(material, 1, 2), jnp.swapaxes(occupancy, 1, 2))
    up = lax.ppermute(last, "narrow", [(i, i + 1) for i in range(narrow - 1)])
    down = lax.ppermute(first, "narrow", [(i + 1, i) for i in range(narrow - 1)])
    message = pl.pallas_call(
        beside_kernel,
        out_shape=one(BLOCKS, MESSAGE, ROWS),
        in_specs=[ANY] + [VMEM] * 3,
        out_specs=ANY,
        scratch_shapes=[pltpu.VMEM((BLOCKS, 8, ROWS), jnp.float32), pltpu.SemaphoreType.DMA],
        input_output_aliases={0: 0},
        name="beside",
    )(message, sides, up, down)
    cells = lax.all_to_all(message, "wide", 0, 0, tiled=True, axis_index_groups=members)
    step = 4.0 / (slices * wide)
    kept, given = pl.pallas_call(
        functools.partial(block_kernel, step),
        out_shape=[one(CHIPS, FIELDS, PIECE, ROWS)] * 2,
        in_specs=[SMEM] + [VMEM] * 3 + [SMEM] * 2 + [VMEM] * 2,
        out_specs=[VMEM] * 2,
        scratch_shapes=[
            pltpu.VMEM((2 * SLICES + 2, COLS, ROWS), jnp.float32),
            pltpu.VMEM((FIELDS, SLICES, COLS // 8, ROWS), jnp.float32),
        ],
        compiler_params=pltpu.CompilerParams(vmem_limit_bytes=40 * 1024 * 1024),
        name="block",
    )(core, cells, before, after, colours, absorb, kernel_x, kernel_y)
    taken = lax.ppermute(given, "wide", [(i, i ^ 1) for i in range(wide)])
    along_z = [
        [32 * x + 2 * ((z + CHIPS * c) % 16) + c for z in range(16)] for x in range(wide // 32) for c in range(2)
    ]
    parts = lax.all_to_all(
        jnp.concatenate([kept, taken], axis=0), "wide", 0, 0, tiled=True, axis_index_groups=along_z
    )
    parts = pl.pallas_call(
        merge_z_kernel,
        out_shape=one(4, FIELDS, PIECE, ROWS),
        in_specs=[SMEM, VMEM],
        out_specs=VMEM,
        name="merge_z",
    )(core, parts)
    along_x = [[32 * x + i for x in range(4)] for i in range(32)]
    parts = lax.all_to_all(parts, "wide", 0, 0, tiled=True, axis_index_groups=along_x)
    return pl.pallas_call(
        merge_x_kernel,
        out_shape=one(FIELDS, PIECE, ROWS),
        in_specs=[VMEM],
        out_specs=VMEM,
        name="merge_x",
    )(parts)


def solution(mesh):
    held = P("wide", None, "narrow")
    return jax.shard_map(
        local,
        mesh=mesh,
        in_specs=(held, held, held, P(), P(), P(), P()),
        out_specs=P(None, "wide", "narrow"),
        check_vma=False,
    )
```

time: 124 us -> 117 us (0.944)
  the two profiles are of different devices: /device:TPU:80 before, /device:TPU:16 now
where the time goes in v3:
time: 117 us; the launch traced here: 116 us
  blocking collectives  49.3 us (42%)
  waiting for transfers between devices  32 us (27%)
  starting transfers between devices  19.7 us (17%)
  Pallas kernels  13.9 us (12%)
    all_to_all x1, blocking collectives, local(): lax.all_to_all(jnp.concatenate([kept, taken], axis=0), 'wide', 0, 0, tile...  39 us
    all_to_all x1, waiting for transfers between devices, local(): lax.all_to_all(message, 'wide', 0, 0, tiled=True, axis_index_groups=members)  15.7 us
    all_to_all x1, blocking collectives, local(): lax.all_to_all(parts, 'wide', 0, 0, tiled=True, axis_index_groups=along_x)  10.4 us
    ppermute x4, waiting for transfers between devices, outer_blocks(): lax.ppermute(lax.dynamic_index_in_dim(given, wanted, 0, keepdims=False),...  10.3 us
    all_to_all x1, starting transfers between devices, local(): lax.all_to_all(message, 'wide', 0, 0, tiled=True, axis_index_groups=members)  6.04 us
    pallas_call x1, Pallas kernels, local(): pl.pallas_call(functools.partial(block_kernel, step), out_shape=[one(CHIP...  5.61 us
    pallas_call x1, Pallas kernels, local(): pl.pallas_call(message_kernel, out_shape=[one(BLOCKS, MESSAGE, ROWS)] + [...  3.67 us
    ppermute x4, starting transfers between devices, outer_blocks(): lax.ppermute(lax.dynamic_index_in_dim(given, wanted, 0, keepdims=False),...  3.43 us
  transfers between devices with their start and end apart: 9, of which 5 were waited for; matrix products, arithmetic and copies ran while one was open for 0% of the time, Pallas kernels for 0%

profile of v3, /device:TPU:16, one launch (start us, length us, event | category | flops | bytes accessed | tf_op | source)
XLA Modules:
  0.0 116.0 jit_solution(18016796010154787536)
XLA Ops:
  0.0 3.7 %message.1 = (f32[8,272,128]{2,1,0:T(8,128)}, f32[8,2,128]{2,1,0:T(2,128)}, f32[8,2,128]{2,1,0:T(2,128)}, f32[8,2,128]{2,1,0:T(2,128)}) custom-call(f32[1,2048,128]{2,1,0:T(8,128)} %cells.1, s32[1,16,256]{2,1,0:T(8,128)} %bitcast.18, s32[1,16,256]{2,1,0:T(8,128)} %bitcast.19), custom_call_target="tpu_custom_call" | custom-call | tf_op jit(solution)/shard_map/message/pallas_call | solution.py:294
  3.7 3.2 %collective-permute-start = (f32[8,2,128]{2,1,0:T(2,128)}, f32[8,2,128]{2,1,0:T(2,128)S(1)}, u32[]{:S(2)}, u32[]{:S(2)}) collective-permute-start(f32[8,2,128]{2,1,0:T(2,128)} %get-tuple-element.13), channel_id=1, source_target_pairs={{0,1},{1,2},{2,3},{4,5},{5,6},{6,7},{8,9},{9,10},{10,11},{12,13},{... | collective-permute-start | bytes 24584 | tf_op jit(solution)/shard_map/ppermute | solution.py:306
  6.9 2.7 %collective-permute-start.1 = (f32[8,2,128]{2,1,0:T(2,128)}, f32[8,2,128]{2,1,0:T(2,128)S(1)}, u32[]{:S(2)}, u32[]{:S(2)}) collective-permute-start(f32[8,2,128]{2,1,0:T(2,128)} %get-tuple-element.14), channel_id=1, source_target_pairs={{1,0},{2,1},{3,2},{5,4},{6,5},{7,6},{9,8},{10,9},{11,10},{13,12},{... | collective-permute-start | bytes 24584 | tf_op jit(solution)/shard_map/ppermute | solution.py:307
  9.5 0.0 collective-permute-done.up
  9.5 0.0 copy-start.5
  9.6 3.1 %collective-permute-done.1.down = f32[8,2,128]{2,1,0:T(2,128)S(1)} collective-permute-done((f32[8,2,128]{2,1,0:T(2,128)}, f32[8,2,128]{2,1,0:T(2,128)S(1)}, u32[]{:S(2)}, u32[]{:S(2)}) %collective-permute-start.1) | collective-permute-done | bytes 8224 | tf_op jit(solution)/shard_map/ppermute | solution.py:307
  12.6 0.0 copy-start.6
  12.6 0.0 copy-done.5
  12.6 0.6 copy-done.6
  13.2 1.4 %beside.1 = f32[8,272,128]{2,1,0:T(8,128)} custom-call(f32[8,272,128]{2,1,0:T(8,128)} %get-tuple-element.11._, f32[8,2,128]{2,1,0:T(2,128)} %get-tuple-element.12.sides, f32[8,2,128]{2,1,0:T(2,128)} %copy-done.5, f32[8,2,128]{2,1,0:T(2,128)} %copy-done.6), custom_call_target="tpu_custom_call", output_to_operand_aliasing={{}: (0, {})} | custom-call | tf_op jit(solution)/shard_map/beside/pallas_call | solution.py:308
  14.6 0.0 copy-start.4
  14.6 6.0 %all-to-all-start = ((f32[8,272,128]{2,1,0:T(8,128)}), f32[8,272,128]{2,1,0:T(8,128)S(1)}, u32[]{:S(2)}, u32[]{:S(2)}) async-start(f32[8,272,128]{2,1,0:T(8,128)} %beside.1), calls=%async_computation | async-start | bytes 2228224 | tf_op jit(solution)/shard_map/all_to_all | solution.py:317
  20.7 0.0 copy-done.4
  20.7 2.4 %collective-permute-start.2 = (f32[4,256,128]{2,1,0:T(8,128)S(1)}, f32[4,256,128]{2,1,0:T(8,128)S(1)}, u32[]{:S(2)}, u32[]{:S(2)}) collective-permute-start(f32[4,256,128]{2,1,0:T(8,128)S(1)} %dynamic-slice_bitcast_fusion), channel_id=1, source_target_pairs={{0,4},{28,24},{32,36},{60,56},{64,68},{92,88},{96,100},{124,120},{... | collective-permute-start | bytes 1572872 | tf_op jit(solution)/shard_map/ppermute | solution.py:262
  23.2 1.4 %collective-permute-done.2 = f32[4,256,128]{2,1,0:T(8,128)S(1)} collective-permute-done((f32[4,256,128]{2,1,0:T(8,128)S(1)}, f32[4,256,128]{2,1,0:T(8,128)S(1)}, u32[]{:S(2)}, u32[]{:S(2)}) %collective-permute-start.2) | collective-permute-done | bytes 524320 | tf_op jit(solution)/shard_map/ppermute | solution.py:262
  24.6 0.1 bitcast_select_fusion
  24.7 0.0 copy-start
  24.7 0.0 copy-start.1
  24.7 0.0 copy-start.2
  24.7 0.0 copy-start.3
  24.7 0.1 dynamic-slice_bitcast_fusion.1
  24.8 1.4 %collective-permute-start.3 = (f32[256,128]{1,0:T(8,128)S(1)}, f32[256,128]{1,0:T(8,128)S(1)}, u32[]{:S(2)}, u32[]{:S(2)}) collective-permute-start(f32[256,128]{1,0:T(8,128)S(1)} %get-tuple-element.22), channel_id=1, source_target_pairs={{24,56},{32,0},{28,60},{36,4},{56,88},{64,32},{60,92},{68,36},{88,... | collective-permute-start | bytes 393224 | tf_op jit(solution)/shard_map/ppermute | solution.py:275
  26.2 0.7 collective-permute-start.4
  26.9 0.7 collective-permute-start.5
  27.6 0.7 collective-permute-start.6
  28.3 10.2 %collective-permute-done.3 = f32[256,128]{1,0:T(8,128)S(1)} collective-permute-done((f32[256,128]{1,0:T(8,128)S(1)}, f32[256,128]{1,0:T(8,128)S(1)}, u32[]{:S(2)}, u32[]{:S(2)}) %collective-permute-start.3) | collective-permute-done | bytes 131104 | tf_op jit(solution)/shard_map/ppermute | solution.py:275
  38.5 0.0 collective-permute-done.4
  38.5 0.0 collective-permute-done.5
  38.5 0.0 collective-permute-done.6
  38.6 15.7 %all-to-all-done.cells = f32[8,272,128]{2,1,0:T(8,128)S(1)} async-done(((f32[8,272,128]{2,1,0:T(8,128)}), f32[8,272,128]{2,1,0:T(8,128)S(1)}, u32[]{:S(2)}, u32[]{:S(2)}) %all-to-all-start) | async-done | bytes 1114144 | tf_op jit(solution)/shard_map/all_to_all | solution.py:317
  54.3 0.0 copy-done
  54.3 0.0 copy-done.1
  54.3 0.0 copy-done.2
  54.3 0.0 copy-done.3
  54.3 5.6 %block.1 = (f32[8,4,16,128]{3,2,1,0:T(8,128)S(1)}, f32[8,4,16,128]{3,2,1,0:T(8,128)S(1)}) custom-call(s32[1]{0:T(128)} %bitcast.core, f32[8,272,128]{2,1,0:T(8,128)S(1)} %all-to-all-done.cells, f32[256,128]{1,0:T(8,128)S(1)} %get-tuple-element.18.before, f32[256,128]{1,0:T(8,128)S(1)} %get-tuple-element.17.after, f32[3,16]{1,0:T(4,128)S(1)} %copy-done.2, ...), custom_call_target="tpu_custom_call" | custom-call | tf_op jit(solution)/shard_map/block/pallas_call | solution.py:319
  59.9 1.9 %collective-permute-start.7 = (f32[8,4,16,128]{3,2,1,0:T(8,128)S(1)}, f32[8,4,16,128]{3,2,1,0:T(8,128)S(1)}, u32[]{:S(2)}, u32[]{:S(2)}) collective-permute-start(f32[8,4,16,128]{3,2,1,0:T(8,128)S(1)} %get-tuple-element.16), channel_id=1, source_target_pairs={{0,4},{4,0},{8,12},{12,8},{16,20},{20,16},{24,28},{28,24},{32,36},... | collective-permute-start | bytes 786440 | tf_op jit(solution)/shard_map/ppermute | solution.py:331
  61.8 1.5 %collective-permute-done.7 = f32[8,4,16,128]{3,2,1,0:T(8,128)S(1)} collective-permute-done((f32[8,4,16,128]{3,2,1,0:T(8,128)S(1)}, f32[8,4,16,128]{3,2,1,0:T(8,128)S(1)}, u32[]{:S(2)}, u32[]{:S(2)}) %collective-permute-start.7) | collective-permute-done | bytes 262176 | tf_op jit(solution)/shard_map/ppermute | solution.py:331
  63.4 39.0 %all_to_all.15.parts = f32[16,4,16,128]{3,2,1,0:T(8,128)} all-to-all(f32[16,4,16,128]{3,2,1,0:T(8,128)S(1)} %pad_maximum_fusion), channel_id=1, replica_groups={{0,8,16,24,32,40,48,56,64,72,80,88,96,104,112,120},{68,76,84,92,100,108..., dimensions={0} | all-to-all | bytes 1048576 | tf_op jit(solution)/shard_map/all_to_all | solution.py:335
  102.4 1.7 %merge_z.1 = f32[4,4,16,128]{3,2,1,0:T(8,128)} custom-call(s32[1]{0:T(128)} %bitcast.core, f32[16,4,16,128]{3,2,1,0:T(8,128)} %all_to_all.15.parts), custom_call_target="tpu_custom_call" | custom-call | tf_op jit(solution)/shard_map/merge_z/pallas_call | solution.py:338
  104.1 10.4 %all_to_all.16.parts = f32[4,4,16,128]{3,2,1,0:T(8,128)} all-to-all(f32[4,4,16,128]{3,2,1,0:T(8,128)} %merge_z.1), channel_id=1, replica_groups={{0,128,256,384},{4,132,260,388},{8,136,264,392},{12,140,268,396},{16,14..., dimensions={0} | all-to-all | bytes 262144 | tf_op jit(solution)/shard_map/all_to_all | solution.py:346
  114.5 1.5 %merge_x.1 = f32[4,16,128]{2,1,0:T(8,128)} custom-call(f32[4,4,16,128]{3,2,1,0:T(8,128)} %all_to_all.16.parts), custom_call_target="tpu_custom_call" | custom-call | tf_op jit(solution)/shard_map/merge_x/pallas_call | solution.py:347
  (3 shorter events, 0.1 us)
Async XLA Ops:
  3.7 5.9 %collective-permute-start = (f32[8,2,128]{2,1,0:T(2,128)}, f32[8,2,128]{2,1,0:T(2,128)S(1)}, u32[]{:S(2)}, u32[]{:S(2)}) collective-permute-start(f32[8,2,128]{2,1,0:T(2,128)} %get-tuple-element.13), channel_id=1, source_target_pairs={{0,1},{1,2},{2,3},{4,5},{5,6},{6,7},{8,9},{9,10},{10,11},{12,13},{... | collective-permute-start | bytes 24584 | tf_op jit(solution)/shard_map/ppermute | solution.py:306
  6.9 5.8 %collective-permute-start.1 = (f32[8,2,128]{2,1,0:T(2,128)}, f32[8,2,128]{2,1,0:T(2,128)S(1)}, u32[]{:S(2)}, u32[]{:S(2)}) collective-permute-start(f32[8,2,128]{2,1,0:T(2,128)} %get-tuple-element.14), channel_id=1, source_target_pairs={{1,0},{2,1},{3,2},{5,4},{6,5},{7,6},{9,8},{10,9},{11,10},{13,12},{... | collective-permute-start | bytes 24584 | tf_op jit(solution)/shard_map/ppermute | solution.py:307
  9.5 3.1 %copy-start.5 = (f32[8,2,128]{2,1,0:T(2,128)}, f32[8,2,128]{2,1,0:T(2,128)S(1)}, u32[]{:S(2)}) copy-start(f32[8,2,128]{2,1,0:T(2,128)S(1)} %collective-permute-done.up) | copy-start | bytes 24580
  12.6 0.6 copy-start.6
  14.6 6.1 %copy-start.4 = (f32[1,2048,128]{2,1,0:T(8,128)S(1)}, f32[1,2048,128]{2,1,0:T(8,128)}, u32[]{:S(2)}) copy-start(f32[1,2048,128]{2,1,0:T(8,128)} %cells.1) | copy-start | bytes 3145732
  14.6 39.7 %all-to-all-start = ((f32[8,272,128]{2,1,0:T(8,128)}), f32[8,272,128]{2,1,0:T(8,128)S(1)}, u32[]{:S(2)}, u32[]{:S(2)}) async-start(f32[8,272,128]{2,1,0:T(8,128)} %beside.1), calls=%async_computation | async-start | bytes 2228224 | tf_op jit(solution)/shard_map/all_to_all | solution.py:317
  20.7 3.9 %collective-permute-start.2 = (f32[4,256,128]{2,1,0:T(8,128)S(1)}, f32[4,256,128]{2,1,0:T(8,128)S(1)}, u32[]{:S(2)}, u32[]{:S(2)}) collective-permute-start(f32[4,256,128]{2,1,0:T(8,128)S(1)} %dynamic-slice_bitcast_fusion), channel_id=1, source_target_pairs={{0,4},{28,24},{32,36},{60,56},{64,68},{92,88},{96,100},{124,120},{... | collective-permute-start | bytes 1572872 | tf_op jit(solution)/shard_map/ppermute | solution.py:262
  24.7 29.6 %copy-start = (f32[256,256]{1,0:T(8,128)S(1)}, f32[256,256]{1,0:T(8,128)}, u32[]{:S(2)}) copy-start(f32[256,256]{1,0:T(8,128)} %kernel_x.1) | copy-start | bytes 786436
  24.7 29.6 %copy-start.1 = (f32[128,128]{1,0:T(8,128)S(1)}, f32[128,128]{1,0:T(8,128)}, u32[]{:S(2)}) copy-start(f32[128,128]{1,0:T(8,128)} %kernel_y.1) | copy-start | bytes 196612
  24.7 29.6 %copy-start.2 = (f32[3,16]{1,0:T(4,128)S(1)}, f32[3,16]{1,0:T(4,128)}, u32[]{:S(2)}) copy-start(f32[3,16]{1,0:T(4,128)} %colours.1) | copy-start | bytes 580
  24.7 29.6 %copy-start.3 = (f32[16]{0:T(128)S(1)}, f32[16]{0:T(128)}, u32[]{:S(2)}) copy-start(f32[16]{0:T(128)} %absorb.1) | copy-start | bytes 196
  24.8 13.7 %collective-permute-start.3 = (f32[256,128]{1,0:T(8,128)S(1)}, f32[256,128]{1,0:T(8,128)S(1)}, u32[]{:S(2)}, u32[]{:S(2)}) collective-permute-start(f32[256,128]{1,0:T(8,128)S(1)} %get-tuple-element.22), channel_id=1, source_target_pairs={{24,56},{32,0},{28,60},{36,4},{56,88},{64,32},{60,92},{68,36},{88,... | collective-permute-start | bytes 393224 | tf_op jit(solution)/shard_map/ppermute | solution.py:275
  26.2 12.3 %collective-permute-start.4 = (f32[256,128]{1,0:T(8,128)S(1)}, f32[256,128]{1,0:T(8,128)S(1)}, u32[]{:S(2)}, u32[]{:S(2)}) collective-permute-start(f32[256,128]{1,0:T(8,128)S(1)} %get-tuple-element.21), channel_id=1, source_target_pairs={{24,48},{32,8},{28,52},{36,12},{56,80},{64,40},{60,84},{68,44},{88... | collective-permute-start | bytes 393224 | tf_op jit(solution)/shard_map/ppermute | solution.py:275
  26.9 11.6 %collective-permute-start.5 = (f32[256,128]{1,0:T(8,128)S(1)}, f32[256,128]{1,0:T(8,128)S(1)}, u32[]{:S(2)}, u32[]{:S(2)}) collective-permute-start(f32[256,128]{1,0:T(8,128)S(1)} %get-tuple-element.20), channel_id=1, source_target_pairs={{24,40},{32,16},{28,44},{36,20},{56,72},{64,48},{60,76},{68,52},{8... | collective-permute-start | bytes 393224 | tf_op jit(solution)/shard_map/ppermute | solution.py:275
  27.6 10.9 %collective-permute-start.6 = (f32[256,128]{1,0:T(8,128)S(1)}, f32[256,128]{1,0:T(8,128)S(1)}, u32[]{:S(2)}, u32[]{:S(2)}) collective-permute-start(f32[256,128]{1,0:T(8,128)S(1)} %get-tuple-element.19), channel_id=1, source_target_pairs={{24,32},{32,24},{28,36},{36,28},{56,64},{64,56},{60,68},{68,60},{8... | collective-permute-start | bytes 393224 | tf_op jit(solution)/shard_map/ppermute | solution.py:275
  59.9 3.4 %collective-permute-start.7 = (f32[8,4,16,128]{3,2,1,0:T(8,128)S(1)}, f32[8,4,16,128]{3,2,1,0:T(8,128)S(1)}, u32[]{:S(2)}, u32[]{:S(2)}) collective-permute-start(f32[8,4,16,128]{3,2,1,0:T(8,128)S(1)} %get-tuple-element.16), channel_id=1, source_target_pairs={{0,4},{4,0},{8,12},{12,8},{16,20},{20,16},{24,28},{28,24},{32,36},... | collective-permute-start | bytes 786440 | tf_op jit(solution)/shard_map/ppermute | solution.py:331

commit v4 on v3

--- a/solution.py
+++ b/solution.py
@@ -51,10 +51,16 @@
     return high, middle, (rest - middle.astype(jnp.float32)).astype(jnp.bfloat16)
 
 
-def message_kernel(cells, material, occupancy, message, first, last, sides, held, bricks, sems):
-    load = pltpu.make_async_copy(cells.at[0], held, sems.at[0])
-    load.start()
-    copies = []
+def message_kernel(cells, material, occupancy, message, held, sems):
+    loads, stores = [], []
+    for block in range(BLOCKS):
+        loads.append(
+            pltpu.make_async_copy(
+                cells.at[0, block * COLS : (block + 1) * COLS], held.at[block, :COLS], sems.at[0, block]
+            )
+        )
+        stores.append(pltpu.make_async_copy(held.at[block], message.at[block], sems.at[1, block]))
+        loads[-1].start()
     brick_rows = material.shape[1]
     lane = iota((brick_rows, ROWS), 1)
     row = iota((brick_rows, ROWS), 0)
@@ -73,50 +79,34 @@
             ones_where(lane == row + (at + brick_rows)),
             preferred_element_type=jnp.float32,
         )
-    bricks[...] = packed.reshape(BLOCKS, 8, ROWS)
-    copies.append(pltpu.make_async_copy(bricks, message.at[:, COLS + 8 : MESSAGE], sems.at[1 + BLOCKS]))
-    copies[-1].start()
-    load.wait()
-    for block in range(BLOCKS):
-        copies.append(
-            pltpu.make_async_copy(
-                held.at[block * COLS : (block + 1) * COLS], message.at[block, :COLS], sems.at[1 + block]
-            )
-        )
-        copies[-1].start()
     ends = ones_where(
         (iota((8, ROWS), 0) == 0) & (iota((8, ROWS), 1) == 0)
         | (iota((8, ROWS), 0) == 1) & (iota((8, ROWS), 1) == ROWS - 1)
     ).astype(jnp.bfloat16)
+    none = jnp.zeros((1, ROWS), jnp.float32)
+    loads[0].wait()
     for block in range(BLOCKS):
-        left, right = block * COLS, (block + 1) * COLS
+        if block < BLOCKS - 1:
+            loads[block + 1].wait()
         taken = sum(
             lax.dot_general(ends, term, (((1,), (1,)), ((), ())), preferred_element_type=jnp.float32)
-            for term in reversed(thirds(held[left:right]))
+            for term in reversed(thirds(held[block, :COLS]))
         )
-        for part in range(2):
-            at = part * ROWS
-            first[block, part : part + 1] = taken[0:1, at : at + ROWS]
-            last[block, part : part + 1] = taken[1:2, at : at + ROWS]
-        none = jnp.zeros((1, ROWS), jnp.float32)
-        sides[block, 0:1] = held[left - 1 : left] if block else none
-        sides[block, 1:2] = held[right : right + 1] if block < BLOCKS - 1 else none
-    for copy in copies:
-        copy.wait()
-
-
-def beside_kernel(_, sides, up, down, message, rows, sem):
-    rows[:, 0:2] = sides[...]
-    rows[:, 2:4] = up[...]
-    rows[:, 4:6] = down[...]
-    rows[:, 6:8] = jnp.zeros((BLOCKS, 2, ROWS), jnp.float32)
-    copy = pltpu.make_async_copy(rows, message.at[:, COLS : COLS + 8], sem)
-    copy.start()
-    copy.wait()
+        held[block, COLS : COLS + 1] = held[block - 1, COLS - 1 : COLS] if block else none
+        held[block, COLS + 1 : COLS + 2] = held[block + 1, 0:1] if block < BLOCKS - 1 else none
+        for end in range(2):
+            for part in range(2):
+                at = COLS + 2 + 2 * end + part
+                held[block, at : at + 1] = taken[end : end + 1, part * ROWS : (part + 1) * ROWS]
+        held[block, COLS + 6 : COLS + 8] = jnp.zeros((2, ROWS), jnp.float32)
+        held[block, COLS + 8 : MESSAGE] = packed[block * 8 : block * 8 + 8]
+        stores[block].start()
+    for store in stores:
+        store.wait()
 
 
 def block_kernel(
-    step, core, cells, before, after, colours, absorb, kernel_x, kernel_y, kept, given, fields, bricks
+    step, core, cells, up, down, before, after, colours, absorb, kernel_x, kernel_y, kept, given, fields, bricks
 ):
     eye_y = ones_where(iota((ROWS, ROWS), 0) == iota((ROWS, ROWS), 1))
     along_y = 0.5 * eye_y + kernel_y[...]
@@ -130,9 +120,9 @@
     along_x = halves((0.5 * eye_x + kernel_x[...]).T)
     beside = jnp.concatenate(
         [
-            jnp.concatenate([cells[s, at : at + 1], cells[s, at + 1 : at + 2]], axis=1)
+            jnp.concatenate([rows[s, 0:1], rows[s, 1:2]], axis=1)
             for s in range(SLICES)
-            for at in (COLS + 2, COLS + 4)
+            for rows in (up, down)
         ],
         axis=0,
     )
@@ -226,31 +216,7 @@
 
 
 def over(nearer, farther):
-    clear = 1.0 - nearer[3]
-    return [nearer[f] + clear * farther[f] for f in range(FIELDS)]
-
-
-def merge_z_kernel(core, parts, image):
-    for block in range(4):
-        for i in range(PIECE // 8):
-            at = slice(8 * i, 8 * i + 8)
-            total = None
-            for group in range(4):
-                chip = (4 * group + block) ^ (CHIPS * core[0])
-                part = [parts[chip, f, at] for f in range(FIELDS)]
-                total = over(total, part) if total else part
-            for f in range(FIELDS):
-                image[block, f, at] = total[f]
-
-
-def merge_x_kernel(parts, image):
-    for i in range(PIECE // 8):
-        at = slice(8 * i, 8 * i + 8)
-        total = [parts[0, f, at] for f in range(FIELDS)]
-        for x in range(1, 4):
-            total = over(total, [parts[x, f, at] for f in range(FIELDS)])
-        for f in range(FIELDS):
-            image[f, at] = total[f]
+    return nearer + (1.0 - nearer[..., 3:4, :, :]) * farther
 
 
 def outer_blocks(distance, groups):
@@ -291,43 +257,30 @@
         return jax.ShapeDtypeStruct(shape, jnp.float32)
 
     before, after = outer_blocks(distance, groups)
-    message, first, last, sides = pl.pallas_call(
+    message = pl.pallas_call(
         message_kernel,
-        out_shape=[one(BLOCKS, MESSAGE, ROWS)] + [one(BLOCKS, 2, ROWS)] * 3,
+        out_shape=one(BLOCKS, MESSAGE, ROWS),
         in_specs=[ANY] + [VMEM] * 2,
-        out_specs=[ANY] + [VMEM] * 3,
-        scratch_shapes=[
-            pltpu.VMEM((col_count, row_count), jnp.float32),
-            pltpu.VMEM((BLOCKS, 8, ROWS), jnp.float32),
-            pltpu.SemaphoreType.DMA((2 + BLOCKS,)),
-        ],
+        out_specs=ANY,
+        scratch_shapes=[pltpu.VMEM((BLOCKS, MESSAGE, ROWS), jnp.float32), pltpu.SemaphoreType.DMA((2, BLOCKS))],
         name="message",
     )(distance, jnp.swapaxes(material, 1, 2), jnp.swapaxes(occupancy, 1, 2))
-    up = lax.ppermute(last, "narrow", [(i, i + 1) for i in range(narrow - 1)])
-    down = lax.ppermute(first, "narrow", [(i + 1, i) for i in range(narrow - 1)])
-    message = pl.pallas_call(
-        beside_kernel,
-        out_shape=one(BLOCKS, MESSAGE, ROWS),
-        in_specs=[ANY] + [VMEM] * 3,
-        out_specs=ANY,
-        scratch_shapes=[pltpu.VMEM((BLOCKS, 8, ROWS), jnp.float32), pltpu.SemaphoreType.DMA],
-        input_output_aliases={0: 0},
-        name="beside",
-    )(message, sides, up, down)
     cells = lax.all_to_all(message, "wide", 0, 0, tiled=True, axis_index_groups=members)
+    up = lax.ppermute(cells[:, COLS + 4 : COLS + 6], "narrow", [(i, i + 1) for i in range(narrow - 1)])
+    down = lax.ppermute(cells[:, COLS + 2 : COLS + 4], "narrow", [(i + 1, i) for i in range(narrow - 1)])
     step = 4.0 / (slices * wide)
     kept, given = pl.pallas_call(
         functools.partial(block_kernel, step),
         out_shape=[one(CHIPS, FIELDS, PIECE, ROWS)] * 2,
-        in_specs=[SMEM] + [VMEM] * 3 + [SMEM] * 2 + [VMEM] * 2,
+        in_specs=[SMEM] + [VMEM] * 5 + [SMEM] * 2 + [VMEM] * 2,
         out_specs=[VMEM] * 2,
         scratch_shapes=[
             pltpu.VMEM((2 * SLICES + 2, COLS, ROWS), jnp.float32),
             pltpu.VMEM((FIELDS, SLICES, COLS // 8, ROWS), jnp.float32),
         ],
-        compiler_params=pltpu.CompilerParams(vmem_limit_bytes=40 * 1024 * 1024),
+        compiler_params=pltpu.CompilerParams(vmem_limit_bytes=24 * 1024 * 1024),
         name="block",
-    )(core, cells, before, after, colours, absorb, kernel_x, kernel_y)
+    )(core, cells, up, down, before, after, colours, absorb, kernel_x, kernel_y)
     taken = lax.ppermute(given, "wide", [(i, i ^ 1) for i in range(wide)])
     along_z = [
         [32 * x + 2 * ((z + CHIPS * c) % 16) + c for z in range(16)] for x in range(wide // 32) for c in range(2)
@@ -335,22 +288,13 @@
     parts = lax.all_to_all(
         jnp.concatenate([kept, taken], axis=0), "wide", 0, 0, tiled=True, axis_index_groups=along_z
     )
-    parts = pl.pallas_call(
-        merge_z_kernel,
-        out_shape=one(4, FIELDS, PIECE, ROWS),
-        in_specs=[SMEM, VMEM],
-        out_specs=VMEM,
-        name="merge_z",
-    )(core, parts)
+    parts = parts.reshape(2, 2, 4, FIELDS, PIECE, ROWS)
+    halves_z = [over(parts[h, 0], parts[h, 1]) for h in range(2)]
+    front = core[0] == 0
+    parts = over(jnp.where(front, halves_z[0], halves_z[1]), jnp.where(front, halves_z[1], halves_z[0]))
     along_x = [[32 * x + i for x in range(4)] for i in range(32)]
     parts = lax.all_to_all(parts, "wide", 0, 0, tiled=True, axis_index_groups=along_x)
-    return pl.pallas_call(
-        merge_x_kernel,
-        out_shape=one(FIELDS, PIECE, ROWS),
-        in_specs=[VMEM],
-        out_specs=VMEM,
-        name="merge_x",
-    )(parts)
+    return over(over(parts[0], parts[1]), over(parts[2], parts[3]))
 
 
 def solution(mesh):

time: 117 us -> 113 us (0.966)
  the two profiles are of different devices: /device:TPU:16 before, /device:TPU:8 now
where the time goes in v4:
time: 113 us
  waiting for transfers between devices  57.5 us (51%)
  starting transfers between devices  33.2 us (29%)
  blocking collectives  10.1 us (9%)
  Pallas kernels  9.71 us (9%)
  other arithmetic  1.7 us (2%)
    all_to_all x1, waiting for transfers between devices, local(): lax.all_to_all(jnp.concatenate([kept, taken], axis=0), 'wide', 0, 0, tile...  26.3 us
    all_to_all x1, waiting for transfers between devices, local(): lax.all_to_all(message, 'wide', 0, 0, tiled=True, axis_index_groups=members)  26 us
    all_to_all x1, starting transfers between devices, local(): lax.all_to_all(jnp.concatenate([kept, taken], axis=0), 'wide', 0, 0, tile...  12.8 us
    all_to_all x1, blocking collectives, local(): lax.all_to_all(parts, 'wide', 0, 0, tiled=True, axis_index_groups=along_x)  10.1 us
    all_to_all x1, starting transfers between devices, local(): lax.all_to_all(message, 'wide', 0, 0, tiled=True, axis_index_groups=members)  6.04 us
    pallas_call x1, Pallas kernels, local(): pl.pallas_call(functools.partial(block_kernel, step), out_shape=[one(CHIP...  5.62 us
    pallas_call x1, Pallas kernels, local(): pl.pallas_call(message_kernel, out_shape=one(BLOCKS, MESSAGE, ROWS), in_s...  4.09 us
    ppermute x1, starting transfers between devices, local(): lax.ppermute(cells[:, COLS + 4:COLS + 6], 'narrow', [(i, i + 1) for i in...  3.48 us
  transfers between devices with their start and end apart: 10, of which 5 were waited for; matrix products, arithmetic and copies ran while one was open for 0% of the time, Pallas kernels for 0%

profile of v4, /device:TPU:8, one launch (start us, length us, event | category | flops | bytes accessed | tf_op | source)
XLA Modules:
  0.0 112.7 jit_solution(3001210655300849999)
XLA Ops:
  0.0 4.1 %message.1 = f32[8,272,128]{2,1,0:T(8,128)} custom-call(f32[1,2048,128]{2,1,0:T(8,128)} %cells.1, s32[1,16,256]{2,1,0:T(8,128)} %bitcast.94, s32[1,16,256]{2,1,0:T(8,128)} %bitcast.95), custom_call_target="tpu_custom_call" | custom-call | tf_op jit(solution)/shard_map/message/pallas_call | solution.py:260
  4.1 0.0 copy-start.4
  4.1 6.0 %all-to-all-start = ((f32[8,272,128]{2,1,0:T(8,128)}), f32[8,272,128]{2,1,0:T(8,128)S(1)}, u32[]{:S(2)}, u32[]{:S(2)}) async-start(f32[8,272,128]{2,1,0:T(8,128)} %message.1), calls=%async_computation | async-start | bytes 2228224 | tf_op jit(solution)/shard_map/all_to_all | solution.py:268
  10.2 0.0 copy-done.4
  10.2 2.4 %collective-permute-start.2 = (f32[4,256,128]{2,1,0:T(8,128)S(1)}, f32[4,256,128]{2,1,0:T(8,128)S(1)}, u32[]{:S(2)}, u32[]{:S(2)}) collective-permute-start(f32[4,256,128]{2,1,0:T(8,128)S(1)} %dynamic-slice_bitcast_fusion), channel_id=1, source_target_pairs={{0,4},{28,24},{32,36},{60,56},{64,68},{92,88},{96,100},{124,120},{... | collective-permute-start | bytes 1572872 | tf_op jit(solution)/shard_map/ppermute | solution.py:228
  12.7 1.4 %collective-permute-done.2 = f32[4,256,128]{2,1,0:T(8,128)S(1)} collective-permute-done((f32[4,256,128]{2,1,0:T(8,128)S(1)}, f32[4,256,128]{2,1,0:T(8,128)S(1)}, u32[]{:S(2)}, u32[]{:S(2)}) %collective-permute-start.2) | collective-permute-done | bytes 524320 | tf_op jit(solution)/shard_map/ppermute | solution.py:228
  14.1 0.1 bitcast_select_fusion
  14.2 0.0 copy-start
  14.2 0.0 copy-start.1
  14.2 0.0 copy-start.2
  14.2 0.0 copy-start.3
  14.2 0.1 dynamic-slice_bitcast_fusion.1
  14.3 1.4 %collective-permute-start.3 = (f32[256,128]{1,0:T(8,128)S(1)}, f32[256,128]{1,0:T(8,128)S(1)}, u32[]{:S(2)}, u32[]{:S(2)}) collective-permute-start(f32[256,128]{1,0:T(8,128)S(1)} %get-tuple-element.18), channel_id=1, source_target_pairs={{24,56},{32,0},{28,60},{36,4},{56,88},{64,32},{60,92},{68,36},{88,... | collective-permute-start | bytes 393224 | tf_op jit(solution)/shard_map/ppermute | solution.py:241
  15.7 0.7 collective-permute-start.4
  16.4 0.7 collective-permute-start.5
  17.1 0.7 collective-permute-start.6
  17.8 26.0 %all-to-all-done.cells = f32[8,272,128]{2,1,0:T(8,128)S(1)} async-done(((f32[8,272,128]{2,1,0:T(8,128)}), f32[8,272,128]{2,1,0:T(8,128)S(1)}, u32[]{:S(2)}, u32[]{:S(2)}) %all-to-all-start) | async-done | bytes 1114144 | tf_op jit(solution)/shard_map/all_to_all | solution.py:268
  43.8 3.5 %collective-permute-start = (f32[8,2,128]{2,1,0:T(2,128)S(1)}, f32[8,2,128]{2,1,0:T(2,128)S(1)}, u32[]{:S(2)}, u32[]{:S(2)}) collective-permute-start(f32[8,2,128]{2,1,0:T(2,128)S(1)} %get-tuple-element.10), channel_id=1, source_target_pairs={{0,1},{1,2},{2,3},{4,5},{5,6},{6,7},{8,9},{9,10},{10,11},{12,13},{... | collective-permute-start | bytes 24584 | tf_op jit(solution)/shard_map/ppermute | solution.py:269
  47.3 0.0 collective-permute-done.3
  47.3 3.1 %collective-permute-start.1 = (f32[8,2,128]{2,1,0:T(2,128)S(1)}, f32[8,2,128]{2,1,0:T(2,128)S(1)}, u32[]{:S(2)}, u32[]{:S(2)}) collective-permute-start(f32[8,2,128]{2,1,0:T(2,128)S(1)} %get-tuple-element.9), channel_id=1, source_target_pairs={{1,0},{2,1},{3,2},{5,4},{6,5},{7,6},{9,8},{10,9},{11,10},{13,12},{... | collective-permute-start | bytes 24584 | tf_op jit(solution)/shard_map/ppermute | solution.py:270
  50.4 0.0 collective-permute-done.4
  50.4 0.0 collective-permute-done.5
  50.4 0.0 collective-permute-done.6
  50.5 0.0 collective-permute-done.up
  50.5 2.3 %collective-permute-done.1.down = f32[8,2,128]{2,1,0:T(2,128)S(1)} collective-permute-done((f32[8,2,128]{2,1,0:T(2,128)S(1)}, f32[8,2,128]{2,1,0:T(2,128)S(1)}, u32[]{:S(2)}, u32[]{:S(2)}) %collective-permute-start.1) | collective-permute-done | bytes 8224 | tf_op jit(solution)/shard_map/ppermute | solution.py:270
  52.8 0.0 copy-done
  52.8 0.0 copy-done.1
  52.8 0.0 copy-done.2
  52.8 0.0 copy-done.3
  52.9 5.6 %block.1 = (f32[8,4,16,128]{3,2,1,0:T(8,128)S(1)}, f32[8,4,16,128]{3,2,1,0:T(8,128)S(1)}) custom-call(s32[1]{0:T(128)} %bitcast.core, f32[8,272,128]{2,1,0:T(8,128)S(1)} %all-to-all-done.cells, f32[8,2,128]{2,1,0:T(2,128)S(1)} %collective-permute-done.up, f32[8,2,128]{2,1,0:T(2,128)S(1)} %collective-permute-done.1.down, ...), custom_call_target="tpu_custom_call" | custom-call | tf_op jit(solution)/shard_map/block/pallas_call | solution.py:272
  58.5 1.9 %collective-permute-start.7 = (f32[8,4,16,128]{3,2,1,0:T(8,128)S(1)}, f32[8,4,16,128]{3,2,1,0:T(8,128)S(1)}, u32[]{:S(2)}, u32[]{:S(2)}) collective-permute-start(f32[8,4,16,128]{3,2,1,0:T(8,128)S(1)} %get-tuple-element.8), channel_id=1, source_target_pairs={{0,4},{4,0},{8,12},{12,8},{16,20},{20,16},{24,28},{28,24},{32,36},... | collective-permute-start | bytes 786440 | tf_op jit(solution)/shard_map/ppermute | solution.py:284
  60.4 1.5 %collective-permute-done.7 = f32[8,4,16,128]{3,2,1,0:T(8,128)S(1)} collective-permute-done((f32[8,4,16,128]{3,2,1,0:T(8,128)S(1)}, f32[8,4,16,128]{3,2,1,0:T(8,128)S(1)}, u32[]{:S(2)}, u32[]{:S(2)}) %collective-permute-start.7) | collective-permute-done | bytes 262176 | tf_op jit(solution)/shard_map/ppermute | solution.py:284
  61.9 0.9 pad_maximum_fusion
  62.8 12.8 %all-to-all-start.1 = ((f32[16,4,16,128]{3,2,1,0:T(8,128)}), f32[16,4,16,128]{3,2,1,0:T(8,128)S(1)}, u32[]{:S(2)}, u32[]{:S(2)}) async-start(f32[16,4,16,128]{3,2,1,0:T(8,128)} %pad_maximum_fusion), calls=%async_computation.1 | async-start | bytes 1048576 | tf_op jit(solution)/shard_map/all_to_all | solution.py:288
  75.6 26.3 %all-to-all-done.1 = f32[16,4,16,128]{3,2,1,0:T(8,128)S(1)} async-done(((f32[16,4,16,128]{3,2,1,0:T(8,128)}), f32[16,4,16,128]{3,2,1,0:T(8,128)S(1)}, u32[]{:S(2)}, u32[]{:S(2)}) %all-to-all-start.1) | async-done | bytes 524320 | tf_op jit(solution)/shard_map/all_to_all | solution.py:288
  102.0 10.1 %all_to_all.15 = f32[4,4,16,128]{3,2,1,0:T(8,128)S(1)} all-to-all(f32[4,4,16,128]{3,2,1,0:T(8,128)S(1)} %multiply_add_fusion), channel_id=1, replica_groups={{0,128,256,384},{4,132,260,388},{8,136,264,392},{12,140,268,396},{16,14..., dimensions={0} | all-to-all | bytes 262144 | tf_op jit(solution)/shard_map/all_to_all | solution.py:296
  112.1 0.6 fusion.7
  (11 shorter events, 0.2 us)
Async XLA Ops:
  4.1 6.1 %copy-start.4 = (f32[1,2048,128]{2,1,0:T(8,128)S(1)}, f32[1,2048,128]{2,1,0:T(8,128)}, u32[]{:S(2)}) copy-start(f32[1,2048,128]{2,1,0:T(8,128)} %cells.1) | copy-start | bytes 3145732
  4.1 39.7 %all-to-all-start = ((f32[8,272,128]{2,1,0:T(8,128)}), f32[8,272,128]{2,1,0:T(8,128)S(1)}, u32[]{:S(2)}, u32[]{:S(2)}) async-start(f32[8,272,128]{2,1,0:T(8,128)} %message.1), calls=%async_computation | async-start | bytes 2228224 | tf_op jit(solution)/shard_map/all_to_all | solution.py:268
  10.2 3.9 %collective-permute-start.2 = (f32[4,256,128]{2,1,0:T(8,128)S(1)}, f32[4,256,128]{2,1,0:T(8,128)S(1)}, u32[]{:S(2)}, u32[]{:S(2)}) collective-permute-start(f32[4,256,128]{2,1,0:T(8,128)S(1)} %dynamic-slice_bitcast_fusion), channel_id=1, source_target_pairs={{0,4},{28,24},{32,36},{60,56},{64,68},{92,88},{96,100},{124,120},{... | collective-permute-start | bytes 1572872 | tf_op jit(solution)/shard_map/ppermute | solution.py:228
  14.2 38.6 %copy-start = (f32[256,256]{1,0:T(8,128)S(1)}, f32[256,256]{1,0:T(8,128)}, u32[]{:S(2)}) copy-start(f32[256,256]{1,0:T(8,128)} %kernel_x.1) | copy-start | bytes 786436
  14.2 38.6 %copy-start.1 = (f32[128,128]{1,0:T(8,128)S(1)}, f32[128,128]{1,0:T(8,128)}, u32[]{:S(2)}) copy-start(f32[128,128]{1,0:T(8,128)} %kernel_y.1) | copy-start | bytes 196612
  14.2 38.6 %copy-start.2 = (f32[3,16]{1,0:T(4,128)S(1)}, f32[3,16]{1,0:T(4,128)}, u32[]{:S(2)}) copy-start(f32[3,16]{1,0:T(4,128)} %colours.1) | copy-start | bytes 580
  14.2 38.6 %copy-start.3 = (f32[16]{0:T(128)S(1)}, f32[16]{0:T(128)}, u32[]{:S(2)}) copy-start(f32[16]{0:T(128)} %absorb.1) | copy-start | bytes 196
  14.3 33.0 %collective-permute-start.3 = (f32[256,128]{1,0:T(8,128)S(1)}, f32[256,128]{1,0:T(8,128)S(1)}, u32[]{:S(2)}, u32[]{:S(2)}) collective-permute-start(f32[256,128]{1,0:T(8,128)S(1)} %get-tuple-element.18), channel_id=1, source_target_pairs={{24,56},{32,0},{28,60},{36,4},{56,88},{64,32},{60,92},{68,36},{88,... | collective-permute-start | bytes 393224 | tf_op jit(solution)/shard_map/ppermute | solution.py:241
  15.7 34.7 %collective-permute-start.4 = (f32[256,128]{1,0:T(8,128)S(1)}, f32[256,128]{1,0:T(8,128)S(1)}, u32[]{:S(2)}, u32[]{:S(2)}) collective-permute-start(f32[256,128]{1,0:T(8,128)S(1)} %get-tuple-element.17), channel_id=1, source_target_pairs={{24,48},{32,8},{28,52},{36,12},{56,80},{64,40},{60,84},{68,44},{88... | collective-permute-start | bytes 393224 | tf_op jit(solution)/shard_map/ppermute | solution.py:241
  16.4 34.0 %collective-permute-start.5 = (f32[256,128]{1,0:T(8,128)S(1)}, f32[256,128]{1,0:T(8,128)S(1)}, u32[]{:S(2)}, u32[]{:S(2)}) collective-permute-start(f32[256,128]{1,0:T(8,128)S(1)} %get-tuple-element.16), channel_id=1, source_target_pairs={{24,40},{32,16},{28,44},{36,20},{56,72},{64,48},{60,76},{68,52},{8... | collective-permute-start | bytes 393224 | tf_op jit(solution)/shard_map/ppermute | solution.py:241
  17.1 33.4 %collective-permute-start.6 = (f32[256,128]{1,0:T(8,128)S(1)}, f32[256,128]{1,0:T(8,128)S(1)}, u32[]{:S(2)}, u32[]{:S(2)}) collective-permute-start(f32[256,128]{1,0:T(8,128)S(1)} %get-tuple-element.15), channel_id=1, source_target_pairs={{24,32},{32,24},{28,36},{36,28},{56,64},{64,56},{60,68},{68,60},{8... | collective-permute-start | bytes 393224 | tf_op jit(solution)/shard_map/ppermute | solution.py:241
  43.8 6.7 %collective-permute-start = (f32[8,2,128]{2,1,0:T(2,128)S(1)}, f32[8,2,128]{2,1,0:T(2,128)S(1)}, u32[]{:S(2)}, u32[]{:S(2)}) collective-permute-start(f32[8,2,128]{2,1,0:T(2,128)S(1)} %get-tuple-element.10), channel_id=1, source_target_pairs={{0,1},{1,2},{2,3},{4,5},{5,6},{6,7},{8,9},{9,10},{10,11},{12,13},{... | collective-permute-start | bytes 24584 | tf_op jit(solution)/shard_map/ppermute | solution.py:269
  47.3 5.5 %collective-permute-start.1 = (f32[8,2,128]{2,1,0:T(2,128)S(1)}, f32[8,2,128]{2,1,0:T(2,128)S(1)}, u32[]{:S(2)}, u32[]{:S(2)}) collective-permute-start(f32[8,2,128]{2,1,0:T(2,128)S(1)} %get-tuple-element.9), channel_id=1, source_target_pairs={{1,0},{2,1},{3,2},{5,4},{6,5},{7,6},{9,8},{10,9},{11,10},{13,12},{... | collective-permute-start | bytes 24584 | tf_op jit(solution)/shard_map/ppermute | solution.py:270
  58.5 3.4 %collective-permute-start.7 = (f32[8,4,16,128]{3,2,1,0:T(8,128)S(1)}, f32[8,4,16,128]{3,2,1,0:T(8,128)S(1)}, u32[]{:S(2)}, u32[]{:S(2)}) collective-permute-start(f32[8,4,16,128]{3,2,1,0:T(8,128)S(1)} %get-tuple-element.8), channel_id=1, source_target_pairs={{0,4},{4,0},{8,12},{12,8},{16,20},{20,16},{24,28},{28,24},{32,36},... | collective-permute-start | bytes 786440 | tf_op jit(solution)/shard_map/ppermute | solution.py:284
  62.8 39.1 %all-to-all-start.1 = ((f32[16,4,16,128]{3,2,1,0:T(8,128)}), f32[16,4,16,128]{3,2,1,0:T(8,128)S(1)}, u32[]{:S(2)}, u32[]{:S(2)}) async-start(f32[16,4,16,128]{3,2,1,0:T(8,128)} %pad_maximum_fusion), calls=%async_computation.1 | async-start | bytes 1048576 | tf_op jit(solution)/shard_map/all_to_all | solution.py:288

commit v5 on v4

--- a/solution.py
+++ b/solution.py
@@ -36,6 +36,16 @@
     return one(a_high, b_high) + (one(a_low, b_high) + one(a_high, b_low))
 
 
+def joined(a, b):
+    a_high, a_low = a
+    b_high, b_low = b
+    return jnp.dot(
+        jnp.concatenate([a_high, a_low, a_high], axis=1),
+        jnp.concatenate([b_high, b_high, b_low], axis=0),
+        preferred_element_type=jnp.float32,
+    )
+
+
 def ones_where(condition):
     return jnp.where(condition, 1.0, 0.0)
 
@@ -44,22 +54,12 @@
     return lax.broadcasted_iota(jnp.int32, shape, dim)
 
 
-def thirds(value):
-    high = value.astype(jnp.bfloat16)
-    rest = value - high.astype(jnp.float32)
-    middle = rest.astype(jnp.bfloat16)
-    return high, middle, (rest - middle.astype(jnp.float32)).astype(jnp.bfloat16)
-
-
-def message_kernel(cells, material, occupancy, message, held, sems):
+def message_kernel(cells, material, occupancy, message, held, tail, sems):
     loads, stores = [], []
     for block in range(BLOCKS):
-        loads.append(
-            pltpu.make_async_copy(
-                cells.at[0, block * COLS : (block + 1) * COLS], held.at[block, :COLS], sems.at[0, block]
-            )
-        )
-        stores.append(pltpu.make_async_copy(held.at[block], message.at[block], sems.at[1, block]))
+        part = held.at[block * COLS : (block + 1) * COLS]
+        loads.append(pltpu.make_async_copy(cells.at[0, block * COLS : (block + 1) * COLS], part, sems.at[0, block]))
+        stores.append(pltpu.make_async_copy(part, message.at[block, :COLS], sems.at[1, block]))
         loads[-1].start()
     brick_rows = material.shape[1]
     lane = iota((brick_rows, ROWS), 1)
@@ -79,82 +79,69 @@
             ones_where(lane == row + (at + brick_rows)),
             preferred_element_type=jnp.float32,
         )
-    ends = ones_where(
-        (iota((8, ROWS), 0) == 0) & (iota((8, ROWS), 1) == 0)
-        | (iota((8, ROWS), 0) == 1) & (iota((8, ROWS), 1) == ROWS - 1)
-    ).astype(jnp.bfloat16)
+    ends = jnp.zeros((COLS, ROWS), jnp.float32)
+    lane = iota((COLS, ROWS), 1)
+    for block in range(BLOCKS):
+        loads[block].wait()
+        stores[block].start()
+        turned = pltpu.roll(held[block * COLS : (block + 1) * COLS], 2 * block + 1, 1)
+        ends = jnp.where(lane // 2 == block, turned, ends)
+    ends = ends.T
     none = jnp.zeros((1, ROWS), jnp.float32)
-    loads[0].wait()
     for block in range(BLOCKS):
-        if block < BLOCKS - 1:
-            loads[block + 1].wait()
-        taken = sum(
-            lax.dot_general(ends, term, (((1,), (1,)), ((), ())), preferred_element_type=jnp.float32)
-            for term in reversed(thirds(held[block, :COLS]))
-        )
-        held[block, COLS : COLS + 1] = held[block - 1, COLS - 1 : COLS] if block else none
-        held[block, COLS + 1 : COLS + 2] = held[block + 1, 0:1] if block < BLOCKS - 1 else none
+        left, right = block * COLS, (block + 1) * COLS
+        tail[block, 0:1] = held[left - 1 : left] if block else none
+        tail[block, 1:2] = held[right : right + 1] if block < BLOCKS - 1 else none
         for end in range(2):
+            row = 2 * block + 1 - end
             for part in range(2):
-                at = COLS + 2 + 2 * end + part
-                held[block, at : at + 1] = taken[end : end + 1, part * ROWS : (part + 1) * ROWS]
-        held[block, COLS + 6 : COLS + 8] = jnp.zeros((2, ROWS), jnp.float32)
-        held[block, COLS + 8 : MESSAGE] = packed[block * 8 : block * 8 + 8]
-        stores[block].start()
+                at = 2 + 2 * end + part
+                tail[block, at : at + 1] = ends[row : row + 1, part * ROWS : (part + 1) * ROWS]
+        tail[block, 6:8] = jnp.zeros((2, ROWS), jnp.float32)
+        tail[block, 8:16] = packed[block * 8 : block * 8 + 8]
+    stores.append(pltpu.make_async_copy(tail, message.at[:, COLS:MESSAGE], sems.at[0, 0]))
+    stores[-1].start()
     for store in stores:
         store.wait()
 
 
-def block_kernel(
-    step, core, cells, up, down, before, after, colours, absorb, kernel_x, kernel_y, kept, given, fields, bricks
+def weights(kernel):
+    size = kernel.shape[0]
+    return 0.5 * ones_where(iota((size, size), 0) == iota((size, size), 1)) + kernel[...]
+
+
+def fields_kernel(
+    step, cells, before, after, colours, absorb, kernel_x, kernel_y, distances, slopes_x, slopes_y, bricks
 ):
-    eye_y = ones_where(iota((ROWS, ROWS), 0) == iota((ROWS, ROWS), 1))
-    along_y = 0.5 * eye_y + kernel_y[...]
+    along_x = halves(weights(kernel_x).T)
+    along_y = weights(kernel_y)
     none = jnp.zeros((1, ROWS), jnp.float32)
     slope_y = 0.5 * (
         jnp.concatenate([none, along_y[:-1]], axis=0) - jnp.concatenate([along_y[1:], none], axis=0)
     )
+    only_y = halves(along_y)
     both_y = halves(jnp.concatenate([along_y, slope_y], axis=1))
-    only_y = halves(along_y)
-    eye_x = ones_where(iota((COLS, COLS), 0) == iota((COLS, COLS), 1))
-    along_x = halves((0.5 * eye_x + kernel_x[...]).T)
-    beside = jnp.concatenate(
-        [
-            jnp.concatenate([rows[s, 0:1], rows[s, 1:2]], axis=1)
-            for s in range(SLICES)
-            for rows in (up, down)
-        ],
-        axis=0,
-    )
-    beside = halves(beside.T)
-    corner = jnp.concatenate([-0.5 * along_y[0:1], 0.5 * along_y[-1:]], axis=0)
     column_ends = jnp.concatenate([cells[s, COLS : COLS + 2] for s in range(SLICES)], axis=0)
     column_ends = product(halves(column_ends), only_y)
-    outer = product(
-        halves(jnp.concatenate([before[...], after[...]], axis=0)), only_y
-    )
+    outer = joined(halves(jnp.concatenate([before[...], after[...]], axis=0)), only_y)
     outer = jnp.concatenate([outer[:COLS], outer[COLS:]], axis=1)
-    outer = product(along_x, halves(outer))
-    fields[0] = outer[:, :ROWS]
-    fields[SLICES + 1] = outer[:, ROWS:]
+    outer = joined(along_x, halves(outer))
+    distances[0] = outer[:, :ROWS]
+    distances[SLICES + 1] = outer[:, ROWS:]
     for pair in range(SLICES // 2):
         parts = []
         for s in (2 * pair, 2 * pair + 1):
-            rows = product(halves(cells[s, :COLS]), both_y)
+            rows = joined(halves(cells[s, :COLS]), both_y)
             value = rows[:, :ROWS]
-            row = iota((2 * SLICES, ROWS), 0)
-            wanted = jnp.where(row == 2 * s, corner[0:1], 0.0) + jnp.where(row == 2 * s + 1, corner[1:2], 0.0)
-            slope = rows[:, ROWS:] + product(beside, halves(wanted))
             ahead = jnp.concatenate([value[1:], column_ends[2 * s + 1 : 2 * s + 2]], axis=0)
             behind = jnp.concatenate([column_ends[2 * s : 2 * s + 1], value[:-1]], axis=0)
-            parts += [value, 0.5 * (ahead - behind), slope]
-        mixed = product(along_x, halves(jnp.concatenate(parts, axis=1)))
+            parts += [value, 0.5 * (ahead - behind), rows[:, ROWS:]]
+        mixed = joined(along_x, halves(jnp.concatenate(parts, axis=1)))
         for i, s in enumerate((2 * pair, 2 * pair + 1)):
             at = 3 * i * ROWS
-            fields[1 + s] = mixed[:, at : at + ROWS]
-            u = mixed[:, at + ROWS : at + 2 * ROWS]
-            v = mixed[:, at + 2 * ROWS : at + 3 * ROWS]
-            fields[SLICES + 2 + s] = u * u + v * v
+            distances[1 + s] = mixed[:, at : at + ROWS]
+            slopes_x[s] = mixed[:, at + ROWS : at + 2 * ROWS]
+            slopes_y[s] = mixed[:, at + 2 * ROWS : at + 3 * ROWS]
     codes = cells[:, COLS + 8 : MESSAGE, :].reshape(SLICES * 8, ROWS)
     brick_rows = ROWS // 8
     masks = pltpu.roll(codes, ROWS - brick_rows, 1)
@@ -184,6 +171,25 @@
                     (f * SLICES + s) * 8 : (f * SLICES + s) * 8 + 8, part * ROWS : (part + 1) * ROWS
                 ]
 
+
+def shade_kernel(core, up, down, kernel_x, kernel_y, distances, slopes_x, slopes_y, bricks, kept, given, edges):
+    beside = jnp.concatenate(
+        [
+            jnp.concatenate([rows[s, 0:1], rows[s, 1:2]], axis=1)
+            for s in range(SLICES)
+            for rows in (up, down)
+        ],
+        axis=0,
+    )
+    beside = halves(product(halves(beside), halves(weights(kernel_x))).T)
+    along_y = weights(kernel_y)
+    row = iota((2 * SLICES, ROWS), 0)
+    for s in range(SLICES):
+        wanted = jnp.where(row == 2 * s, -0.5 * along_y[0:1], 0.0) + jnp.where(
+            row == 2 * s + 1, 0.5 * along_y[ROWS - 1 : ROWS], 0.0
+        )
+        edges[s] = product(beside, halves(wanted))
+
     def shade(image, piece, chunk, part):
         row = chunk * (PIECE // 8) + part
         at = pl.ds(pl.multiple_of(row * 8, 8), 8)
@@ -191,9 +197,11 @@
         transmit = jnp.ones((8, ROWS), jnp.float32)
         total = [jnp.zeros((8, ROWS), jnp.float32)] * FIELDS
         for s in range(SLICES):
-            d = fields[1 + s, at]
-            w = 0.5 * (fields[2 + s, at] - fields[s, at])
-            norm = jnp.maximum(fields[SLICES + 2 + s, at] + w * w, 0.1)
+            d = distances[1 + s, at]
+            u = slopes_x[s, at]
+            v = slopes_y[s, at] + edges[s, at]
+            w = 0.5 * (distances[2 + s, at] - distances[s, at])
+            norm = jnp.maximum(u * u + v * v + w * w, 0.1)
             facing = 0.25 + 0.75 * jnp.abs(w) * lax.rsqrt(norm)
             density = jnp.exp(-2.0 * d * d)
             opacity = 1.0 - jnp.exp(-bricks[3, s, brick] * density)
@@ -262,25 +270,40 @@
         out_shape=one(BLOCKS, MESSAGE, ROWS),
         in_specs=[ANY] + [VMEM] * 2,
         out_specs=ANY,
-        scratch_shapes=[pltpu.VMEM((BLOCKS, MESSAGE, ROWS), jnp.float32), pltpu.SemaphoreType.DMA((2, BLOCKS))],
+        scratch_shapes=[
+            pltpu.VMEM((col_count, ROWS), jnp.float32),
+            pltpu.VMEM((BLOCKS, MESSAGE - COLS, ROWS), jnp.float32),
+            pltpu.SemaphoreType.DMA((2, BLOCKS)),
+        ],
         name="message",
     )(distance, jnp.swapaxes(material, 1, 2), jnp.swapaxes(occupancy, 1, 2))
     cells = lax.all_to_all(message, "wide", 0, 0, tiled=True, axis_index_groups=members)
     up = lax.ppermute(cells[:, COLS + 4 : COLS + 6], "narrow", [(i, i + 1) for i in range(narrow - 1)])
     down = lax.ppermute(cells[:, COLS + 2 : COLS + 4], "narrow", [(i + 1, i) for i in range(narrow - 1)])
     step = 4.0 / (slices * wide)
+    fields = pl.pallas_call(
+        functools.partial(fields_kernel, step),
+        out_shape=[
+            one(SLICES + 2, COLS, ROWS),
+            one(SLICES, COLS, ROWS),
+            one(SLICES, COLS, ROWS),
+            one(FIELDS, SLICES, COLS // 8, ROWS),
+        ],
+        in_specs=[VMEM] * 3 + [SMEM] * 2 + [VMEM] * 2,
+        out_specs=[VMEM] * 4,
+        compiler_params=pltpu.CompilerParams(vmem_limit_bytes=24 * 1024 * 1024),
+        cost_estimate=pl.CostEstimate(flops=4 * 10**9, bytes_accessed=6 * 1024 * 1024, transcendentals=0),
+        name="fields",
+    )(cells, before, after, colours, absorb, kernel_x, kernel_y)
     kept, given = pl.pallas_call(
-        functools.partial(block_kernel, step),
+        shade_kernel,
         out_shape=[one(CHIPS, FIELDS, PIECE, ROWS)] * 2,
-        in_specs=[SMEM] + [VMEM] * 5 + [SMEM] * 2 + [VMEM] * 2,
+        in_specs=[SMEM] + [VMEM] * 8,
         out_specs=[VMEM] * 2,
-        scratch_shapes=[
-            pltpu.VMEM((2 * SLICES + 2, COLS, ROWS), jnp.float32),
-            pltpu.VMEM((FIELDS, SLICES, COLS // 8, ROWS), jnp.float32),
-        ],
+        scratch_shapes=[pltpu.VMEM((SLICES, COLS, ROWS), jnp.float32)],
         compiler_params=pltpu.CompilerParams(vmem_limit_bytes=24 * 1024 * 1024),
-        name="block",
-    )(core, cells, up, down, before, after, colours, absorb, kernel_x, kernel_y)
+        name="shade",
+    )(core, up, down, kernel_x, kernel_y, *fields)
     taken = lax.ppermute(given, "wide", [(i, i ^ 1) for i in range(wide)])
     along_z = [
         [32 * x + 2 * ((z + CHIPS * c) % 16) + c for z in range(16)] for x in range(wide // 32) for c in range(2)

time: 113 us -> 110 us (0.973)
  the two profiles are of different devices: /device:TPU:8 before, /device:TPU:16 now
where the time goes in v5:
time: 110 us; the launch traced here: 109 us
  waiting for transfers between devices  55.1 us (50%)
  starting transfers between devices  32.4 us (29%)
  blocking collectives  10.1 us (9%)
  Pallas kernels  9.36 us (9%)
  other arithmetic  1.71 us (2%)
    all_to_all x1, waiting for transfers between devices, local(): lax.all_to_all(jnp.concatenate([kept, taken], axis=0), 'wide', 0, 0, tile...  26.3 us
    all_to_all x1, waiting for transfers between devices, local(): lax.all_to_all(message, 'wide', 0, 0, tiled=True, axis_index_groups=members)  15.7 us
    all_to_all x1, starting transfers between devices, local(): lax.all_to_all(jnp.concatenate([kept, taken], axis=0), 'wide', 0, 0, tile...  12.8 us
    ppermute x4, waiting for transfers between devices, outer_blocks(): lax.ppermute(lax.dynamic_index_in_dim(given, wanted, 0, keepdims=False),...  10.3 us
    all_to_all x1, blocking collectives, local(): lax.all_to_all(parts, 'wide', 0, 0, tiled=True, axis_index_groups=along_x)  10.1 us
    all_to_all x1, starting transfers between devices, local(): lax.all_to_all(message, 'wide', 0, 0, tiled=True, axis_index_groups=members)  6.04 us
    pallas_call x1, Pallas kernels, local(): pl.pallas_call(functools.partial(fields_kernel, step), out_shape=[one(SLI...  3.9 us
    ppermute x4, starting transfers between devices, outer_blocks(): lax.ppermute(lax.dynamic_index_in_dim(given, wanted, 0, keepdims=False),...  3.43 us
  transfers between devices with their start and end apart: 10, of which 5 were waited for; matrix products, arithmetic and copies ran while one was open for 0% of the time, Pallas kernels for 4%

profile of v5, /device:TPU:16, one launch (start us, length us, event | category | flops | bytes accessed | tf_op | source)
XLA Modules:
  0.0 109.2 jit_solution(1738352128254408131)
XLA Ops:
  0.0 3.3 %message.1 = f32[8,272,128]{2,1,0:T(8,128)} custom-call(f32[1,2048,128]{2,1,0:T(8,128)} %cells.1, s32[1,16,256]{2,1,0:T(8,128)} %bitcast.94, s32[1,16,256]{2,1,0:T(8,128)} %bitcast.95), custom_call_target="tpu_custom_call" | custom-call | tf_op jit(solution)/shard_map/message/pallas_call | solution.py:268
  3.3 0.0 copy-start.4
  3.3 6.0 %all-to-all-start = ((f32[8,272,128]{2,1,0:T(8,128)}), f32[8,272,128]{2,1,0:T(8,128)S(1)}, u32[]{:S(2)}, u32[]{:S(2)}) async-start(f32[8,272,128]{2,1,0:T(8,128)} %message.1), calls=%async_computation | async-start | bytes 2228224 | tf_op jit(solution)/shard_map/all_to_all | solution.py:280
  9.3 0.0 copy-done.4
  9.4 2.4 %collective-permute-start.2 = (f32[4,256,128]{2,1,0:T(8,128)S(1)}, f32[4,256,128]{2,1,0:T(8,128)S(1)}, u32[]{:S(2)}, u32[]{:S(2)}) collective-permute-start(f32[4,256,128]{2,1,0:T(8,128)S(1)} %dynamic-slice_bitcast_fusion), channel_id=1, source_target_pairs={{0,4},{28,24},{32,36},{60,56},{64,68},{92,88},{96,100},{124,120},{... | collective-permute-start | bytes 1572872 | tf_op jit(solution)/shard_map/ppermute | solution.py:236
  11.9 1.4 %collective-permute-done.2 = f32[4,256,128]{2,1,0:T(8,128)S(1)} collective-permute-done((f32[4,256,128]{2,1,0:T(8,128)S(1)}, f32[4,256,128]{2,1,0:T(8,128)S(1)}, u32[]{:S(2)}, u32[]{:S(2)}) %collective-permute-start.2) | collective-permute-done | bytes 524320 | tf_op jit(solution)/shard_map/ppermute | solution.py:236
  13.3 0.1 bitcast_select_fusion
  13.4 0.0 copy-start
  13.4 0.0 copy-start.1
  13.4 0.0 copy-start.2
  13.4 0.0 copy-start.3
  13.4 0.1 dynamic-slice_bitcast_fusion.1
  13.5 1.4 %collective-permute-start.3 = (f32[256,128]{1,0:T(8,128)S(1)}, f32[256,128]{1,0:T(8,128)S(1)}, u32[]{:S(2)}, u32[]{:S(2)}) collective-permute-start(f32[256,128]{1,0:T(8,128)S(1)} %get-tuple-element.26), channel_id=1, source_target_pairs={{24,56},{32,0},{28,60},{36,4},{56,88},{64,32},{60,92},{68,36},{88,... | collective-permute-start | bytes 393224 | tf_op jit(solution)/shard_map/ppermute | solution.py:249
  14.9 0.7 collective-permute-start.4
  15.6 0.7 collective-permute-start.5
  16.3 0.7 collective-permute-start.6
  16.9 10.2 %collective-permute-done.3 = f32[256,128]{1,0:T(8,128)S(1)} collective-permute-done((f32[256,128]{1,0:T(8,128)S(1)}, f32[256,128]{1,0:T(8,128)S(1)}, u32[]{:S(2)}, u32[]{:S(2)}) %collective-permute-start.3) | collective-permute-done | bytes 131104 | tf_op jit(solution)/shard_map/ppermute | solution.py:249
  27.2 0.0 collective-permute-done.4
  27.2 0.0 collective-permute-done.5
  27.2 0.0 collective-permute-done.6
  27.2 15.7 %all-to-all-done.cells = f32[8,272,128]{2,1,0:T(8,128)S(1)} async-done(((f32[8,272,128]{2,1,0:T(8,128)}), f32[8,272,128]{2,1,0:T(8,128)S(1)}, u32[]{:S(2)}, u32[]{:S(2)}) %all-to-all-start) | async-done | bytes 1114144 | tf_op jit(solution)/shard_map/all_to_all | solution.py:280
  43.0 3.2 %collective-permute-start = (f32[8,2,128]{2,1,0:T(2,128)S(1)}, f32[8,2,128]{2,1,0:T(2,128)S(1)}, u32[]{:S(2)}, u32[]{:S(2)}) collective-permute-start(f32[8,2,128]{2,1,0:T(2,128)S(1)} %get-tuple-element.18), channel_id=1, source_target_pairs={{0,1},{1,2},{2,3},{4,5},{5,6},{6,7},{8,9},{9,10},{10,11},{12,13},{... | collective-permute-start | bytes 24584 | tf_op jit(solution)/shard_map/ppermute | solution.py:281
  46.2 2.7 %collective-permute-start.1 = (f32[8,2,128]{2,1,0:T(2,128)S(1)}, f32[8,2,128]{2,1,0:T(2,128)S(1)}, u32[]{:S(2)}, u32[]{:S(2)}) collective-permute-start(f32[8,2,128]{2,1,0:T(2,128)S(1)} %get-tuple-element.17), channel_id=1, source_target_pairs={{1,0},{2,1},{3,2},{5,4},{6,5},{7,6},{9,8},{10,9},{11,10},{13,12},{... | collective-permute-start | bytes 24584 | tf_op jit(solution)/shard_map/ppermute | solution.py:282
  48.8 0.0 copy-done
  48.8 0.0 copy-done.1
  48.8 0.0 copy-done.2
  48.8 0.0 copy-done.3
  48.9 3.9 %fields.1 = (f32[10,256,128]{2,1,0:T(8,128)S(1)}, f32[8,256,128]{2,1,0:T(8,128)S(1)}, f32[8,256,128]{2,1,0:T(8,128)S(1)}, f32[4,8,32,128]{3,2,1,0:T(8,128)S(1)}) custom-call(f32[8,272,128]{2,1,0:T(8,128)S(1)} %all-to-all-done.cells, f32[256,128]{1,0:T(8,128)S(1)} %get-tuple-element.22.before, f32[256,128]{1,0:T(8,128)S(1)} %get-tuple-element.21.after, ...), custom_call_target="tpu_custom_call" | custom-call | flops 4000000000 | bytes 6291456 | tf_op jit(solution)/shard_map/fields/pallas_call | solution.py:284
  52.8 0.0 collective-permute-done.up
  52.8 0.0 collective-permute-done.1.down
  52.8 2.2 %shade.1 = (f32[8,4,16,128]{3,2,1,0:T(8,128)S(1)}, f32[8,4,16,128]{3,2,1,0:T(8,128)S(1)}) custom-call(s32[1]{0:T(128)} %bitcast.core, f32[8,2,128]{2,1,0:T(2,128)S(1)} %collective-permute-done.up, f32[8,2,128]{2,1,0:T(2,128)S(1)} %collective-permute-done.1.down, f32[256,256]{1,0:T(8,128)S(1)} %copy-done, f32[128,128]{1,0:T(8,128)S(1)} %copy-done.1, ...), custom_call_target="tpu_custom_call" | custom-call | tf_op jit(solution)/shard_map/shade/pallas_call | solution.py:298
  55.0 1.9 %collective-permute-start.7 = (f32[8,4,16,128]{3,2,1,0:T(8,128)S(1)}, f32[8,4,16,128]{3,2,1,0:T(8,128)S(1)}, u32[]{:S(2)}, u32[]{:S(2)}) collective-permute-start(f32[8,4,16,128]{3,2,1,0:T(8,128)S(1)} %get-tuple-element.16), channel_id=1, source_target_pairs={{0,4},{4,0},{8,12},{12,8},{16,20},{20,16},{24,28},{28,24},{32,36},... | collective-permute-start | bytes 786440 | tf_op jit(solution)/shard_map/ppermute | solution.py:307
  56.9 1.5 %collective-permute-done.7 = f32[8,4,16,128]{3,2,1,0:T(8,128)S(1)} collective-permute-done((f32[8,4,16,128]{3,2,1,0:T(8,128)S(1)}, f32[8,4,16,128]{3,2,1,0:T(8,128)S(1)}, u32[]{:S(2)}, u32[]{:S(2)}) %collective-permute-start.7) | collective-permute-done | bytes 262176 | tf_op jit(solution)/shard_map/ppermute | solution.py:307
  58.4 0.9 pad_maximum_fusion
  59.3 12.8 %all-to-all-start.1 = ((f32[16,4,16,128]{3,2,1,0:T(8,128)}), f32[16,4,16,128]{3,2,1,0:T(8,128)S(1)}, u32[]{:S(2)}, u32[]{:S(2)}) async-start(f32[16,4,16,128]{3,2,1,0:T(8,128)} %pad_maximum_fusion), calls=%async_computation.1 | async-start | bytes 1048576 | tf_op jit(solution)/shard_map/all_to_all | solution.py:311
  72.1 26.3 %all-to-all-done.1 = f32[16,4,16,128]{3,2,1,0:T(8,128)S(1)} async-done(((f32[16,4,16,128]{3,2,1,0:T(8,128)}), f32[16,4,16,128]{3,2,1,0:T(8,128)S(1)}, u32[]{:S(2)}, u32[]{:S(2)}) %all-to-all-start.1) | async-done | bytes 524320 | tf_op jit(solution)/shard_map/all_to_all | solution.py:311
  98.5 10.1 %all_to_all.15 = f32[4,4,16,128]{3,2,1,0:T(8,128)S(1)} all-to-all(f32[4,4,16,128]{3,2,1,0:T(8,128)S(1)} %multiply_add_fusion), channel_id=1, replica_groups={{0,128,256,384},{4,132,260,388},{8,136,264,392},{12,140,268,396},{16,14..., dimensions={0} | all-to-all | bytes 262144 | tf_op jit(solution)/shard_map/all_to_all | solution.py:319
  108.6 0.6 fusion.7
  (11 shorter events, 0.2 us)
Async XLA Ops:
  3.3 6.1 %copy-start.4 = (f32[1,2048,128]{2,1,0:T(8,128)S(1)}, f32[1,2048,128]{2,1,0:T(8,128)}, u32[]{:S(2)}) copy-start(f32[1,2048,128]{2,1,0:T(8,128)} %cells.1) | copy-start | bytes 3145732
  3.3 39.7 %all-to-all-start = ((f32[8,272,128]{2,1,0:T(8,128)}), f32[8,272,128]{2,1,0:T(8,128)S(1)}, u32[]{:S(2)}, u32[]{:S(2)}) async-start(f32[8,272,128]{2,1,0:T(8,128)} %message.1), calls=%async_computation | async-start | bytes 2228224 | tf_op jit(solution)/shard_map/all_to_all | solution.py:280
  9.4 3.9 %collective-permute-start.2 = (f32[4,256,128]{2,1,0:T(8,128)S(1)}, f32[4,256,128]{2,1,0:T(8,128)S(1)}, u32[]{:S(2)}, u32[]{:S(2)}) collective-permute-start(f32[4,256,128]{2,1,0:T(8,128)S(1)} %dynamic-slice_bitcast_fusion), channel_id=1, source_target_pairs={{0,4},{28,24},{32,36},{60,56},{64,68},{92,88},{96,100},{124,120},{... | collective-permute-start | bytes 1572872 | tf_op jit(solution)/shard_map/ppermute | solution.py:236
  13.4 35.5 %copy-start = (f32[256,256]{1,0:T(8,128)S(1)}, f32[256,256]{1,0:T(8,128)}, u32[]{:S(2)}) copy-start(f32[256,256]{1,0:T(8,128)} %kernel_x.3) | copy-start | bytes 786436
  13.4 35.5 %copy-start.1 = (f32[128,128]{1,0:T(8,128)S(1)}, f32[128,128]{1,0:T(8,128)}, u32[]{:S(2)}) copy-start(f32[128,128]{1,0:T(8,128)} %kernel_y.3) | copy-start | bytes 196612
  13.4 35.5 %copy-start.2 = (f32[3,16]{1,0:T(4,128)S(1)}, f32[3,16]{1,0:T(4,128)}, u32[]{:S(2)}) copy-start(f32[3,16]{1,0:T(4,128)} %colours.1) | copy-start | bytes 580
  13.4 35.4 %copy-start.3 = (f32[16]{0:T(128)S(1)}, f32[16]{0:T(128)}, u32[]{:S(2)}) copy-start(f32[16]{0:T(128)} %absorb.1) | copy-start | bytes 196
  13.5 13.7 %collective-permute-start.3 = (f32[256,128]{1,0:T(8,128)S(1)}, f32[256,128]{1,0:T(8,128)S(1)}, u32[]{:S(2)}, u32[]{:S(2)}) collective-permute-start(f32[256,128]{1,0:T(8,128)S(1)} %get-tuple-element.26), channel_id=1, source_target_pairs={{24,56},{32,0},{28,60},{36,4},{56,88},{64,32},{60,92},{68,36},{88,... | collective-permute-start | bytes 393224 | tf_op jit(solution)/shard_map/ppermute | solution.py:249
  14.9 12.3 %collective-permute-start.4 = (f32[256,128]{1,0:T(8,128)S(1)}, f32[256,128]{1,0:T(8,128)S(1)}, u32[]{:S(2)}, u32[]{:S(2)}) collective-permute-start(f32[256,128]{1,0:T(8,128)S(1)} %get-tuple-element.25), channel_id=1, source_target_pairs={{24,48},{32,8},{28,52},{36,12},{56,80},{64,40},{60,84},{68,44},{88... | collective-permute-start | bytes 393224 | tf_op jit(solution)/shard_map/ppermute | solution.py:249
  15.6 11.6 %collective-permute-start.5 = (f32[256,128]{1,0:T(8,128)S(1)}, f32[256,128]{1,0:T(8,128)S(1)}, u32[]{:S(2)}, u32[]{:S(2)}) collective-permute-start(f32[256,128]{1,0:T(8,128)S(1)} %get-tuple-element.24), channel_id=1, source_target_pairs={{24,40},{32,16},{28,44},{36,20},{56,72},{64,48},{60,76},{68,52},{8... | collective-permute-start | bytes 393224 | tf_op jit(solution)/shard_map/ppermute | solution.py:249
  16.3 10.9 %collective-permute-start.6 = (f32[256,128]{1,0:T(8,128)S(1)}, f32[256,128]{1,0:T(8,128)S(1)}, u32[]{:S(2)}, u32[]{:S(2)}) collective-permute-start(f32[256,128]{1,0:T(8,128)S(1)} %get-tuple-element.23), channel_id=1, source_target_pairs={{24,32},{32,24},{28,36},{36,28},{56,64},{64,56},{60,68},{68,60},{8... | collective-permute-start | bytes 393224 | tf_op jit(solution)/shard_map/ppermute | solution.py:249
  43.0 9.8 %collective-permute-start = (f32[8,2,128]{2,1,0:T(2,128)S(1)}, f32[8,2,128]{2,1,0:T(2,128)S(1)}, u32[]{:S(2)}, u32[]{:S(2)}) collective-permute-start(f32[8,2,128]{2,1,0:T(2,128)S(1)} %get-tuple-element.18), channel_id=1, source_target_pairs={{0,1},{1,2},{2,3},{4,5},{5,6},{6,7},{8,9},{9,10},{10,11},{12,13},{... | collective-permute-start | bytes 24584 | tf_op jit(solution)/shard_map/ppermute | solution.py:281
  46.2 6.6 %collective-permute-start.1 = (f32[8,2,128]{2,1,0:T(2,128)S(1)}, f32[8,2,128]{2,1,0:T(2,128)S(1)}, u32[]{:S(2)}, u32[]{:S(2)}) collective-permute-start(f32[8,2,128]{2,1,0:T(2,128)S(1)} %get-tuple-element.17), channel_id=1, source_target_pairs={{1,0},{2,1},{3,2},{5,4},{6,5},{7,6},{9,8},{10,9},{11,10},{13,12},{... | collective-permute-start | bytes 24584 | tf_op jit(solution)/shard_map/ppermute | solution.py:282
  55.0 3.4 %collective-permute-start.7 = (f32[8,4,16,128]{3,2,1,0:T(8,128)S(1)}, f32[8,4,16,128]{3,2,1,0:T(8,128)S(1)}, u32[]{:S(2)}, u32[]{:S(2)}) collective-permute-start(f32[8,4,16,128]{3,2,1,0:T(8,128)S(1)} %get-tuple-element.16), channel_id=1, source_target_pairs={{0,4},{4,0},{8,12},{12,8},{16,20},{20,16},{24,28},{28,24},{32,36},... | collective-permute-start | bytes 786440 | tf_op jit(solution)/shard_map/ppermute | solution.py:307
  59.3 39.1 %all-to-all-start.1 = ((f32[16,4,16,128]{3,2,1,0:T(8,128)}), f32[16,4,16,128]{3,2,1,0:T(8,128)S(1)}, u32[]{:S(2)}, u32[]{:S(2)}) async-start(f32[16,4,16,128]{3,2,1,0:T(8,128)} %pad_maximum_fusion), calls=%async_computation.1 | async-start | bytes 1048576 | tf_op jit(solution)/shard_map/all_to_all | solution.py:311

commit v6 on v5

--- a/solution.py
+++ b/solution.py
@@ -172,35 +172,19 @@
                 ]
 
 
-def shade_kernel(core, up, down, kernel_x, kernel_y, distances, slopes_x, slopes_y, bricks, kept, given, edges):
-    beside = jnp.concatenate(
-        [
-            jnp.concatenate([rows[s, 0:1], rows[s, 1:2]], axis=1)
-            for s in range(SLICES)
-            for rows in (up, down)
-        ],
-        axis=0,
-    )
-    beside = halves(product(halves(beside), halves(weights(kernel_x))).T)
-    along_y = weights(kernel_y)
-    row = iota((2 * SLICES, ROWS), 0)
-    for s in range(SLICES):
-        wanted = jnp.where(row == 2 * s, -0.5 * along_y[0:1], 0.0) + jnp.where(
-            row == 2 * s + 1, 0.5 * along_y[ROWS - 1 : ROWS], 0.0
-        )
-        edges[s] = product(beside, halves(wanted))
-
-    def shade(image, piece, chunk, part):
-        row = chunk * (PIECE // 8) + part
+def shade(core, distances, slopes_x, slopes_y, edges, bricks, image):
+    def tile(chip, part):
+        row = (2 * chip + core) * (PIECE // 8) + part
         at = pl.ds(pl.multiple_of(row * 8, 8), 8)
         brick = pl.ds(row, 1)
         transmit = jnp.ones((8, ROWS), jnp.float32)
         total = [jnp.zeros((8, ROWS), jnp.float32)] * FIELDS
+        d_of = [distances[s, at] for s in range(SLICES + 2)]
         for s in range(SLICES):
-            d = distances[1 + s, at]
+            d = d_of[1 + s]
             u = slopes_x[s, at]
             v = slopes_y[s, at] + edges[s, at]
-            w = 0.5 * (distances[2 + s, at] - distances[s, at])
+            w = 0.5 * (d_of[2 + s] - d_of[s])
             norm = jnp.maximum(u * u + v * v + w * w, 0.1)
             facing = 0.25 + 0.75 * jnp.abs(w) * lax.rsqrt(norm)
             density = jnp.exp(-2.0 * d * d)
@@ -212,15 +196,39 @@
             total[3] = total[3] + weight
             transmit = transmit * (1.0 - opacity)
         for f in range(FIELDS):
-            image[piece, f, 8 * part : 8 * part + 8] = total[f]
-
-    def shade_chip(chip, _):
-        for part in range(PIECE // 8):
-            shade(given, chip, 2 * chip + (1 - core[0]), part)
-            shade(kept, chip, 2 * chip + core[0], part)
+            image[chip, f, 8 * part : 8 * part + 8] = total[f]
+
+    def two(i, _):
+        for chip in (2 * i, 2 * i + 1):
+            for part in range(PIECE // 8):
+                tile(chip, part)
         return 0
 
-    lax.fori_loop(0, CHIPS, shade_chip, 0)
+    lax.fori_loop(0, CHIPS // 2, two, 0)
+
+
+def given_kernel(core, up, down, kernel_x, kernel_y, distances, slopes_x, slopes_y, bricks, given, edges):
+    beside = jnp.concatenate(
+        [
+            jnp.concatenate([rows[s, 0:1], rows[s, 1:2]], axis=1)
+            for s in range(SLICES)
+            for rows in (up, down)
+        ],
+        axis=0,
+    )
+    beside = halves(product(halves(beside), halves(weights(kernel_x))).T)
+    along_y = weights(kernel_y)
+    row = iota((2 * SLICES, ROWS), 0)
+    for s in range(SLICES):
+        wanted = jnp.where(row == 2 * s, -0.5 * along_y[0:1], 0.0) + jnp.where(
+            row == 2 * s + 1, 0.5 * along_y[ROWS - 1 : ROWS], 0.0
+        )
+        edges[s] = product(beside, halves(wanted))
+    shade(1 - core[0], distances, slopes_x, slopes_y, edges, bricks, given)
+
+
+def kept_kernel(core, distances, slopes_x, slopes_y, bricks, edges, kept):
+    shade(core[0], distances, slopes_x, slopes_y, edges, bricks, kept)
 
 
 def over(nearer, farther):
@@ -295,16 +303,27 @@
         cost_estimate=pl.CostEstimate(flops=4 * 10**9, bytes_accessed=6 * 1024 * 1024, transcendentals=0),
         name="fields",
     )(cells, before, after, colours, absorb, kernel_x, kernel_y)
-    kept, given = pl.pallas_call(
-        shade_kernel,
-        out_shape=[one(CHIPS, FIELDS, PIECE, ROWS)] * 2,
+    params = pltpu.CompilerParams(vmem_limit_bytes=24 * 1024 * 1024)
+    half = one(CHIPS, FIELDS, PIECE, ROWS)
+    given, edges = pl.pallas_call(
+        given_kernel,
+        out_shape=[half, one(SLICES, COLS, ROWS)],
         in_specs=[SMEM] + [VMEM] * 8,
         out_specs=[VMEM] * 2,
-        scratch_shapes=[pltpu.VMEM((SLICES, COLS, ROWS), jnp.float32)],
-        compiler_params=pltpu.CompilerParams(vmem_limit_bytes=24 * 1024 * 1024),
-        name="shade",
+        compiler_params=params,
+        name="given",
     )(core, up, down, kernel_x, kernel_y, *fields)
     taken = lax.ppermute(given, "wide", [(i, i ^ 1) for i in range(wide)])
+    taken, front = lax.optimization_barrier((taken, jnp.broadcast_to(core == 0, (PIECE, ROWS))))
+    kept = pl.pallas_call(
+        kept_kernel,
+        out_shape=half,
+        in_specs=[SMEM] + [VMEM] * 5,
+        out_specs=VMEM,
+        compiler_params=params,
+        cost_estimate=pl.CostEstimate(flops=10**8, bytes_accessed=6 * 1024 * 1024, transcendentals=0),
+        name="kept",
+    )(core, *fields, edges)
     along_z = [
         [32 * x + 2 * ((z + CHIPS * c) % 16) + c for z in range(16)] for x in range(wide // 32) for c in range(2)
     ]
@@ -313,7 +332,6 @@
     )
     parts = parts.reshape(2, 2, 4, FIELDS, PIECE, ROWS)
     halves_z = [over(parts[h, 0], parts[h, 1]) for h in range(2)]
-    front = core[0] == 0
     parts = over(jnp.where(front, halves_z[0], halves_z[1]), jnp.where(front, halves_z[1], halves_z[0]))
     along_x = [[32 * x + i for x in range(4)] for i in range(32)]
     parts = lax.all_to_all(parts, "wide", 0, 0, tiled=True, axis_index_groups=along_x)

time: 110 us -> 108 us (0.982)
  blocking collectives: 10.1 us -> 48.9 us
  waiting for transfers between devices: 55.1 us -> 28.2 us
  starting transfers between devices: 32.4 us -> 19.7 us
    all_to_all x0 -> x1, blocking collectives: none -> 38.9 us  [local(): lax.all_to_all(jnp.concatenate([kept, taken], axis=0), 'wide', 0, 0, tile...]
    all_to_all x1 -> x0, waiting for transfers between devices: 26.3 us -> none  [local(): lax.all_to_all(jnp.concatenate([kept, taken], axis=0), 'wide', 0, 0, tile...]
    all_to_all x1 -> x0, starting transfers between devices: 12.8 us -> none  [local(): lax.all_to_all(jnp.concatenate([kept, taken], axis=0), 'wide', 0, 0, tile...]
    pallas_call x1 -> x2, Pallas kernels: 2.2 us -> 2.19 us  [the longest x1 1.56 us: local(): pl.pallas_call(given_kernel, out_shape=[half, one(SLICES, COLS, ROWS)], i...]
  transfers between devices with their start and end apart: 10 -> 9, of which waited for: 5 -> 4; matrix products, arithmetic and copies ran while one was open for 0% -> 0% of each run, Pallas kernels for 4% -> 4%
where the time goes in v6:
time: 108 us
  blocking collectives  48.9 us (45%)
  waiting for transfers between devices  28.2 us (26%)
  starting transfers between devices  19.7 us (18%)
  Pallas kernels  9.34 us (9%)
    all_to_all x1, blocking collectives, local(): lax.all_to_all(jnp.concatenate([kept, taken], axis=0), 'wide', 0, 0, tile...  38.9 us
    all_to_all x1, waiting for transfers between devices, local(): lax.all_to_all(message, 'wide', 0, 0, tiled=True, axis_index_groups=members)  15.7 us
    ppermute x4, waiting for transfers between devices, outer_blocks(): lax.ppermute(lax.dynamic_index_in_dim(given, wanted, 0, keepdims=False),...  10.3 us
    all_to_all x1, blocking collectives, local(): lax.all_to_all(parts, 'wide', 0, 0, tiled=True, axis_index_groups=along_x)  10.1 us
    all_to_all x1, starting transfers between devices, local(): lax.all_to_all(message, 'wide', 0, 0, tiled=True, axis_index_groups=members)  6.04 us
    pallas_call x1, Pallas kernels, local(): pl.pallas_call(functools.partial(fields_kernel, step), out_shape=[one(SLI...  3.9 us
    ppermute x4, starting transfers between devices, outer_blocks(): lax.ppermute(lax.dynamic_index_in_dim(given, wanted, 0, keepdims=False),...  3.43 us
    pallas_call x1, Pallas kernels, local(): pl.pallas_call(message_kernel, out_shape=one(BLOCKS, MESSAGE, ROWS), in_s...  3.25 us
  transfers between devices with their start and end apart: 9, of which 4 were waited for; matrix products, arithmetic and copies ran while one was open for 0% of the time, Pallas kernels for 4%

profile of v6, /device:TPU:16, one launch (start us, length us, event | category | flops | bytes accessed | tf_op | source)
XLA Modules:
  0.0 107.5 jit_solution(2309228792924959908)
XLA Ops:
  0.0 3.3 %message.1 = f32[8,272,128]{2,1,0:T(8,128)} custom-call(f32[1,2048,128]{2,1,0:T(8,128)} %cells.1, s32[1,16,256]{2,1,0:T(8,128)} %bitcast.95, s32[1,16,256]{2,1,0:T(8,128)} %bitcast.96), custom_call_target="tpu_custom_call" | custom-call | tf_op jit(solution)/shard_map/message/pallas_call | solution.py:276
  3.3 0.0 copy-start.4
  3.3 6.0 %all-to-all-start = ((f32[8,272,128]{2,1,0:T(8,128)}), f32[8,272,128]{2,1,0:T(8,128)S(1)}, u32[]{:S(2)}, u32[]{:S(2)}) async-start(f32[8,272,128]{2,1,0:T(8,128)} %message.1), calls=%async_computation | async-start | bytes 2228224 | tf_op jit(solution)/shard_map/all_to_all | solution.py:288
  9.3 0.0 copy-done.4
  9.4 2.4 %collective-permute-start.2 = (f32[4,256,128]{2,1,0:T(8,128)S(1)}, f32[4,256,128]{2,1,0:T(8,128)S(1)}, u32[]{:S(2)}, u32[]{:S(2)}) collective-permute-start(f32[4,256,128]{2,1,0:T(8,128)S(1)} %dynamic-slice_bitcast_fusion), channel_id=1, source_target_pairs={{0,4},{28,24},{32,36},{60,56},{64,68},{92,88},{96,100},{124,120},{... | collective-permute-start | bytes 1572872 | tf_op jit(solution)/shard_map/ppermute | solution.py:244
  11.9 1.4 %collective-permute-done.2 = f32[4,256,128]{2,1,0:T(8,128)S(1)} collective-permute-done((f32[4,256,128]{2,1,0:T(8,128)S(1)}, f32[4,256,128]{2,1,0:T(8,128)S(1)}, u32[]{:S(2)}, u32[]{:S(2)}) %collective-permute-start.2) | collective-permute-done | bytes 524320 | tf_op jit(solution)/shard_map/ppermute | solution.py:244
  13.3 0.1 bitcast_select_fusion
  13.4 0.0 copy-start
  13.4 0.0 copy-start.1
  13.4 0.0 copy-start.2
  13.4 0.0 copy-start.3
  13.4 0.1 dynamic-slice_bitcast_fusion.1
  13.5 1.4 %collective-permute-start.3 = (f32[256,128]{1,0:T(8,128)S(1)}, f32[256,128]{1,0:T(8,128)S(1)}, u32[]{:S(2)}, u32[]{:S(2)}) collective-permute-start(f32[256,128]{1,0:T(8,128)S(1)} %get-tuple-element.30), channel_id=1, source_target_pairs={{24,56},{32,0},{28,60},{36,4},{56,88},{64,32},{60,92},{68,36},{88,... | collective-permute-start | bytes 393224 | tf_op jit(solution)/shard_map/ppermute | solution.py:257
  14.9 0.7 collective-permute-start.4
  15.6 0.7 collective-permute-start.5
  16.2 0.7 collective-permute-start.6
  16.9 10.2 %collective-permute-done.3 = f32[256,128]{1,0:T(8,128)S(1)} collective-permute-done((f32[256,128]{1,0:T(8,128)S(1)}, f32[256,128]{1,0:T(8,128)S(1)}, u32[]{:S(2)}, u32[]{:S(2)}) %collective-permute-start.3) | collective-permute-done | bytes 131104 | tf_op jit(solution)/shard_map/ppermute | solution.py:257
  27.2 0.0 collective-permute-done.4
  27.2 0.0 collective-permute-done.5
  27.2 0.0 collective-permute-done.6
  27.2 15.7 %all-to-all-done.cells = f32[8,272,128]{2,1,0:T(8,128)S(1)} async-done(((f32[8,272,128]{2,1,0:T(8,128)}), f32[8,272,128]{2,1,0:T(8,128)S(1)}, u32[]{:S(2)}, u32[]{:S(2)}) %all-to-all-start) | async-done | bytes 1114144 | tf_op jit(solution)/shard_map/all_to_all | solution.py:288
  42.9 3.2 %collective-permute-start = (f32[8,2,128]{2,1,0:T(2,128)S(1)}, f32[8,2,128]{2,1,0:T(2,128)S(1)}, u32[]{:S(2)}, u32[]{:S(2)}) collective-permute-start(f32[8,2,128]{2,1,0:T(2,128)S(1)} %get-tuple-element.22), channel_id=1, source_target_pairs={{0,1},{1,2},{2,3},{4,5},{5,6},{6,7},{8,9},{9,10},{10,11},{12,13},{... | collective-permute-start | bytes 24584 | tf_op jit(solution)/shard_map/ppermute | solution.py:289
  46.1 2.7 %collective-permute-start.1 = (f32[8,2,128]{2,1,0:T(2,128)S(1)}, f32[8,2,128]{2,1,0:T(2,128)S(1)}, u32[]{:S(2)}, u32[]{:S(2)}) collective-permute-start(f32[8,2,128]{2,1,0:T(2,128)S(1)} %get-tuple-element.21), channel_id=1, source_target_pairs={{1,0},{2,1},{3,2},{5,4},{6,5},{7,6},{9,8},{10,9},{11,10},{13,12},{... | collective-permute-start | bytes 24584 | tf_op jit(solution)/shard_map/ppermute | solution.py:290
  48.8 0.0 copy-done
  48.8 0.0 copy-done.1
  48.8 0.0 copy-done.2
  48.8 0.0 copy-done.3
  48.8 3.9 %fields.1 = (f32[10,256,128]{2,1,0:T(8,128)S(1)}, f32[8,256,128]{2,1,0:T(8,128)S(1)}, f32[8,256,128]{2,1,0:T(8,128)S(1)}, f32[4,8,32,128]{3,2,1,0:T(8,128)S(1)}) custom-call(f32[8,272,128]{2,1,0:T(8,128)S(1)} %all-to-all-done.cells, f32[256,128]{1,0:T(8,128)S(1)} %get-tuple-element.26.before, f32[256,128]{1,0:T(8,128)S(1)} %get-tuple-element.25.after, ...), custom_call_target="tpu_custom_call" | custom-call | flops 4000000000 | bytes 6291456 | tf_op jit(solution)/shard_map/fields/pallas_call | solution.py:292
  52.7 0.0 collective-permute-done.up
  52.8 0.0 collective-permute-done.1.down
  52.8 1.6 %given.1 = (f32[8,4,16,128]{3,2,1,0:T(8,128)S(1)}, f32[8,256,128]{2,1,0:T(8,128)S(1)}) custom-call(s32[1]{0:T(128)} %bitcast.core, f32[8,2,128]{2,1,0:T(2,128)S(1)} %collective-permute-done.up, f32[8,2,128]{2,1,0:T(2,128)S(1)} %collective-permute-done.1.down, f32[256,256]{1,0:T(8,128)S(1)} %copy-done, f32[128,128]{1,0:T(8,128)S(1)} %copy-done.1, ...), custom_call_target="tpu_custom_call" | custom-call | tf_op jit(solution)/shard_map/given/pallas_call | solution.py:308
  54.3 1.9 %collective-permute-start.7 = (f32[8,4,16,128]{3,2,1,0:T(8,128)S(1)}, f32[8,4,16,128]{3,2,1,0:T(8,128)S(1)}, u32[]{:S(2)}, u32[]{:S(2)}) collective-permute-start(f32[8,4,16,128]{3,2,1,0:T(8,128)S(1)} %get-tuple-element.17), channel_id=1, source_target_pairs={{0,4},{4,0},{8,12},{12,8},{16,20},{20,16},{24,28},{28,24},{32,36},... | collective-permute-start | bytes 786440 | tf_op jit(solution)/shard_map/ppermute | solution.py:316
  56.3 0.6 kept.1
  56.9 0.9 collective-permute-done.7
  57.8 38.9 %all_to_all.15 = f32[16,4,16,128]{3,2,1,0:T(8,128)S(1)} all-to-all(f32[16,4,16,128]{3,2,1,0:T(8,128)S(1)} %pad_maximum_fusion), channel_id=1, replica_groups={{0,8,16,24,32,40,48,56,64,72,80,88,96,104,112,120},{68,76,84,92,100,108..., dimensions={0} | all-to-all | bytes 1048576 | tf_op jit(solution)/shard_map/all_to_all | solution.py:330
  96.8 10.1 %all_to_all.16 = f32[4,4,16,128]{3,2,1,0:T(8,128)S(1)} all-to-all(f32[4,4,16,128]{3,2,1,0:T(8,128)S(1)} %multiply_add_fusion), channel_id=1, replica_groups={{0,128,256,384},{4,132,260,388},{8,136,264,392},{12,140,268,396},{16,14..., dimensions={0} | all-to-all | bytes 262144 | tf_op jit(solution)/shard_map/all_to_all | solution.py:337
  106.9 0.6 fusion.7
  (13 shorter events, 0.3 us)
Async XLA Ops:
  3.3 6.1 %copy-start.4 = (f32[1,2048,128]{2,1,0:T(8,128)S(1)}, f32[1,2048,128]{2,1,0:T(8,128)}, u32[]{:S(2)}) copy-start(f32[1,2048,128]{2,1,0:T(8,128)} %cells.1) | copy-start | bytes 3145732
  3.3 39.7 %all-to-all-start = ((f32[8,272,128]{2,1,0:T(8,128)}), f32[8,272,128]{2,1,0:T(8,128)S(1)}, u32[]{:S(2)}, u32[]{:S(2)}) async-start(f32[8,272,128]{2,1,0:T(8,128)} %message.1), calls=%async_computation | async-start | bytes 2228224 | tf_op jit(solution)/shard_map/all_to_all | solution.py:288
  9.4 3.9 %collective-permute-start.2 = (f32[4,256,128]{2,1,0:T(8,128)S(1)}, f32[4,256,128]{2,1,0:T(8,128)S(1)}, u32[]{:S(2)}, u32[]{:S(2)}) collective-permute-start(f32[4,256,128]{2,1,0:T(8,128)S(1)} %dynamic-slice_bitcast_fusion), channel_id=1, source_target_pairs={{0,4},{28,24},{32,36},{60,56},{64,68},{92,88},{96,100},{124,120},{... | collective-permute-start | bytes 1572872 | tf_op jit(solution)/shard_map/ppermute | solution.py:244
  13.4 35.5 %copy-start = (f32[256,256]{1,0:T(8,128)S(1)}, f32[256,256]{1,0:T(8,128)}, u32[]{:S(2)}) copy-start(f32[256,256]{1,0:T(8,128)} %kernel_x.3) | copy-start | bytes 786436
  13.4 35.5 %copy-start.1 = (f32[128,128]{1,0:T(8,128)S(1)}, f32[128,128]{1,0:T(8,128)}, u32[]{:S(2)}) copy-start(f32[128,128]{1,0:T(8,128)} %kernel_y.3) | copy-start | bytes 196612
  13.4 35.5 %copy-start.2 = (f32[3,16]{1,0:T(4,128)S(1)}, f32[3,16]{1,0:T(4,128)}, u32[]{:S(2)}) copy-start(f32[3,16]{1,0:T(4,128)} %colours.1) | copy-start | bytes 580
  13.4 35.4 %copy-start.3 = (f32[16]{0:T(128)S(1)}, f32[16]{0:T(128)}, u32[]{:S(2)}) copy-start(f32[16]{0:T(128)} %absorb.1) | copy-start | bytes 196
  13.5 13.7 %collective-permute-start.3 = (f32[256,128]{1,0:T(8,128)S(1)}, f32[256,128]{1,0:T(8,128)S(1)}, u32[]{:S(2)}, u32[]{:S(2)}) collective-permute-start(f32[256,128]{1,0:T(8,128)S(1)} %get-tuple-element.30), channel_id=1, source_target_pairs={{24,56},{32,0},{28,60},{36,4},{56,88},{64,32},{60,92},{68,36},{88,... | collective-permute-start | bytes 393224 | tf_op jit(solution)/shard_map/ppermute | solution.py:257
  14.9 12.3 %collective-permute-start.4 = (f32[256,128]{1,0:T(8,128)S(1)}, f32[256,128]{1,0:T(8,128)S(1)}, u32[]{:S(2)}, u32[]{:S(2)}) collective-permute-start(f32[256,128]{1,0:T(8,128)S(1)} %get-tuple-element.29), channel_id=1, source_target_pairs={{24,48},{32,8},{28,52},{36,12},{56,80},{64,40},{60,84},{68,44},{88... | collective-permute-start | bytes 393224 | tf_op jit(solution)/shard_map/ppermute | solution.py:257
  15.6 11.6 %collective-permute-start.5 = (f32[256,128]{1,0:T(8,128)S(1)}, f32[256,128]{1,0:T(8,128)S(1)}, u32[]{:S(2)}, u32[]{:S(2)}) collective-permute-start(f32[256,128]{1,0:T(8,128)S(1)} %get-tuple-element.28), channel_id=1, source_target_pairs={{24,40},{32,16},{28,44},{36,20},{56,72},{64,48},{60,76},{68,52},{8... | collective-permute-start | bytes 393224 | tf_op jit(solution)/shard_map/ppermute | solution.py:257
  16.2 10.9 %collective-permute-start.6 = (f32[256,128]{1,0:T(8,128)S(1)}, f32[256,128]{1,0:T(8,128)S(1)}, u32[]{:S(2)}, u32[]{:S(2)}) collective-permute-start(f32[256,128]{1,0:T(8,128)S(1)} %get-tuple-element.27), channel_id=1, source_target_pairs={{24,32},{32,24},{28,36},{36,28},{56,64},{64,56},{60,68},{68,60},{8... | collective-permute-start | bytes 393224 | tf_op jit(solution)/shard_map/ppermute | solution.py:257
  42.9 9.8 %collective-permute-start = (f32[8,2,128]{2,1,0:T(2,128)S(1)}, f32[8,2,128]{2,1,0:T(2,128)S(1)}, u32[]{:S(2)}, u32[]{:S(2)}) collective-permute-start(f32[8,2,128]{2,1,0:T(2,128)S(1)} %get-tuple-element.22), channel_id=1, source_target_pairs={{0,1},{1,2},{2,3},{4,5},{5,6},{6,7},{8,9},{9,10},{10,11},{12,13},{... | collective-permute-start | bytes 24584 | tf_op jit(solution)/shard_map/ppermute | solution.py:289
  46.1 6.6 %collective-permute-start.1 = (f32[8,2,128]{2,1,0:T(2,128)S(1)}, f32[8,2,128]{2,1,0:T(2,128)S(1)}, u32[]{:S(2)}, u32[]{:S(2)}) collective-permute-start(f32[8,2,128]{2,1,0:T(2,128)S(1)} %get-tuple-element.21), channel_id=1, source_target_pairs={{1,0},{2,1},{3,2},{5,4},{6,5},{7,6},{9,8},{10,9},{11,10},{13,12},{... | collective-permute-start | bytes 24584 | tf_op jit(solution)/shard_map/ppermute | solution.py:290
  54.3 3.4 %collective-permute-start.7 = (f32[8,4,16,128]{3,2,1,0:T(8,128)S(1)}, f32[8,4,16,128]{3,2,1,0:T(8,128)S(1)}, u32[]{:S(2)}, u32[]{:S(2)}) collective-permute-start(f32[8,4,16,128]{3,2,1,0:T(8,128)S(1)} %get-tuple-element.17), channel_id=1, source_target_pairs={{0,4},{4,0},{8,12},{12,8},{16,20},{20,16},{24,28},{28,24},{32,36},... | collective-permute-start | bytes 786440 | tf_op jit(solution)/shard_map/ppermute | solution.py:316

commit v7 on v6

--- a/solution.py
+++ b/solution.py
@@ -54,13 +54,21 @@
     return lax.broadcasted_iota(jnp.int32, shape, dim)
 
 
-def message_kernel(cells, material, occupancy, message, held, tail, sems):
+def message_kernel(cells, material_in, occupancy_in, message, held, tail, material, occupancy, sems):
     loads, stores = [], []
+    brick_loads = [
+        pltpu.make_async_copy(material_in, material, sems.at[0, BLOCKS]),
+        pltpu.make_async_copy(occupancy_in, occupancy, sems.at[1, BLOCKS]),
+    ]
+    for load in brick_loads:
+        load.start()
     for block in range(BLOCKS):
         part = held.at[block * COLS : (block + 1) * COLS]
         loads.append(pltpu.make_async_copy(cells.at[0, block * COLS : (block + 1) * COLS], part, sems.at[0, block]))
         stores.append(pltpu.make_async_copy(part, message.at[block, :COLS], sems.at[1, block]))
         loads[-1].start()
+    for load in brick_loads:
+        load.wait()
     brick_rows = material.shape[1]
     lane = iota((brick_rows, ROWS), 1)
     row = iota((brick_rows, ROWS), 0)
@@ -276,12 +284,14 @@
     message = pl.pallas_call(
         message_kernel,
         out_shape=one(BLOCKS, MESSAGE, ROWS),
-        in_specs=[ANY] + [VMEM] * 2,
+        in_specs=[ANY] * 3,
         out_specs=ANY,
         scratch_shapes=[
             pltpu.VMEM((col_count, ROWS), jnp.float32),
             pltpu.VMEM((BLOCKS, MESSAGE - COLS, ROWS), jnp.float32),
-            pltpu.SemaphoreType.DMA((2, BLOCKS)),
+            pltpu.VMEM((1, material.shape[2], material.shape[1]), jnp.int32),
+            pltpu.VMEM((1, material.shape[2], material.shape[1]), jnp.int32),
+            pltpu.SemaphoreType.DMA((2, BLOCKS + 1)),
         ],
         name="message",
     )(distance, jnp.swapaxes(material, 1, 2), jnp.swapaxes(occupancy, 1, 2))

time: 108 us -> 107 us (level)
  no operation moved by 1% of the time
where the time goes in v7:
time: 107 us
  blocking collectives  48.9 us (46%)
  waiting for transfers between devices  28.2 us (26%)
  starting transfers between devices  19.7 us (18%)
  Pallas kernels  8.74 us (8%)
    all_to_all x1, blocking collectives, local(): lax.all_to_all(jnp.concatenate([kept, taken], axis=0), 'wide', 0, 0, tile...  38.9 us
    all_to_all x1, waiting for transfers between devices, local(): lax.all_to_all(message, 'wide', 0, 0, tiled=True, axis_index_groups=members)  15.7 us
    ppermute x4, waiting for transfers between devices, outer_blocks(): lax.ppermute(lax.dynamic_index_in_dim(given, wanted, 0, keepdims=False),...  10.3 us
    all_to_all x1, blocking collectives, local(): lax.all_to_all(parts, 'wide', 0, 0, tiled=True, axis_index_groups=along_x)  10.1 us
    all_to_all x1, starting transfers between devices, local(): lax.all_to_all(message, 'wide', 0, 0, tiled=True, axis_index_groups=members)  6.04 us
    pallas_call x1, Pallas kernels, local(): pl.pallas_call(functools.partial(fields_kernel, step), out_shape=[one(SLI...  3.89 us
    ppermute x4, starting transfers between devices, outer_blocks(): lax.ppermute(lax.dynamic_index_in_dim(given, wanted, 0, keepdims=False),...  3.43 us
    ppermute x1, starting transfers between devices, local(): lax.ppermute(cells[:, COLS + 4:COLS + 6], 'narrow', [(i, i + 1) for i in...  3.19 us
  transfers between devices with their start and end apart: 9, of which 4 were waited for; matrix products, arithmetic and copies ran while one was open for 0% of the time, Pallas kernels for 4%

profile of v7, /device:TPU:16, one launch (start us, length us, event | category | flops | bytes accessed | tf_op | source)
XLA Modules:
  0.0 106.9 jit_solution(17999227050515619119)
XLA Ops:
  0.0 2.6 %message.1 = f32[8,272,128]{2,1,0:T(8,128)} custom-call(f32[1,2048,128]{2,1,0:T(8,128)} %cells.1, s32[1,16,256]{2,1,0:T(8,128)} %bitcast.95, s32[1,16,256]{2,1,0:T(8,128)} %bitcast.96), custom_call_target="tpu_custom_call" | custom-call | tf_op jit(solution)/shard_map/message/pallas_call | solution.py:284
  2.7 0.0 copy-start.4
  2.7 6.0 %all-to-all-start = ((f32[8,272,128]{2,1,0:T(8,128)}), f32[8,272,128]{2,1,0:T(8,128)S(1)}, u32[]{:S(2)}, u32[]{:S(2)}) async-start(f32[8,272,128]{2,1,0:T(8,128)} %message.1), calls=%async_computation | async-start | bytes 2228224 | tf_op jit(solution)/shard_map/all_to_all | solution.py:298
  8.7 0.0 copy-done.4
  8.8 2.4 %collective-permute-start.2 = (f32[4,256,128]{2,1,0:T(8,128)S(1)}, f32[4,256,128]{2,1,0:T(8,128)S(1)}, u32[]{:S(2)}, u32[]{:S(2)}) collective-permute-start(f32[4,256,128]{2,1,0:T(8,128)S(1)} %dynamic-slice_bitcast_fusion), channel_id=1, source_target_pairs={{0,4},{28,24},{32,36},{60,56},{64,68},{92,88},{96,100},{124,120},{... | collective-permute-start | bytes 1572872 | tf_op jit(solution)/shard_map/ppermute | solution.py:252
  11.3 1.4 %collective-permute-done.2 = f32[4,256,128]{2,1,0:T(8,128)S(1)} collective-permute-done((f32[4,256,128]{2,1,0:T(8,128)S(1)}, f32[4,256,128]{2,1,0:T(8,128)S(1)}, u32[]{:S(2)}, u32[]{:S(2)}) %collective-permute-start.2) | collective-permute-done | bytes 524320 | tf_op jit(solution)/shard_map/ppermute | solution.py:252
  12.7 0.1 bitcast_select_fusion
  12.8 0.0 copy-start
  12.8 0.0 copy-start.1
  12.8 0.0 copy-start.2
  12.8 0.0 copy-start.3
  12.8 0.1 dynamic-slice_bitcast_fusion.1
  12.9 1.4 %collective-permute-start.3 = (f32[256,128]{1,0:T(8,128)S(1)}, f32[256,128]{1,0:T(8,128)S(1)}, u32[]{:S(2)}, u32[]{:S(2)}) collective-permute-start(f32[256,128]{1,0:T(8,128)S(1)} %get-tuple-element.30), channel_id=1, source_target_pairs={{24,56},{32,0},{28,60},{36,4},{56,88},{64,32},{60,92},{68,36},{88,... | collective-permute-start | bytes 393224 | tf_op jit(solution)/shard_map/ppermute | solution.py:265
  14.3 0.7 collective-permute-start.4
  15.0 0.7 collective-permute-start.5
  15.6 0.7 collective-permute-start.6
  16.3 10.2 %collective-permute-done.3 = f32[256,128]{1,0:T(8,128)S(1)} collective-permute-done((f32[256,128]{1,0:T(8,128)S(1)}, f32[256,128]{1,0:T(8,128)S(1)}, u32[]{:S(2)}, u32[]{:S(2)}) %collective-permute-start.3) | collective-permute-done | bytes 131104 | tf_op jit(solution)/shard_map/ppermute | solution.py:265
  26.6 0.0 collective-permute-done.4
  26.6 0.0 collective-permute-done.5
  26.6 0.0 collective-permute-done.6
  26.6 15.7 %all-to-all-done.cells = f32[8,272,128]{2,1,0:T(8,128)S(1)} async-done(((f32[8,272,128]{2,1,0:T(8,128)}), f32[8,272,128]{2,1,0:T(8,128)S(1)}, u32[]{:S(2)}, u32[]{:S(2)}) %all-to-all-start) | async-done | bytes 1114144 | tf_op jit(solution)/shard_map/all_to_all | solution.py:298
  42.3 3.2 %collective-permute-start = (f32[8,2,128]{2,1,0:T(2,128)S(1)}, f32[8,2,128]{2,1,0:T(2,128)S(1)}, u32[]{:S(2)}, u32[]{:S(2)}) collective-permute-start(f32[8,2,128]{2,1,0:T(2,128)S(1)} %get-tuple-element.22), channel_id=1, source_target_pairs={{0,1},{1,2},{2,3},{4,5},{5,6},{6,7},{8,9},{9,10},{10,11},{12,13},{... | collective-permute-start | bytes 24584 | tf_op jit(solution)/shard_map/ppermute | solution.py:299
  45.5 2.7 %collective-permute-start.1 = (f32[8,2,128]{2,1,0:T(2,128)S(1)}, f32[8,2,128]{2,1,0:T(2,128)S(1)}, u32[]{:S(2)}, u32[]{:S(2)}) collective-permute-start(f32[8,2,128]{2,1,0:T(2,128)S(1)} %get-tuple-element.21), channel_id=1, source_target_pairs={{1,0},{2,1},{3,2},{5,4},{6,5},{7,6},{9,8},{10,9},{11,10},{13,12},{... | collective-permute-start | bytes 24584 | tf_op jit(solution)/shard_map/ppermute | solution.py:300
  48.2 0.0 copy-done
  48.2 0.0 copy-done.1
  48.2 0.0 copy-done.2
  48.2 0.0 copy-done.3
  48.2 3.9 %fields.1 = (f32[10,256,128]{2,1,0:T(8,128)S(1)}, f32[8,256,128]{2,1,0:T(8,128)S(1)}, f32[8,256,128]{2,1,0:T(8,128)S(1)}, f32[4,8,32,128]{3,2,1,0:T(8,128)S(1)}) custom-call(f32[8,272,128]{2,1,0:T(8,128)S(1)} %all-to-all-done.cells, f32[256,128]{1,0:T(8,128)S(1)} %get-tuple-element.26.before, f32[256,128]{1,0:T(8,128)S(1)} %get-tuple-element.25.after, ...), custom_call_target="tpu_custom_call" | custom-call | flops 4000000000 | bytes 6291456 | tf_op jit(solution)/shard_map/fields/pallas_call | solution.py:302
  52.1 0.0 collective-permute-done.up
  52.2 0.0 collective-permute-done.1.down
  52.2 1.6 %given.1 = (f32[8,4,16,128]{3,2,1,0:T(8,128)S(1)}, f32[8,256,128]{2,1,0:T(8,128)S(1)}) custom-call(s32[1]{0:T(128)} %bitcast.core, f32[8,2,128]{2,1,0:T(2,128)S(1)} %collective-permute-done.up, f32[8,2,128]{2,1,0:T(2,128)S(1)} %collective-permute-done.1.down, f32[256,256]{1,0:T(8,128)S(1)} %copy-done, f32[128,128]{1,0:T(8,128)S(1)} %copy-done.1, ...), custom_call_target="tpu_custom_call" | custom-call | tf_op jit(solution)/shard_map/given/pallas_call | solution.py:318
  53.7 1.9 %collective-permute-start.7 = (f32[8,4,16,128]{3,2,1,0:T(8,128)S(1)}, f32[8,4,16,128]{3,2,1,0:T(8,128)S(1)}, u32[]{:S(2)}, u32[]{:S(2)}) collective-permute-start(f32[8,4,16,128]{3,2,1,0:T(8,128)S(1)} %get-tuple-element.17), channel_id=1, source_target_pairs={{0,4},{4,0},{8,12},{12,8},{16,20},{20,16},{24,28},{28,24},{32,36},... | collective-permute-start | bytes 786440 | tf_op jit(solution)/shard_map/ppermute | solution.py:326
  55.7 0.6 kept.1
  56.3 0.9 collective-permute-done.7
  57.2 38.9 %all_to_all.15 = f32[16,4,16,128]{3,2,1,0:T(8,128)S(1)} all-to-all(f32[16,4,16,128]{3,2,1,0:T(8,128)S(1)} %pad_maximum_fusion), channel_id=1, replica_groups={{0,8,16,24,32,40,48,56,64,72,80,88,96,104,112,120},{68,76,84,92,100,108..., dimensions={0} | all-to-all | bytes 1048576 | tf_op jit(solution)/shard_map/all_to_all | solution.py:340
  96.2 10.1 %all_to_all.16 = f32[4,4,16,128]{3,2,1,0:T(8,128)S(1)} all-to-all(f32[4,4,16,128]{3,2,1,0:T(8,128)S(1)} %multiply_add_fusion), channel_id=1, replica_groups={{0,128,256,384},{4,132,260,388},{8,136,264,392},{12,140,268,396},{16,14..., dimensions={0} | all-to-all | bytes 262144 | tf_op jit(solution)/shard_map/all_to_all | solution.py:347
  106.3 0.6 fusion.7
  (13 shorter events, 0.3 us)
Async XLA Ops:
  2.7 6.1 %copy-start.4 = (f32[1,2048,128]{2,1,0:T(8,128)S(1)}, f32[1,2048,128]{2,1,0:T(8,128)}, u32[]{:S(2)}) copy-start(f32[1,2048,128]{2,1,0:T(8,128)} %cells.1) | copy-start | bytes 3145732
  2.7 39.7 %all-to-all-start = ((f32[8,272,128]{2,1,0:T(8,128)}), f32[8,272,128]{2,1,0:T(8,128)S(1)}, u32[]{:S(2)}, u32[]{:S(2)}) async-start(f32[8,272,128]{2,1,0:T(8,128)} %message.1), calls=%async_computation | async-start | bytes 2228224 | tf_op jit(solution)/shard_map/all_to_all | solution.py:298
  8.8 3.9 %collective-permute-start.2 = (f32[4,256,128]{2,1,0:T(8,128)S(1)}, f32[4,256,128]{2,1,0:T(8,128)S(1)}, u32[]{:S(2)}, u32[]{:S(2)}) collective-permute-start(f32[4,256,128]{2,1,0:T(8,128)S(1)} %dynamic-slice_bitcast_fusion), channel_id=1, source_target_pairs={{0,4},{28,24},{32,36},{60,56},{64,68},{92,88},{96,100},{124,120},{... | collective-permute-start | bytes 1572872 | tf_op jit(solution)/shard_map/ppermute | solution.py:252
  12.8 35.5 %copy-start = (f32[256,256]{1,0:T(8,128)S(1)}, f32[256,256]{1,0:T(8,128)}, u32[]{:S(2)}) copy-start(f32[256,256]{1,0:T(8,128)} %kernel_x.3) | copy-start | bytes 786436
  12.8 35.5 %copy-start.1 = (f32[128,128]{1,0:T(8,128)S(1)}, f32[128,128]{1,0:T(8,128)}, u32[]{:S(2)}) copy-start(f32[128,128]{1,0:T(8,128)} %kernel_y.3) | copy-start | bytes 196612
  12.8 35.5 %copy-start.2 = (f32[3,16]{1,0:T(4,128)S(1)}, f32[3,16]{1,0:T(4,128)}, u32[]{:S(2)}) copy-start(f32[3,16]{1,0:T(4,128)} %colours.1) | copy-start | bytes 580
  12.8 35.4 %copy-start.3 = (f32[16]{0:T(128)S(1)}, f32[16]{0:T(128)}, u32[]{:S(2)}) copy-start(f32[16]{0:T(128)} %absorb.1) | copy-start | bytes 196
  12.9 13.7 %collective-permute-start.3 = (f32[256,128]{1,0:T(8,128)S(1)}, f32[256,128]{1,0:T(8,128)S(1)}, u32[]{:S(2)}, u32[]{:S(2)}) collective-permute-start(f32[256,128]{1,0:T(8,128)S(1)} %get-tuple-element.30), channel_id=1, source_target_pairs={{24,56},{32,0},{28,60},{36,4},{56,88},{64,32},{60,92},{68,36},{88,... | collective-permute-start | bytes 393224 | tf_op jit(solution)/shard_map/ppermute | solution.py:265
  14.3 12.3 %collective-permute-start.4 = (f32[256,128]{1,0:T(8,128)S(1)}, f32[256,128]{1,0:T(8,128)S(1)}, u32[]{:S(2)}, u32[]{:S(2)}) collective-permute-start(f32[256,128]{1,0:T(8,128)S(1)} %get-tuple-element.29), channel_id=1, source_target_pairs={{24,48},{32,8},{28,52},{36,12},{56,80},{64,40},{60,84},{68,44},{88... | collective-permute-start | bytes 393224 | tf_op jit(solution)/shard_map/ppermute | solution.py:265
  15.0 11.6 %collective-permute-start.5 = (f32[256,128]{1,0:T(8,128)S(1)}, f32[256,128]{1,0:T(8,128)S(1)}, u32[]{:S(2)}, u32[]{:S(2)}) collective-permute-start(f32[256,128]{1,0:T(8,128)S(1)} %get-tuple-element.28), channel_id=1, source_target_pairs={{24,40},{32,16},{28,44},{36,20},{56,72},{64,48},{60,76},{68,52},{8... | collective-permute-start | bytes 393224 | tf_op jit(solution)/shard_map/ppermute | solution.py:265
  15.6 10.9 %collective-permute-start.6 = (f32[256,128]{1,0:T(8,128)S(1)}, f32[256,128]{1,0:T(8,128)S(1)}, u32[]{:S(2)}, u32[]{:S(2)}) collective-permute-start(f32[256,128]{1,0:T(8,128)S(1)} %get-tuple-element.27), channel_id=1, source_target_pairs={{24,32},{32,24},{28,36},{36,28},{56,64},{64,56},{60,68},{68,60},{8... | collective-permute-start | bytes 393224 | tf_op jit(solution)/shard_map/ppermute | solution.py:265
  42.3 9.8 %collective-permute-start = (f32[8,2,128]{2,1,0:T(2,128)S(1)}, f32[8,2,128]{2,1,0:T(2,128)S(1)}, u32[]{:S(2)}, u32[]{:S(2)}) collective-permute-start(f32[8,2,128]{2,1,0:T(2,128)S(1)} %get-tuple-element.22), channel_id=1, source_target_pairs={{0,1},{1,2},{2,3},{4,5},{5,6},{6,7},{8,9},{9,10},{10,11},{12,13},{... | collective-permute-start | bytes 24584 | tf_op jit(solution)/shard_map/ppermute | solution.py:299
  45.5 6.6 %collective-permute-start.1 = (f32[8,2,128]{2,1,0:T(2,128)S(1)}, f32[8,2,128]{2,1,0:T(2,128)S(1)}, u32[]{:S(2)}, u32[]{:S(2)}) collective-permute-start(f32[8,2,128]{2,1,0:T(2,128)S(1)} %get-tuple-element.21), channel_id=1, source_target_pairs={{1,0},{2,1},{3,2},{5,4},{6,5},{7,6},{9,8},{10,9},{11,10},{13,12},{... | collective-permute-start | bytes 24584 | tf_op jit(solution)/shard_map/ppermute | solution.py:300
  53.7 3.4 %collective-permute-start.7 = (f32[8,4,16,128]{3,2,1,0:T(8,128)S(1)}, f32[8,4,16,128]{3,2,1,0:T(8,128)S(1)}, u32[]{:S(2)}, u32[]{:S(2)}) collective-permute-start(f32[8,4,16,128]{3,2,1,0:T(8,128)S(1)} %get-tuple-element.17), channel_id=1, source_target_pairs={{0,4},{4,0},{8,12},{12,8},{16,20},{20,16},{24,28},{28,24},{32,36},... | collective-permute-start | bytes 786440 | tf_op jit(solution)/shard_map/ppermute | solution.py:326

commit v8 on v7

--- a/solution.py
+++ b/solution.py
@@ -254,7 +254,7 @@
     first = chip == 0
     given = jnp.where(jnp.where(first, core == 0, core == 1), own, shared)
     before = after = jnp.zeros((COLS, ROWS), jnp.float32)
-    for j in range(chips):
+    for j in (3, 0, 2, 1):
         back = chips - 1 - j
         pairs = []
         for k in range(groups - 1):

time: 107 us -> 107 us (level)
    all_to_all x1, waiting for transfers between devices: 15.7 us -> 8.23 us  [local(): lax.all_to_all(message, 'wide', 0, 0, tiled=True, axis_index_groups=members)]
    ppermute x4, waiting for transfers between devices: 10.3 us -> 17.7 us  [outer_blocks(): lax.ppermute(lax.dynamic_index_in_dim(given, wanted, 0, keepdims=False),...]
where the time goes in v8:
time: 107 us
  blocking collectives  48.9 us (46%)
  waiting for transfers between devices  28.2 us (26%)
  starting transfers between devices  19.7 us (18%)
  Pallas kernels  8.74 us (8%)
    all_to_all x1, blocking collectives, local(): lax.all_to_all(jnp.concatenate([kept, taken], axis=0), 'wide', 0, 0, tile...  38.9 us
    ppermute x4, waiting for transfers between devices, outer_blocks(): lax.ppermute(lax.dynamic_index_in_dim(given, wanted, 0, keepdims=False),...  17.7 us
    all_to_all x1, blocking collectives, local(): lax.all_to_all(parts, 'wide', 0, 0, tiled=True, axis_index_groups=along_x)  10.1 us
    all_to_all x1, waiting for transfers between devices, local(): lax.all_to_all(message, 'wide', 0, 0, tiled=True, axis_index_groups=members)  8.23 us
    all_to_all x1, starting transfers between devices, local(): lax.all_to_all(message, 'wide', 0, 0, tiled=True, axis_index_groups=members)  6.04 us
    pallas_call x1, Pallas kernels, local(): pl.pallas_call(functools.partial(fields_kernel, step), out_shape=[one(SLI...  3.89 us
    ppermute x4, starting transfers between devices, outer_blocks(): lax.ppermute(lax.dynamic_index_in_dim(given, wanted, 0, keepdims=False),...  3.43 us
    ppermute x1, starting transfers between devices, local(): lax.ppermute(cells[:, COLS + 4:COLS + 6], 'narrow', [(i, i + 1) for i in...  3.19 us
  transfers between devices with their start and end apart: 9, of which 4 were waited for; matrix products, arithmetic and copies ran while one was open for 0% of the time, Pallas kernels for 4%

profile of v8, /device:TPU:16, one launch (start us, length us, event | category | flops | bytes accessed | tf_op | source)
XLA Modules:
  0.0 106.9 jit_solution(11368345547773784306)
XLA Ops:
  0.0 2.6 %message.1 = f32[8,272,128]{2,1,0:T(8,128)} custom-call(f32[1,2048,128]{2,1,0:T(8,128)} %cells.1, s32[1,16,256]{2,1,0:T(8,128)} %bitcast.95, s32[1,16,256]{2,1,0:T(8,128)} %bitcast.96), custom_call_target="tpu_custom_call" | custom-call | tf_op jit(solution)/shard_map/message/pallas_call | solution.py:284
  2.7 0.0 copy-start.4
  2.7 6.0 %all-to-all-start = ((f32[8,272,128]{2,1,0:T(8,128)}), f32[8,272,128]{2,1,0:T(8,128)S(1)}, u32[]{:S(2)}, u32[]{:S(2)}) async-start(f32[8,272,128]{2,1,0:T(8,128)} %message.1), calls=%async_computation | async-start | bytes 2228224 | tf_op jit(solution)/shard_map/all_to_all | solution.py:298
  8.7 0.0 copy-done.4
  8.8 2.4 %collective-permute-start.2 = (f32[4,256,128]{2,1,0:T(8,128)S(1)}, f32[4,256,128]{2,1,0:T(8,128)S(1)}, u32[]{:S(2)}, u32[]{:S(2)}) collective-permute-start(f32[4,256,128]{2,1,0:T(8,128)S(1)} %dynamic-slice_bitcast_fusion), channel_id=1, source_target_pairs={{0,4},{28,24},{32,36},{60,56},{64,68},{92,88},{96,100},{124,120},{... | collective-permute-start | bytes 1572872 | tf_op jit(solution)/shard_map/ppermute | solution.py:252
  11.3 1.4 %collective-permute-done.2 = f32[4,256,128]{2,1,0:T(8,128)S(1)} collective-permute-done((f32[4,256,128]{2,1,0:T(8,128)S(1)}, f32[4,256,128]{2,1,0:T(8,128)S(1)}, u32[]{:S(2)}, u32[]{:S(2)}) %collective-permute-start.2) | collective-permute-done | bytes 524320 | tf_op jit(solution)/shard_map/ppermute | solution.py:252
  12.7 0.1 bitcast_select_fusion
  12.8 0.0 copy-start
  12.8 0.0 copy-start.1
  12.8 0.0 copy-start.2
  12.8 0.0 copy-start.3
  12.8 0.1 dynamic-slice_bitcast_fusion.1
  12.9 0.8 collective-permute-start.3
  13.7 0.7 collective-permute-start.4
  14.3 0.7 collective-permute-start.5
  15.0 1.3 %collective-permute-start.6 = (f32[256,128]{1,0:T(8,128)S(1)}, f32[256,128]{1,0:T(8,128)S(1)}, u32[]{:S(2)}, u32[]{:S(2)}) collective-permute-start(f32[256,128]{1,0:T(8,128)S(1)} %get-tuple-element.27), channel_id=1, source_target_pairs={{24,56},{32,0},{28,60},{36,4},{56,88},{64,32},{60,92},{68,36},{88,... | collective-permute-start | bytes 393224 | tf_op jit(solution)/shard_map/ppermute | solution.py:265
  16.3 0.0 collective-permute-done.3
  16.3 0.0 collective-permute-done.4
  16.4 0.0 collective-permute-done.5
  16.4 17.7 %collective-permute-done.6 = f32[256,128]{1,0:T(8,128)S(1)} collective-permute-done((f32[256,128]{1,0:T(8,128)S(1)}, f32[256,128]{1,0:T(8,128)S(1)}, u32[]{:S(2)}, u32[]{:S(2)}) %collective-permute-start.6) | collective-permute-done | bytes 131104 | tf_op jit(solution)/shard_map/ppermute | solution.py:265
  34.1 8.2 %all-to-all-done.cells = f32[8,272,128]{2,1,0:T(8,128)S(1)} async-done(((f32[8,272,128]{2,1,0:T(8,128)}), f32[8,272,128]{2,1,0:T(8,128)S(1)}, u32[]{:S(2)}, u32[]{:S(2)}) %all-to-all-start) | async-done | bytes 1114144 | tf_op jit(solution)/shard_map/all_to_all | solution.py:298
  42.3 3.2 %collective-permute-start = (f32[8,2,128]{2,1,0:T(2,128)S(1)}, f32[8,2,128]{2,1,0:T(2,128)S(1)}, u32[]{:S(2)}, u32[]{:S(2)}) collective-permute-start(f32[8,2,128]{2,1,0:T(2,128)S(1)} %get-tuple-element.22), channel_id=1, source_target_pairs={{0,1},{1,2},{2,3},{4,5},{5,6},{6,7},{8,9},{9,10},{10,11},{12,13},{... | collective-permute-start | bytes 24584 | tf_op jit(solution)/shard_map/ppermute | solution.py:299
  45.5 2.7 %collective-permute-start.1 = (f32[8,2,128]{2,1,0:T(2,128)S(1)}, f32[8,2,128]{2,1,0:T(2,128)S(1)}, u32[]{:S(2)}, u32[]{:S(2)}) collective-permute-start(f32[8,2,128]{2,1,0:T(2,128)S(1)} %get-tuple-element.21), channel_id=1, source_target_pairs={{1,0},{2,1},{3,2},{5,4},{6,5},{7,6},{9,8},{10,9},{11,10},{13,12},{... | collective-permute-start | bytes 24584 | tf_op jit(solution)/shard_map/ppermute | solution.py:300
  48.2 0.0 copy-done
  48.2 0.0 copy-done.1
  48.2 0.0 copy-done.2
  48.2 0.0 copy-done.3
  48.2 3.9 %fields.1 = (f32[10,256,128]{2,1,0:T(8,128)S(1)}, f32[8,256,128]{2,1,0:T(8,128)S(1)}, f32[8,256,128]{2,1,0:T(8,128)S(1)}, f32[4,8,32,128]{3,2,1,0:T(8,128)S(1)}) custom-call(f32[8,272,128]{2,1,0:T(8,128)S(1)} %all-to-all-done.cells, f32[256,128]{1,0:T(8,128)S(1)} %get-tuple-element.26.before, f32[256,128]{1,0:T(8,128)S(1)} %get-tuple-element.25.after, ...), custom_call_target="tpu_custom_call" | custom-call | flops 4000000000 | bytes 6291456 | tf_op jit(solution)/shard_map/fields/pallas_call | solution.py:302
  52.1 0.0 collective-permute-done.up
  52.2 0.0 collective-permute-done.1.down
  52.2 1.6 %given.1 = (f32[8,4,16,128]{3,2,1,0:T(8,128)S(1)}, f32[8,256,128]{2,1,0:T(8,128)S(1)}) custom-call(s32[1]{0:T(128)} %bitcast.core, f32[8,2,128]{2,1,0:T(2,128)S(1)} %collective-permute-done.up, f32[8,2,128]{2,1,0:T(2,128)S(1)} %collective-permute-done.1.down, f32[256,256]{1,0:T(8,128)S(1)} %copy-done, f32[128,128]{1,0:T(8,128)S(1)} %copy-done.1, ...), custom_call_target="tpu_custom_call" | custom-call | tf_op jit(solution)/shard_map/given/pallas_call | solution.py:318
  53.7 1.9 %collective-permute-start.7 = (f32[8,4,16,128]{3,2,1,0:T(8,128)S(1)}, f32[8,4,16,128]{3,2,1,0:T(8,128)S(1)}, u32[]{:S(2)}, u32[]{:S(2)}) collective-permute-start(f32[8,4,16,128]{3,2,1,0:T(8,128)S(1)} %get-tuple-element.17), channel_id=1, source_target_pairs={{0,4},{4,0},{8,12},{12,8},{16,20},{20,16},{24,28},{28,24},{32,36},... | collective-permute-start | bytes 786440 | tf_op jit(solution)/shard_map/ppermute | solution.py:326
  55.7 0.6 kept.1
  56.3 0.9 collective-permute-done.7
  57.2 38.9 %all_to_all.15 = f32[16,4,16,128]{3,2,1,0:T(8,128)S(1)} all-to-all(f32[16,4,16,128]{3,2,1,0:T(8,128)S(1)} %pad_maximum_fusion), channel_id=1, replica_groups={{0,8,16,24,32,40,48,56,64,72,80,88,96,104,112,120},{68,76,84,92,100,108..., dimensions={0} | all-to-all | bytes 1048576 | tf_op jit(solution)/shard_map/all_to_all | solution.py:340
  96.2 10.1 %all_to_all.16 = f32[4,4,16,128]{3,2,1,0:T(8,128)S(1)} all-to-all(f32[4,4,16,128]{3,2,1,0:T(8,128)S(1)} %multiply_add_fusion), channel_id=1, replica_groups={{0,128,256,384},{4,132,260,388},{8,136,264,392},{12,140,268,396},{16,14..., dimensions={0} | all-to-all | bytes 262144 | tf_op jit(solution)/shard_map/all_to_all | solution.py:347
  106.3 0.6 fusion.7
  (13 shorter events, 0.3 us)
Async XLA Ops:
  2.7 6.1 %copy-start.4 = (f32[1,2048,128]{2,1,0:T(8,128)S(1)}, f32[1,2048,128]{2,1,0:T(8,128)}, u32[]{:S(2)}) copy-start(f32[1,2048,128]{2,1,0:T(8,128)} %cells.1) | copy-start | bytes 3145732
  2.7 39.7 %all-to-all-start = ((f32[8,272,128]{2,1,0:T(8,128)}), f32[8,272,128]{2,1,0:T(8,128)S(1)}, u32[]{:S(2)}, u32[]{:S(2)}) async-start(f32[8,272,128]{2,1,0:T(8,128)} %message.1), calls=%async_computation | async-start | bytes 2228224 | tf_op jit(solution)/shard_map/all_to_all | solution.py:298
  8.8 3.9 %collective-permute-start.2 = (f32[4,256,128]{2,1,0:T(8,128)S(1)}, f32[4,256,128]{2,1,0:T(8,128)S(1)}, u32[]{:S(2)}, u32[]{:S(2)}) collective-permute-start(f32[4,256,128]{2,1,0:T(8,128)S(1)} %dynamic-slice_bitcast_fusion), channel_id=1, source_target_pairs={{0,4},{28,24},{32,36},{60,56},{64,68},{92,88},{96,100},{124,120},{... | collective-permute-start | bytes 1572872 | tf_op jit(solution)/shard_map/ppermute | solution.py:252
  12.8 35.5 %copy-start = (f32[256,256]{1,0:T(8,128)S(1)}, f32[256,256]{1,0:T(8,128)}, u32[]{:S(2)}) copy-start(f32[256,256]{1,0:T(8,128)} %kernel_x.3) | copy-start | bytes 786436
  12.8 35.5 %copy-start.1 = (f32[128,128]{1,0:T(8,128)S(1)}, f32[128,128]{1,0:T(8,128)}, u32[]{:S(2)}) copy-start(f32[128,128]{1,0:T(8,128)} %kernel_y.3) | copy-start | bytes 196612
  12.8 35.5 %copy-start.2 = (f32[3,16]{1,0:T(4,128)S(1)}, f32[3,16]{1,0:T(4,128)}, u32[]{:S(2)}) copy-start(f32[3,16]{1,0:T(4,128)} %colours.1) | copy-start | bytes 580
  12.8 35.4 %copy-start.3 = (f32[16]{0:T(128)S(1)}, f32[16]{0:T(128)}, u32[]{:S(2)}) copy-start(f32[16]{0:T(128)} %absorb.1) | copy-start | bytes 196
  12.9 3.5 %collective-permute-start.3 = (f32[256,128]{1,0:T(8,128)S(1)}, f32[256,128]{1,0:T(8,128)S(1)}, u32[]{:S(2)}, u32[]{:S(2)}) collective-permute-start(f32[256,128]{1,0:T(8,128)S(1)} %get-tuple-element.30), channel_id=1, source_target_pairs={{24,40},{32,16},{28,44},{36,20},{56,72},{64,48},{60,76},{68,52},{8... | collective-permute-start | bytes 393224 | tf_op jit(solution)/shard_map/ppermute | solution.py:265
  13.7 2.7 %collective-permute-start.4 = (f32[256,128]{1,0:T(8,128)S(1)}, f32[256,128]{1,0:T(8,128)S(1)}, u32[]{:S(2)}, u32[]{:S(2)}) collective-permute-start(f32[256,128]{1,0:T(8,128)S(1)} %get-tuple-element.29), channel_id=1, source_target_pairs={{24,48},{32,8},{28,52},{36,12},{56,80},{64,40},{60,84},{68,44},{88... | collective-permute-start | bytes 393224 | tf_op jit(solution)/shard_map/ppermute | solution.py:265
  14.3 2.0 %collective-permute-start.5 = (f32[256,128]{1,0:T(8,128)S(1)}, f32[256,128]{1,0:T(8,128)S(1)}, u32[]{:S(2)}, u32[]{:S(2)}) collective-permute-start(f32[256,128]{1,0:T(8,128)S(1)} %get-tuple-element.28), channel_id=1, source_target_pairs={{24,32},{32,24},{28,36},{36,28},{56,64},{64,56},{60,68},{68,60},{8... | collective-permute-start | bytes 393224 | tf_op jit(solution)/shard_map/ppermute | solution.py:265
  15.0 19.0 %collective-permute-start.6 = (f32[256,128]{1,0:T(8,128)S(1)}, f32[256,128]{1,0:T(8,128)S(1)}, u32[]{:S(2)}, u32[]{:S(2)}) collective-permute-start(f32[256,128]{1,0:T(8,128)S(1)} %get-tuple-element.27), channel_id=1, source_target_pairs={{24,56},{32,0},{28,60},{36,4},{56,88},{64,32},{60,92},{68,36},{88,... | collective-permute-start | bytes 393224 | tf_op jit(solution)/shard_map/ppermute | solution.py:265
  42.3 9.8 %collective-permute-start = (f32[8,2,128]{2,1,0:T(2,128)S(1)}, f32[8,2,128]{2,1,0:T(2,128)S(1)}, u32[]{:S(2)}, u32[]{:S(2)}) collective-permute-start(f32[8,2,128]{2,1,0:T(2,128)S(1)} %get-tuple-element.22), channel_id=1, source_target_pairs={{0,1},{1,2},{2,3},{4,5},{5,6},{6,7},{8,9},{9,10},{10,11},{12,13},{... | collective-permute-start | bytes 24584 | tf_op jit(solution)/shard_map/ppermute | solution.py:299
  45.5 6.6 %collective-permute-start.1 = (f32[8,2,128]{2,1,0:T(2,128)S(1)}, f32[8,2,128]{2,1,0:T(2,128)S(1)}, u32[]{:S(2)}, u32[]{:S(2)}) collective-permute-start(f32[8,2,128]{2,1,0:T(2,128)S(1)} %get-tuple-element.21), channel_id=1, source_target_pairs={{1,0},{2,1},{3,2},{5,4},{6,5},{7,6},{9,8},{10,9},{11,10},{13,12},{... | collective-permute-start | bytes 24584 | tf_op jit(solution)/shard_map/ppermute | solution.py:300
  53.7 3.4 %collective-permute-start.7 = (f32[8,4,16,128]{3,2,1,0:T(8,128)S(1)}, f32[8,4,16,128]{3,2,1,0:T(8,128)S(1)}, u32[]{:S(2)}, u32[]{:S(2)}) collective-permute-start(f32[8,4,16,128]{3,2,1,0:T(8,128)S(1)} %get-tuple-element.17), channel_id=1, source_target_pairs={{0,4},{4,0},{8,12},{12,8},{16,20},{20,16},{24,28},{28,24},{32,36},... | collective-permute-start | bytes 786440 | tf_op jit(solution)/shard_map/ppermute | solution.py:326

commit v9 on v7

--- a/solution.py
+++ b/solution.py
@@ -67,6 +67,13 @@
         loads.append(pltpu.make_async_copy(cells.at[0, block * COLS : (block + 1) * COLS], part, sems.at[0, block]))
         stores.append(pltpu.make_async_copy(part, message.at[block, :COLS], sems.at[1, block]))
         loads[-1].start()
+    ends = jnp.zeros((COLS, ROWS), jnp.float32)
+    lane = iota((COLS, ROWS), 1)
+    for block in range(BLOCKS):
+        loads[block].wait()
+        stores[block].start()
+        turned = pltpu.roll(held[block * COLS : (block + 1) * COLS], 2 * block + 1, 1)
+        ends = jnp.where(lane // 2 == block, turned, ends)
     for load in brick_loads:
         load.wait()
     brick_rows = material.shape[1]
@@ -87,13 +94,6 @@
             ones_where(lane == row + (at + brick_rows)),
             preferred_element_type=jnp.float32,
         )
-    ends = jnp.zeros((COLS, ROWS), jnp.float32)
-    lane = iota((COLS, ROWS), 1)
-    for block in range(BLOCKS):
-        loads[block].wait()
-        stores[block].start()
-        turned = pltpu.roll(held[block * COLS : (block + 1) * COLS], 2 * block + 1, 1)
-        ends = jnp.where(lane // 2 == block, turned, ends)
     ends = ends.T
     none = jnp.zeros((1, ROWS), jnp.float32)
     for block in range(BLOCKS):

time: 107 us -> 108 us (level)
  no operation moved by 1% of the time
where the time goes in v9:
time: 108 us; the launch traced here: 107 us
  blocking collectives  48.9 us (45%)
  waiting for transfers between devices  28.2 us (26%)
  starting transfers between devices  19.7 us (18%)
  Pallas kernels  8.9 us (8%)
    all_to_all x1, blocking collectives, local(): lax.all_to_all(jnp.concatenate([kept, taken], axis=0), 'wide', 0, 0, tile...  38.9 us
    all_to_all x1, waiting for transfers between devices, local(): lax.all_to_all(message, 'wide', 0, 0, tiled=True, axis_index_groups=members)  15.7 us
    ppermute x4, waiting for transfers between devices, outer_blocks(): lax.ppermute(lax.dynamic_index_in_dim(given, wanted, 0, keepdims=False),...  10.3 us
    all_to_all x1, blocking collectives, local(): lax.all_to_all(parts, 'wide', 0, 0, tiled=True, axis_index_groups=along_x)  10.1 us
    all_to_all x1, starting transfers between devices, local(): lax.all_to_all(message, 'wide', 0, 0, tiled=True, axis_index_groups=members)  6.04 us
    pallas_call x1, Pallas kernels, local(): pl.pallas_call(functools.partial(fields_kernel, step), out_shape=[one(SLI...  3.9 us
    ppermute x4, starting transfers between devices, outer_blocks(): lax.ppermute(lax.dynamic_index_in_dim(given, wanted, 0, keepdims=False),...  3.43 us
    ppermute x1, starting transfers between devices, local(): lax.ppermute(cells[:, COLS + 4:COLS + 6], 'narrow', [(i, i + 1) for i in...  3.19 us
  transfers between devices with their start and end apart: 9, of which 4 were waited for; matrix products, arithmetic and copies ran while one was open for 0% of the time, Pallas kernels for 4%

profile of v9, /device:TPU:16, one launch (start us, length us, event | category | flops | bytes accessed | tf_op | source)
XLA Modules:
  0.0 107.1 jit_solution(2633248590335024901)
XLA Ops:
  0.0 2.8 %message.1 = f32[8,272,128]{2,1,0:T(8,128)} custom-call(f32[1,2048,128]{2,1,0:T(8,128)} %cells.1, s32[1,16,256]{2,1,0:T(8,128)} %bitcast.95, s32[1,16,256]{2,1,0:T(8,128)} %bitcast.96), custom_call_target="tpu_custom_call" | custom-call | tf_op jit(solution)/shard_map/message/pallas_call | solution.py:284
  2.8 0.0 copy-start.4
  2.8 6.0 %all-to-all-start = ((f32[8,272,128]{2,1,0:T(8,128)}), f32[8,272,128]{2,1,0:T(8,128)S(1)}, u32[]{:S(2)}, u32[]{:S(2)}) async-start(f32[8,272,128]{2,1,0:T(8,128)} %message.1), calls=%async_computation | async-start | bytes 2228224 | tf_op jit(solution)/shard_map/all_to_all | solution.py:298
  8.9 0.0 copy-done.4
  8.9 2.4 %collective-permute-start.2 = (f32[4,256,128]{2,1,0:T(8,128)S(1)}, f32[4,256,128]{2,1,0:T(8,128)S(1)}, u32[]{:S(2)}, u32[]{:S(2)}) collective-permute-start(f32[4,256,128]{2,1,0:T(8,128)S(1)} %dynamic-slice_bitcast_fusion), channel_id=1, source_target_pairs={{0,4},{28,24},{32,36},{60,56},{64,68},{92,88},{96,100},{124,120},{... | collective-permute-start | bytes 1572872 | tf_op jit(solution)/shard_map/ppermute | solution.py:252
  11.4 1.4 %collective-permute-done.2 = f32[4,256,128]{2,1,0:T(8,128)S(1)} collective-permute-done((f32[4,256,128]{2,1,0:T(8,128)S(1)}, f32[4,256,128]{2,1,0:T(8,128)S(1)}, u32[]{:S(2)}, u32[]{:S(2)}) %collective-permute-start.2) | collective-permute-done | bytes 524320 | tf_op jit(solution)/shard_map/ppermute | solution.py:252
  12.9 0.1 bitcast_select_fusion
  12.9 0.0 copy-start
  12.9 0.0 copy-start.1
  12.9 0.0 copy-start.2
  13.0 0.0 copy-start.3
  13.0 0.1 dynamic-slice_bitcast_fusion.1
  13.0 1.4 %collective-permute-start.3 = (f32[256,128]{1,0:T(8,128)S(1)}, f32[256,128]{1,0:T(8,128)S(1)}, u32[]{:S(2)}, u32[]{:S(2)}) collective-permute-start(f32[256,128]{1,0:T(8,128)S(1)} %get-tuple-element.30), channel_id=1, source_target_pairs={{24,56},{32,0},{28,60},{36,4},{56,88},{64,32},{60,92},{68,36},{88,... | collective-permute-start | bytes 393224 | tf_op jit(solution)/shard_map/ppermute | solution.py:265
  14.5 0.7 collective-permute-start.4
  15.1 0.7 collective-permute-start.5
  15.8 0.7 collective-permute-start.6
  16.5 10.2 %collective-permute-done.3 = f32[256,128]{1,0:T(8,128)S(1)} collective-permute-done((f32[256,128]{1,0:T(8,128)S(1)}, f32[256,128]{1,0:T(8,128)S(1)}, u32[]{:S(2)}, u32[]{:S(2)}) %collective-permute-start.3) | collective-permute-done | bytes 131104 | tf_op jit(solution)/shard_map/ppermute | solution.py:265
  26.7 0.0 collective-permute-done.4
  26.8 0.0 collective-permute-done.5
  26.8 0.0 collective-permute-done.6
  26.8 15.7 %all-to-all-done.cells = f32[8,272,128]{2,1,0:T(8,128)S(1)} async-done(((f32[8,272,128]{2,1,0:T(8,128)}), f32[8,272,128]{2,1,0:T(8,128)S(1)}, u32[]{:S(2)}, u32[]{:S(2)}) %all-to-all-start) | async-done | bytes 1114144 | tf_op jit(solution)/shard_map/all_to_all | solution.py:298
  42.5 3.2 %collective-permute-start = (f32[8,2,128]{2,1,0:T(2,128)S(1)}, f32[8,2,128]{2,1,0:T(2,128)S(1)}, u32[]{:S(2)}, u32[]{:S(2)}) collective-permute-start(f32[8,2,128]{2,1,0:T(2,128)S(1)} %get-tuple-element.22), channel_id=1, source_target_pairs={{0,1},{1,2},{2,3},{4,5},{5,6},{6,7},{8,9},{9,10},{10,11},{12,13},{... | collective-permute-start | bytes 24584 | tf_op jit(solution)/shard_map/ppermute | solution.py:299
  45.7 2.7 %collective-permute-start.1 = (f32[8,2,128]{2,1,0:T(2,128)S(1)}, f32[8,2,128]{2,1,0:T(2,128)S(1)}, u32[]{:S(2)}, u32[]{:S(2)}) collective-permute-start(f32[8,2,128]{2,1,0:T(2,128)S(1)} %get-tuple-element.21), channel_id=1, source_target_pairs={{1,0},{2,1},{3,2},{5,4},{6,5},{7,6},{9,8},{10,9},{11,10},{13,12},{... | collective-permute-start | bytes 24584 | tf_op jit(solution)/shard_map/ppermute | solution.py:300
  48.4 0.0 copy-done
  48.4 0.0 copy-done.1
  48.4 0.0 copy-done.2
  48.4 0.0 copy-done.3
  48.4 3.9 %fields.1 = (f32[10,256,128]{2,1,0:T(8,128)S(1)}, f32[8,256,128]{2,1,0:T(8,128)S(1)}, f32[8,256,128]{2,1,0:T(8,128)S(1)}, f32[4,8,32,128]{3,2,1,0:T(8,128)S(1)}) custom-call(f32[8,272,128]{2,1,0:T(8,128)S(1)} %all-to-all-done.cells, f32[256,128]{1,0:T(8,128)S(1)} %get-tuple-element.26.before, f32[256,128]{1,0:T(8,128)S(1)} %get-tuple-element.25.after, ...), custom_call_target="tpu_custom_call" | custom-call | flops 4000000000 | bytes 6291456 | tf_op jit(solution)/shard_map/fields/pallas_call | solution.py:302
  52.3 0.0 collective-permute-done.up
  52.3 0.0 collective-permute-done.1.down
  52.3 1.6 %given.1 = (f32[8,4,16,128]{3,2,1,0:T(8,128)S(1)}, f32[8,256,128]{2,1,0:T(8,128)S(1)}) custom-call(s32[1]{0:T(128)} %bitcast.core, f32[8,2,128]{2,1,0:T(2,128)S(1)} %collective-permute-done.up, f32[8,2,128]{2,1,0:T(2,128)S(1)} %collective-permute-done.1.down, f32[256,256]{1,0:T(8,128)S(1)} %copy-done, f32[128,128]{1,0:T(8,128)S(1)} %copy-done.1, ...), custom_call_target="tpu_custom_call" | custom-call | tf_op jit(solution)/shard_map/given/pallas_call | solution.py:318
  53.9 1.9 %collective-permute-start.7 = (f32[8,4,16,128]{3,2,1,0:T(8,128)S(1)}, f32[8,4,16,128]{3,2,1,0:T(8,128)S(1)}, u32[]{:S(2)}, u32[]{:S(2)}) collective-permute-start(f32[8,4,16,128]{3,2,1,0:T(8,128)S(1)} %get-tuple-element.17), channel_id=1, source_target_pairs={{0,4},{4,0},{8,12},{12,8},{16,20},{20,16},{24,28},{28,24},{32,36},... | collective-permute-start | bytes 786440 | tf_op jit(solution)/shard_map/ppermute | solution.py:326
  55.8 0.6 kept.1
  56.5 0.9 collective-permute-done.7
  57.4 38.9 %all_to_all.15 = f32[16,4,16,128]{3,2,1,0:T(8,128)S(1)} all-to-all(f32[16,4,16,128]{3,2,1,0:T(8,128)S(1)} %pad_maximum_fusion), channel_id=1, replica_groups={{0,8,16,24,32,40,48,56,64,72,80,88,96,104,112,120},{68,76,84,92,100,108..., dimensions={0} | all-to-all | bytes 1048576 | tf_op jit(solution)/shard_map/all_to_all | solution.py:340
  96.4 10.1 %all_to_all.16 = f32[4,4,16,128]{3,2,1,0:T(8,128)S(1)} all-to-all(f32[4,4,16,128]{3,2,1,0:T(8,128)S(1)} %multiply_add_fusion), channel_id=1, replica_groups={{0,128,256,384},{4,132,260,388},{8,136,264,392},{12,140,268,396},{16,14..., dimensions={0} | all-to-all | bytes 262144 | tf_op jit(solution)/shard_map/all_to_all | solution.py:347
  106.5 0.6 fusion.7
  (13 shorter events, 0.3 us)
Async XLA Ops:
  2.8 6.1 %copy-start.4 = (f32[1,2048,128]{2,1,0:T(8,128)S(1)}, f32[1,2048,128]{2,1,0:T(8,128)}, u32[]{:S(2)}) copy-start(f32[1,2048,128]{2,1,0:T(8,128)} %cells.1) | copy-start | bytes 3145732
  2.8 39.7 %all-to-all-start = ((f32[8,272,128]{2,1,0:T(8,128)}), f32[8,272,128]{2,1,0:T(8,128)S(1)}, u32[]{:S(2)}, u32[]{:S(2)}) async-start(f32[8,272,128]{2,1,0:T(8,128)} %message.1), calls=%async_computation | async-start | bytes 2228224 | tf_op jit(solution)/shard_map/all_to_all | solution.py:298
  8.9 3.9 %collective-permute-start.2 = (f32[4,256,128]{2,1,0:T(8,128)S(1)}, f32[4,256,128]{2,1,0:T(8,128)S(1)}, u32[]{:S(2)}, u32[]{:S(2)}) collective-permute-start(f32[4,256,128]{2,1,0:T(8,128)S(1)} %dynamic-slice_bitcast_fusion), channel_id=1, source_target_pairs={{0,4},{28,24},{32,36},{60,56},{64,68},{92,88},{96,100},{124,120},{... | collective-permute-start | bytes 1572872 | tf_op jit(solution)/shard_map/ppermute | solution.py:252
  12.9 35.5 %copy-start = (f32[256,256]{1,0:T(8,128)S(1)}, f32[256,256]{1,0:T(8,128)}, u32[]{:S(2)}) copy-start(f32[256,256]{1,0:T(8,128)} %kernel_x.3) | copy-start | bytes 786436
  12.9 35.5 %copy-start.1 = (f32[128,128]{1,0:T(8,128)S(1)}, f32[128,128]{1,0:T(8,128)}, u32[]{:S(2)}) copy-start(f32[128,128]{1,0:T(8,128)} %kernel_y.3) | copy-start | bytes 196612
  12.9 35.5 %copy-start.2 = (f32[3,16]{1,0:T(4,128)S(1)}, f32[3,16]{1,0:T(4,128)}, u32[]{:S(2)}) copy-start(f32[3,16]{1,0:T(4,128)} %colours.1) | copy-start | bytes 580
  13.0 35.4 %copy-start.3 = (f32[16]{0:T(128)S(1)}, f32[16]{0:T(128)}, u32[]{:S(2)}) copy-start(f32[16]{0:T(128)} %absorb.1) | copy-start | bytes 196
  13.0 13.7 %collective-permute-start.3 = (f32[256,128]{1,0:T(8,128)S(1)}, f32[256,128]{1,0:T(8,128)S(1)}, u32[]{:S(2)}, u32[]{:S(2)}) collective-permute-start(f32[256,128]{1,0:T(8,128)S(1)} %get-tuple-element.30), channel_id=1, source_target_pairs={{24,56},{32,0},{28,60},{36,4},{56,88},{64,32},{60,92},{68,36},{88,... | collective-permute-start | bytes 393224 | tf_op jit(solution)/shard_map/ppermute | solution.py:265
  14.5 12.3 %collective-permute-start.4 = (f32[256,128]{1,0:T(8,128)S(1)}, f32[256,128]{1,0:T(8,128)S(1)}, u32[]{:S(2)}, u32[]{:S(2)}) collective-permute-start(f32[256,128]{1,0:T(8,128)S(1)} %get-tuple-element.29), channel_id=1, source_target_pairs={{24,48},{32,8},{28,52},{36,12},{56,80},{64,40},{60,84},{68,44},{88... | collective-permute-start | bytes 393224 | tf_op jit(solution)/shard_map/ppermute | solution.py:265
  15.1 11.6 %collective-permute-start.5 = (f32[256,128]{1,0:T(8,128)S(1)}, f32[256,128]{1,0:T(8,128)S(1)}, u32[]{:S(2)}, u32[]{:S(2)}) collective-permute-start(f32[256,128]{1,0:T(8,128)S(1)} %get-tuple-element.28), channel_id=1, source_target_pairs={{24,40},{32,16},{28,44},{36,20},{56,72},{64,48},{60,76},{68,52},{8... | collective-permute-start | bytes 393224 | tf_op jit(solution)/shard_map/ppermute | solution.py:265
  15.8 10.9 %collective-permute-start.6 = (f32[256,128]{1,0:T(8,128)S(1)}, f32[256,128]{1,0:T(8,128)S(1)}, u32[]{:S(2)}, u32[]{:S(2)}) collective-permute-start(f32[256,128]{1,0:T(8,128)S(1)} %get-tuple-element.27), channel_id=1, source_target_pairs={{24,32},{32,24},{28,36},{36,28},{56,64},{64,56},{60,68},{68,60},{8... | collective-permute-start | bytes 393224 | tf_op jit(solution)/shard_map/ppermute | solution.py:265
  42.5 9.8 %collective-permute-start = (f32[8,2,128]{2,1,0:T(2,128)S(1)}, f32[8,2,128]{2,1,0:T(2,128)S(1)}, u32[]{:S(2)}, u32[]{:S(2)}) collective-permute-start(f32[8,2,128]{2,1,0:T(2,128)S(1)} %get-tuple-element.22), channel_id=1, source_target_pairs={{0,1},{1,2},{2,3},{4,5},{5,6},{6,7},{8,9},{9,10},{10,11},{12,13},{... | collective-permute-start | bytes 24584 | tf_op jit(solution)/shard_map/ppermute | solution.py:299
  45.7 6.6 %collective-permute-start.1 = (f32[8,2,128]{2,1,0:T(2,128)S(1)}, f32[8,2,128]{2,1,0:T(2,128)S(1)}, u32[]{:S(2)}, u32[]{:S(2)}) collective-permute-start(f32[8,2,128]{2,1,0:T(2,128)S(1)} %get-tuple-element.21), channel_id=1, source_target_pairs={{1,0},{2,1},{3,2},{5,4},{6,5},{7,6},{9,8},{10,9},{11,10},{13,12},{... | collective-permute-start | bytes 24584 | tf_op jit(solution)/shard_map/ppermute | solution.py:300
  53.9 3.4 %collective-permute-start.7 = (f32[8,4,16,128]{3,2,1,0:T(8,128)S(1)}, f32[8,4,16,128]{3,2,1,0:T(8,128)S(1)}, u32[]{:S(2)}, u32[]{:S(2)}) collective-permute-start(f32[8,4,16,128]{3,2,1,0:T(8,128)S(1)} %get-tuple-element.17), channel_id=1, source_target_pairs={{0,4},{4,0},{8,12},{12,8},{16,20},{20,16},{24,28},{28,24},{32,36},... | collective-permute-start | bytes 786440 | tf_op jit(solution)/shard_map/ppermute | solution.py:326
